TPU v7x, 128 devices: a whole 4x4x4 slice. The times are simulated.
128 devices in a mesh: aux: 4 (over z), pair: 32 (over x, y, core).
Axes of the slice: x: 4, y: 4, z: 4, core: 2. Of those that a mesh axis runs over, the one named last changes fastest.
Arguments:
- integrals: bfloat16 [96, 64, 1536, 128], P('pair', None, 'aux'), may hold values from -0.375 to 0.375
- coefficients: bfloat16 [8192, 64], P('pair'), may hold values from -6 to 6
- nu_blocks: int32 [4, 96], P('aux', 'pair'), may hold values from 0 to 63
- tile_count: int32 [4, 32], P('aux', 'pair'), may hold values from 1 to 3, as said below
- metric_root: bfloat16 [1536, 1536], replicated
Outputs:
- fitted: bfloat16 [64, 64, 32, 1536], P('aux', None, 'pair')
Inputs may be any that keep to these rules, and one draw needn't show every extreme that they name: `nu_blocks`: a slot's basis row block covers basis functions 128 * v to 128 * v + 127; slots may repeat a block. `tile_count`: some device holds 3 live tiles in every draw.
All inputs are finite; a program needn't handle non-finite values.
Results may differ from a plain program's by a relative error of at most 0.005.
Values may be sent and summed in bfloat16 or wider, within the bound.
No kernel may reach another device: no remote copies, remote signals or barrier semaphores. Data moves between devices by JAX's collectives and lax.ppermute only.
A program may use at most 128 MiB of HBM per device.

v0:
```python
import jax
import jax.numpy as jnp
from jax import lax
from jax.sharding import PartitionSpec as P


def regroup(source):
    arrived = lax.all_to_all(source, "aux", split_axis=0, concat_axis=2, tiled=True)
    occ_part, row_count, total_aux = arrived.shape
    return arrived.reshape(occ_part, row_count, 1, total_aux)


def shards(integrals, coefficients, nu_blocks, tile_count, metric_root):
    basis_rows, occ_count = coefficients.shape
    paired_rows = coefficients.reshape(basis_rows // 2, 2 * occ_count)
    whole_coeff = lax.all_gather(paired_rows, "pair", axis=0, tiled=True).reshape(-1, occ_count)
    slot_total, mu_rows, aux_width, block_width = integrals.shape
    live_count = tile_count[0, 0]
    empty_half = jnp.zeros((occ_count, mu_rows, aux_width), jnp.float32)
    running = empty_half
    for slot_index in range(slot_total):
        first_row = nu_blocks[0, slot_index] * block_width
        coeff_block = lax.dynamic_slice_in_dim(whole_coeff, first_row, block_width, 0)
        tile_data = lax.dynamic_index_in_dim(integrals, slot_index, 0, keepdims=False)
        running = running + jnp.einsum(
            "mpn,ni->imp", tile_data, coeff_block, preferred_element_type=jnp.float32
        ) * (slot_index < live_count).astype(jnp.float32)
    half = running.astype(jnp.bfloat16)
    arrived = regroup(half)
    occ_part, row_count, home_count, total_aux = arrived.shape
    product = lax.dot_general(
        arrived.reshape(occ_part * row_count, total_aux),
        metric_root,
        (((1,), (1,)), ((), ())),
        preferred_element_type=jnp.float32,
    )
    return product.astype(jnp.bfloat16).reshape(occ_part, row_count, home_count, total_aux)


def solution(mesh):
    placed = (
        P("pair", None, "aux", None),
        P("pair", None),
        P("aux", "pair"),
        P("aux", "pair"),
        P(),
    )
    return jax.shard_map(
        shards, mesh=mesh, in_specs=placed, out_specs=P("aux", None, "pair", None), check_vma=False
    )
```

profile of v0, /device:TPU:6, one launch (start us, length us, event | category | flops | bytes accessed | tf_op | source)
XLA Modules:
  0.0 134.2 jit_solution(8648295810152444854)
XLA Ops:
  6.5 0.0 all-gather.2.cloned.1.call-start
  6.5 0.9 copy.13
  7.4 0.7 reshape.28
  8.1 0.0 all-gather.2.cloned.1.call-update
  8.2 1.4 %fusion.20 = (s32[1,1]{1,0:T(1,128)}, s32[1,1]{1,0:T(1,128)}, s32[1,1]{1,0:T(1,128)}) fusion(s32[1,3]{1,0:T(1,128)} %param.7), kind=kLoop, calls=%fused_computation.20 | loop fusion | bytes 24 | tf_op jit(solution)/shard_map/slice | solution.py:22
  12.0 42.3 %all-gather.2.cloned.1.call-done = bf16[4096,128]{1,0:T(8,128)(2,1)} async-done(((bf16[128,128]{1,0:T(8,128)(2,1)}), bf16[4096,128]{1,0:T(8,128)(2,1)}) %all-gather.2.cloned.1.call-update) | async-done | bytes 1048592 | tf_op jit(solution)/shard_map/all_gather | solution.py:16
  54.3 2.7 %reshape.29 = bf16[8192,64]{1,0:T(8,128)(2,1)S(1)} reshape(bf16[4096,128]{1,0:T(8,128)(2,1)} %all-gather.2.cloned.1.call-done) | data formatting | bytes 2097152 | tf_op jit(solution)/shard_map/reshape | solution.py:16
  57.0 0.0 copy-start
  57.0 5.9 %fusion.4 = f32[64,64,384]{2,0,1:T(8,128)S(1)} fusion(bf16[3,64,384,128]{3,2,1,0:T(8,128)(2,1)} %param.5, bf16[8192,64]{1,0:T(8,128)(2,1)S(1)} %reshape.29, s32[]{:T(128)S(6)} %select_n.13), kind=kOutput, calls=%fused_computation.4 | convolution fusion | flops 402653184 | bytes 12615684 | tf_op jit(solution)/shard_map/mpn,ni->imp/dot_general | solution.py:25
  62.9 0.0 copy-done
  62.9 5.1 %fusion = f32[64,64,384]{2,0,1:T(8,128)S(1)} fusion(bf16[3,64,384,128]{3,2,1,0:T(8,128)(2,1)} %param.5, bf16[8192,64]{1,0:T(8,128)(2,1)S(1)} %reshape.29, s32[]{:T(128)S(6)} %select_n.15), kind=kOutput, calls=%fused_computation | convolution fusion | flops 402653184 | bytes 12615684 | tf_op jit(solution)/shard_map/mpn,ni->imp/dot_general | solution.py:25
  68.1 5.3 %add_convert_fusion = bf16[64,64,384]{2,0,1:T(8,128)(2,1)S(1)} fusion(f32[64,64,384]{2,0,1:T(8,128)S(1)} %fusion, f32[64,64,384]{2,0,1:T(8,128)S(1)} %fusion.4, f32[]{:T(128)} %bitcast.11, f32[]{:T(128)} %bitcast.7, f32[]{:T(128)} %bitcast.3, bf16[3,64,384,128]{3,2,1,0:T(8,128)(2,1)} %param.5, bf16[8192,64]{1,0:T(8,128)(2,1)} %copy-done, s32[]{:T(128)S(6)} %select_n.14), kind=kOutput, calls=%fused_computation.6 | convolution fusion | flops 412090368 | bytes 22054404 | tf_op jit(solution)/shard_map/mpn,ni->imp/dot_general | solution.py:25
  73.4 1.9 %copy.17 = bf16[64,64,384]{2,1,0:T(8,128)(2,1)S(1)} copy(bf16[64,64,384]{2,0,1:T(8,128)(2,1)S(1)} %add_convert_fusion) | data formatting | bytes 6291456 | tf_op jit(solution)/shard_map/convert_element_type | solution.py:28
  75.2 0.0 slice-start
  75.3 42.5 %all_to_all.15 = bf16[64,64,384]{2,1,0:T(8,128)(2,1)S(1)} all-to-all(bf16[64,64,384]{2,1,0:T(8,128)(2,1)S(1)} %copy.17), channel_id=1, replica_groups=mesh['aux'=4,'pair'=32] {'aux'}, dimensions={0} | all-to-all | bytes 6291456 | tf_op jit(solution)/shard_map/all_to_all | solution.py:8
  117.7 0.0 slice-start.1
  117.7 2.6 %copy.18 = bf16[4,16,64,384]{3,0,2,1:T(4,128)(2,1)S(1)} copy(bf16[4,16,64,384]{3,2,1,0:T(8,128)(2,1)S(1)} %bitcast.39) | data formatting | bytes 6291456 | tf_op jit(solution)/shard_map/all_to_all | solution.py:8
  120.4 0.5 copy.23
  120.9 0.0 slice-done
  120.9 0.0 slice-done.1
  121.0 6.4 %convolution_convert_fusion = bf16[1024,1536]{1,0:T(8,128)(2,1)} fusion(bf16[1024,1536]{1,0:T(8,128)(2,1)S(1)} %bitcast.41, bf16[1536,1536]{1,0:T(8,128)(2,1)S(1)} %bitcast.43), kind=kOutput, calls=%fused_computation.10 | convolution fusion | flops 4833411072 | bytes 11010048 | tf_op jit(solution)/shard_map/dot_general | solution.py:31
  (1 shorter events, 0.0 us)
Async XLA Ops:
  6.5 47.7 %all-gather.2.cloned.1.call-start = ((), (), s32[]{:S(2)}) async-start(), calls=%async_computation.1 | async-start | bytes 1081344 | tf_op jit(solution)/shard_map/all_gather | solution.py:16
  57.0 5.9 %copy-start = (bf16[8192,64]{1,0:T(8,128)(2,1)}, bf16[8192,64]{1,0:T(8,128)(2,1)S(1)}, u32[]{:S(2)}) copy-start(bf16[8192,64]{1,0:T(8,128)(2,1)S(1)} %reshape.29) | copy-start | bytes 3145732
  75.2 45.7 %slice-start = ((s8[4718592]{0:T(1024)(128)(4,1)}), s8[4194304]{0:T(1024)(128)(4,1)S(1)}, s32[]{:S(2)}) async-start(s8[4718592]{0:T(1024)(128)(4,1)} %bitcast.42), calls=%async_computation.2 | async-start | bytes 8388608
  117.7 3.2 %slice-start.1 = ((s8[4718592]{0:T(1024)(128)(4,1)}), s8[524288]{0:T(1024)(128)(4,1)S(1)}, s32[]{:S(2)}) async-start(s8[4718592]{0:T(1024)(128)(4,1)} %bitcast.42), calls=%async_computation.3 | async-start | bytes 1048576
Sparse Core Ops, SparseCore 0:
  9.6 44.6 all-gather.1
where the time goes:
time: 135 us; the launch traced here: 134 us
  blocking collectives  42.5 us (31%)
  waiting for transfers between devices  42.3 us (31%)
  matrix products  22.8 us (17%)
  between operations  15.9 us (12%)
  local copies, waits for them, and re-layouts  10.8 us (8%)
    all_to_all x1, blocking collectives, regroup(): lax.all_to_all(source, 'aux', split_axis=0, concat_axis=2, tiled=True)  42.5 us
    all_gather x1, waiting for transfers between devices, shards(): lax.all_gather(paired_rows, 'pair', axis=0, tiled=True)  42.3 us
    dot_general x3, matrix products, shards(): jnp.einsum('mpn,ni->imp', tile_data, coeff_block, preferred_element_type=...  16.3 us
    dot_general x1, matrix products, shards(): lax.dot_general(arrived.reshape(occ_part * row_count, total_aux), metric_...  6.43 us
    reshape x1, local copies, waits for them, and re-layouts, shards(): lax.all_gather(paired_rows, 'pair', axis=0, tiled=True)  2.74 us
  transfers between devices with their start and end apart: 1, of which 1 were waited for; matrix products, arithmetic and copies ran while one was open for 1% of the time, Pallas kernels for 0%

commit v1 on v0

v1 whole, which is shorter than its diff:
```python
import functools

import jax
import jax.numpy as jnp
from jax import lax
from jax.experimental import pallas as pl
from jax.experimental.pallas import tpu as pltpu
from jax.sharding import PartitionSpec as P

NT = (((1,), (1,)), ((), ()))
VMEM = pl.BlockSpec(memory_space=pltpu.VMEM)
SMEM = pl.BlockSpec(memory_space=pltpu.SMEM)
HBM = pl.BlockSpec(memory_space=pltpu.HBM)

SIDE = 4
GROUP = 16
BLOCK = 4
CHUNKS = ((0, 16), (32, 32), (16, 16))
OFFSETS = (0, 2, 1, 3)


def place_of(offset):
    return jnp.where(offset == 2, 1, jnp.where(offset == 1, 2, offset))


def coords(p):
    return p // (2 * SIDE), (p // 2) % SIDE, p % 2


def line_perm(phase, step):
    pairs = []
    for p in range(2 * SIDE * SIDE):
        x, y, core = coords(p)
        if core == phase:
            x = (x + step) % SIDE
        else:
            y = (y + step) % SIDE
        pairs.append((p, (x * SIDE + y) * 2 + core))
    return pairs


def gather_coeff(coeff_t):
    mine = coeff_t[None]
    for phase in (0, 1):
        mine = jnp.concatenate(
            [mine] + [lax.ppermute(mine, "pair", line_perm(phase, step)) for step in OFFSETS[1:]], 0
        )
    partner = lax.ppermute(mine, "pair", [(p, p ^ 1) for p in range(2 * SIDE * SIDE)])
    return mine, partner


def pick_coeff(nu_ref, count_ref, mine_ref, partner_ref, cc_ref):
    aux = lax.axis_index("aux")
    pair = lax.axis_index("pair")
    my_x, my_y, my_core = coords(pair)
    width = cc_ref.shape[1] // 3
    for slot in range(3):
        block = nu_ref[0, slot]
        x, y, core = coords(block // 2)
        step_x = place_of((my_x - x + SIDE) % SIDE)
        step_y = place_of((my_y - y + SIDE) % SIDE)
        piece = jnp.where(core == 0, step_y * SIDE + step_x, step_x * SIDE + step_y)
        lanes = pl.ds(pl.multiple_of((block % 2) * width, width), width)
        live = slot < count_ref[0, 0]
        for d in range(SIDE):
            rows = pl.ds(pl.multiple_of(((aux + d) % SIDE) * 16, 16), 16)
            own = mine_ref[piece, rows, lanes]
            other = partner_ref[piece, rows, lanes]
            chosen = jnp.where(core == my_core, own, other)
            cc_ref[16 * d:16 * d + 16, width * slot:width * (slot + 1)] = jnp.where(
                live, chosen, jnp.zeros_like(chosen)
            )


def half_body(first, count, integrals_ref, cc_ref, out_refs, tiles, acc, sems, before_dots):
    copies = []
    for b in range(count // BLOCK):
        copy = pltpu.make_async_copy(
            integrals_ref.at[:, pl.ds(first + b * BLOCK, BLOCK)], tiles.at[b], sems.at[b]
        )
        copy.start()
        copies.append(copy)
    before_dots()
    cc = cc_ref[...]
    width = tiles.shape[3]
    parts = width // 128
    for g in range(count // GROUP):
        for k in range(GROUP // BLOCK):
            b = g * (GROUP // BLOCK) + k
            copies[b].wait()
            tile = jnp.concatenate([tiles[b, s].reshape(BLOCK * width, 128) for s in range(3)], axis=1)
            prod = lax.dot_general(cc, tile, NT, preferred_element_type=jnp.float32)
            for j in range(BLOCK):
                for q in range(parts):
                    lane = (j * parts + q) * 128
                    acc[g, q, pl.ds(k * BLOCK + j, 64, stride=GROUP), :] = prod[:, lane:lane + 128]
        for d in range(SIDE):
            for q in range(parts):
                rows = acc[g, q, 256 * d:256 * d + 256, :].astype(jnp.bfloat16)
                out_refs[d][:, GROUP * g:GROUP * (g + 1), 128 * q:128 * (q + 1)] = rows.reshape(16, GROUP, 128)


def half_first(first, count, nu_ref, count_ref, mine_ref, partner_ref, integrals_ref,
               o0, o1, o2, o3, cc_ref, tiles, acc, sems):
    def before():
        pick_coeff(nu_ref, count_ref, mine_ref, partner_ref, cc_ref)

    half_body(first, count, integrals_ref, cc_ref, (o0, o1, o2, o3), tiles, acc, sems, before)


def half_next(first, count, cc_ref, integrals_ref, o0, o1, o2, o3, tiles, acc, sems):
    half_body(first, count, integrals_ref, cc_ref, (o0, o1, o2, o3), tiles, acc, sems, lambda: None)


def half_call(first, count, integrals, cc=None, picked_from=None):
    width = integrals.shape[2]
    outs = [jax.ShapeDtypeStruct((16, count, width), jnp.bfloat16)] * SIDE
    common = dict(
        scratch_shapes=[
            pltpu.VMEM((count // BLOCK, 3, BLOCK, width, 128), jnp.bfloat16),
            pltpu.VMEM((count // GROUP, width // 128, 64 * GROUP, 128), jnp.float32),
            pltpu.SemaphoreType.DMA((count // BLOCK,)),
        ],
        compiler_params=pltpu.CompilerParams(vmem_limit_bytes=48 * 2**20),
        cost_estimate=pl.CostEstimate(
            flops=2 * count * width * 384 * 256, bytes_accessed=count * width * 384 * 2, transcendentals=0
        ),
    )
    if cc is None:
        res = pl.pallas_call(
            functools.partial(half_first, first, count),
            in_specs=[SMEM, SMEM, VMEM, VMEM, HBM],
            out_specs=[VMEM] * 5,
            out_shape=outs + [jax.ShapeDtypeStruct((64, 384), jnp.bfloat16)],
            **common,
        )(*picked_from, integrals)
        return res[:SIDE], res[SIDE]
    res = pl.pallas_call(
        functools.partial(half_next, first, count),
        in_specs=[VMEM, HBM],
        out_specs=[VMEM] * 4,
        out_shape=outs,
        **common,
    )(cc, integrals)
    return res, cc


def fit_kernel(first, count, *refs):
    a_refs, root_ref, (out_ref, stage, sems) = refs[:4], refs[4], refs[-3:]
    rows = 16 * count
    step = stage.shape[3]
    arrived = jnp.concatenate([a[...].reshape(rows, a.shape[2]) for a in a_refs], axis=1)
    copies = []
    for q in range(stage.shape[0]):
        prod = lax.dot_general(
            arrived, root_ref[q * step:(q + 1) * step, :], NT, preferred_element_type=jnp.float32
        )
        stage[q] = prod.astype(jnp.bfloat16).reshape(16, count, step)
        copy = pltpu.make_async_copy(
            stage.at[q], out_ref.at[:, pl.ds(first, count), pl.ds(q * step, step)], sems.at[q]
        )
        copy.start()
        copies.append(copy)
    for copy in copies:
        copy.wait()


def fit_call(first, count, arrived, root, out):
    total = root.shape[0]
    step = 512
    operands = list(arrived) + [root]
    specs = [VMEM] * 5
    aliases = {}
    if out is not None:
        operands.append(out)
        specs.append(HBM)
        aliases = {5: 0}
    return pl.pallas_call(
        functools.partial(fit_kernel, first, count),
        in_specs=specs,
        out_specs=HBM,
        out_shape=jax.ShapeDtypeStruct((16, 64, total), jnp.bfloat16),
        scratch_shapes=[
            pltpu.VMEM((total // step, 16, count, step), jnp.bfloat16),
            pltpu.SemaphoreType.DMA((total // step,)),
        ],
        input_output_aliases=aliases,
        compiler_params=pltpu.CompilerParams(vmem_limit_bytes=24 * 2**20),
        cost_estimate=pl.CostEstimate(
            flops=2 * 16 * count * total * total, bytes_accessed=16 * count * total * 4, transcendentals=0
        ),
    )(*operands)


def shards(integrals, coefficients, nu_blocks, tile_count, metric_root):
    aux = lax.axis_index("aux")
    width = integrals.shape[2]
    root = jnp.concatenate(
        [
            lax.dynamic_slice_in_dim(metric_root, ((aux - d + SIDE) % SIDE) * width, width, 1)
            for d in range(SIDE)
        ],
        axis=1,
    )
    mine, partner = gather_coeff(coefficients.T)
    cc = None
    held = []
    for first, count in CHUNKS:
        parts, cc = half_call(first, count, integrals, cc, (nu_blocks, tile_count, mine, partner))
        sent = {
            d: lax.ppermute(parts[d], "aux", [(i, (i + d) % SIDE) for i in range(SIDE)]) for d in (2, 1, 3)
        }
        held.append((parts[0], sent[1], sent[2], sent[3]))
    out = None
    for (first, count), arrived in zip(CHUNKS, held):
        out = fit_call(first, count, arrived, root, out)
    return out.reshape(out.shape[0], out.shape[1], 1, out.shape[2])


def solution(mesh):
    placed = (
        P("pair", None, "aux", None),
        P("pair", None),
        P("aux", "pair"),
        P("aux", "pair"),
        P(),
    )
    return jax.shard_map(
        shards, mesh=mesh, in_specs=placed, out_specs=P("aux", None, "pair", None), check_vma=False
    )
```

time: 135 us -> 71.9 us (0.53)
  blocking collectives: 42.5 us -> 0 us
  starting transfers between devices: 0.01 us -> 23.4 us
  matrix products: 22.8 us -> 0 us
  waiting for transfers between devices: 42.3 us -> 19.7 us
  Pallas kernels: 0 us -> 22.5 us
  between operations: 15.9 us -> 1.01 us
  local copies, waits for them, and re-layouts: 10.8 us -> 3.73 us
    all_to_all x1 -> x0, blocking collectives: 42.5 us -> none  [regroup(): lax.all_to_all(source, 'aux', split_axis=0, concat_axis=2, tiled=True)]
    all_gather x1 -> x0, waiting for transfers between devices: 42.3 us -> none  [shards(): lax.all_gather(paired_rows, 'pair', axis=0, tiled=True)]
    ppermute x0 -> x16, starting transfers between devices: none -> 23.4 us  [the longest x9 13.3 us: shards(): lax.ppermute(parts[d], 'aux', [(i, (i + d) % SIDE) for i in range(SIDE)])]
    dot_general x4 -> x0, matrix products: 22.8 us -> none  [the longest x3 16.3 us: shards(): jnp.einsum('mpn,ni->imp', tile_data, coeff_block, preferred_element_type=...]
    pallas_call x0 -> x6, Pallas kernels: none -> 22.5 us  [the longest x2 9.43 us: half_call(): pl.pallas_call(functools.partial(half_next, first, count), in_specs=[VMEM...]
    ppermute x0 -> x16, waiting for transfers between devices: none -> 19.7 us  [the longest x9 12.3 us: shards(): lax.ppermute(parts[d], 'aux', [(i, (i + d) % SIDE) for i in range(SIDE)])]
    reshape x2 -> x0, local copies, waits for them, and re-layouts: 3.46 us -> none  [the longest x1 2.74 us: shards(): lax.all_gather(paired_rows, 'pair', axis=0, tiled=True)]
    dynamic_slice x0 -> x1, local copies, waits for them, and re-layouts: none -> 2.86 us  [shards(): lax.dynamic_slice_in_dim(metric_root, (aux - d + SIDE) % SIDE * width, wi...]
  transfers between devices with their start and end apart: 1 -> 16, of which waited for: 1 -> 7; matrix products, arithmetic and copies ran while one was open for 1% -> 6% of each run, Pallas kernels for 0% -> 22%
where the time goes in v1:
time: 71.9 us; the launch traced here: 71.5 us
  starting transfers between devices  23.4 us (33%)
  Pallas kernels  22.5 us (31%)
  waiting for transfers between devices  19.7 us (27%)
  local copies, waits for them, and re-layouts  3.73 us (5%)
  other arithmetic  1.19 us (2%)
  between operations  1.01 us (1%)
    ppermute x9, starting transfers between devices, shards(): lax.ppermute(parts[d], 'aux', [(i, (i + d) % SIDE) for i in range(SIDE)])  13.3 us
    ppermute x9, waiting for transfers between devices, shards(): lax.ppermute(parts[d], 'aux', [(i, (i + d) % SIDE) for i in range(SIDE)])  12.3 us
    ppermute x6, starting transfers between devices, gather_coeff(): lax.ppermute(mine, 'pair', line_perm(phase, step))  10 us
    pallas_call x2, Pallas kernels, half_call(): pl.pallas_call(functools.partial(half_next, first, count), in_specs=[VMEM...  9.43 us
    pallas_call x3, Pallas kernels, fit_call(): pl.pallas_call(functools.partial(fit_kernel, first, count), in_specs=spec...  8.93 us
    ppermute x6, waiting for transfers between devices, gather_coeff(): lax.ppermute(mine, 'pair', line_perm(phase, step))  7.42 us
    pallas_call x1, Pallas kernels, half_call(): pl.pallas_call(functools.partial(half_first, first, count), in_specs=[SME...  4.11 us
    dynamic_slice x1, local copies, waits for them, and re-layouts, shards(): lax.dynamic_slice_in_dim(metric_root, (aux - d + SIDE) % SIDE * width, wi...  2.86 us
  transfers between devices with their start and end apart: 16, of which 7 were waited for; matrix products, arithmetic and copies ran while one was open for 6% of the time, Pallas kernels for 22%

profile of v1, /device:TPU:6, one launch (start us, length us, event | category | flops | bytes accessed | tf_op | source)
XLA Modules:
  0.0 71.5 jit_solution(12180530343534489667)
XLA Ops:
  0.0 1.4 %collective-permute-start = (bf16[1,64,256]{2,1,0:T(8,128)(2,1)}, bf16[1,64,256]{2,1,0:T(8,128)(2,1)S(1)}, u32[]{:S(2)}, u32[]{:S(2)}) collective-permute-start(bf16[1,64,256]{2,1,0:T(8,128)(2,1)} %bitcast.7), channel_id=1, source_target_pairs={{0,16},{1,5},{2,18},{3,7},{4,20},{5,1},{6,22},{7,3},{8,24},{9,13},... | collective-permute-start | bytes 98312 | tf_op jit(solution)/shard_map/ppermute | solution.py:46
  1.4 2.1 %collective-permute-start.1 = (bf16[1,64,256]{2,1,0:T(8,128)(2,1)}, bf16[1,64,256]{2,1,0:T(8,128)(2,1)S(1)}, u32[]{:S(2)}, u32[]{:S(2)}) collective-permute-start(bf16[1,64,256]{2,1,0:T(8,128)(2,1)} %bitcast.8), channel_id=1, source_target_pairs={{0,8},{1,3},{2,10},{3,5},{4,12},{5,7},{6,14},{7,1},{8,16},{9,11},{... | collective-permute-start | bytes 98312 | tf_op jit(solution)/shard_map/ppermute | solution.py:46
  3.5 0.0 collective-permute-start.2
  3.5 0.8 %constant_dynamic-update-slice_fusion.6 = bf16[16,64,256]{2,1,0:T(8,128)(2,1)S(1)} fusion(bf16[256,64]{0,1:T(8,128)(2,1)} %param.6), kind=kLoop, calls=%fused_computation.8 | loop fusion | bytes 65536
  4.3 1.3 %collective-permute-done = bf16[1,64,256]{2,1,0:T(8,128)(2,1)S(1)} collective-permute-done((bf16[1,64,256]{2,1,0:T(8,128)(2,1)}, bf16[1,64,256]{2,1,0:T(8,128)(2,1)S(1)}, u32[]{:S(2)}, u32[]{:S(2)}) %collective-permute-start) | collective-permute-done | bytes 32800 | tf_op jit(solution)/shard_map/ppermute | solution.py:46
  5.6 0.0 collective-permute-done.1
  5.6 3.2 %collective-permute-done.2 = bf16[1,64,256]{2,1,0:T(8,128)(2,1)S(1)} collective-permute-done((bf16[1,64,256]{2,1,0:T(8,128)(2,1)}, bf16[1,64,256]{2,1,0:T(8,128)(2,1)S(1)}, u32[]{:S(2)}, u32[]{:S(2)}) %collective-permute-start.2) | collective-permute-done | bytes 32800 | tf_op jit(solution)/shard_map/ppermute | solution.py:46
  8.8 0.8 %pad_maximum_fusion.1 = bf16[4,64,256]{2,1,0:T(8,128)(2,1)S(1)} fusion(bf16[1,64,256]{2,1,0:T(8,128)(2,1)S(1)} %collective-permute-done.2, bf16[1,64,256]{2,1,0:T(8,128)(2,1)S(1)} %collective-permute-done.1, bf16[1,64,256]{2,1,0:T(8,128)(2,1)S(1)} %collective-permute-done, bf16[1,64,256]{2,1,0:T(8,128)(2,1)} %bitcast.10), kind=kLoop, calls=%fused_computation.1 | loop fusion | flops 196608 | bytes 262144 | tf_op jit(solution)/shard_map/concatenate | solution.py:45
  9.6 3.3 %collective-permute-start.3 = (bf16[4,64,256]{2,1,0:T(8,128)(2,1)S(1)}, bf16[4,64,256]{2,1,0:T(8,128)(2,1)S(1)}, u32[]{:S(2)}, u32[]{:S(2)}) collective-permute-start(bf16[4,64,256]{2,1,0:T(8,128)(2,1)S(1)} %pad_maximum_fusion.1), channel_id=1, source_target_pairs={{0,4},{1,17},{2,6},{3,19},{4,0},{5,21},{6,2},{7,23},{8,12},{9,25},... | collective-permute-start | bytes 393224 | tf_op jit(solution)/shard_map/ppermute | solution.py:46
  12.9 0.7 collective-permute-start.4
  13.6 2.6 %collective-permute-start.5 = (bf16[4,64,256]{2,1,0:T(8,128)(2,1)S(1)}, bf16[4,64,256]{2,1,0:T(8,128)(2,1)S(1)}, u32[]{:S(2)}, u32[]{:S(2)}) collective-permute-start(bf16[4,64,256]{2,1,0:T(8,128)(2,1)S(1)} %pad_maximum_fusion.1), channel_id=1, source_target_pairs={{0,6},{1,25},{2,0},{3,27},{4,2},{5,29},{6,4},{7,31},{8,14},{9,1},{... | collective-permute-start | bytes 393224 | tf_op jit(solution)/shard_map/ppermute | solution.py:46
  16.1 0.0 collective-permute-done.3
  16.2 2.9 %collective-permute-done.4 = bf16[4,64,256]{2,1,0:T(8,128)(2,1)S(1)} collective-permute-done((bf16[4,64,256]{2,1,0:T(8,128)(2,1)S(1)}, bf16[4,64,256]{2,1,0:T(8,128)(2,1)S(1)}, u32[]{:S(2)}, u32[]{:S(2)}) %collective-permute-start.4) | collective-permute-done | bytes 131104 | tf_op jit(solution)/shard_map/ppermute | solution.py:46
  19.1 0.0 collective-permute-done.5
  19.1 0.1 collective-permute-start.6
  19.9 0.0 copy-start
  19.9 2.9 %constant_dynamic-slice_fusion.3 = (bf16[1536,384]{1,0:T(8,128)(2,1)S(1)}, bf16[1536,384]{1,0:T(8,128)(2,1)S(1)}, bf16[1536,384]{1,0:T(8,128)(2,1)S(1)}, bf16[1536,384]{1,0:T(8,128)(2,1)S(1)}) fusion(bf16[1536,1536]{1,0:T(8,128)(2,1)} %param.9, s32[]{:T(128)S(6)} %select_n.32, s32[]{:T(128)S(6)} %select_n.34, s32[]{:T(128)S(6)} %select_n.38, s32[]{:T(128)S(6)} %select_n.36), kind=kLoop, calls=%fused_computation.12 | loop fusion | bytes 9437200 | tf_op jit(solution)/shard_map/dynamic_slice | solution.py:200
  22.8 0.0 collective-permute-done.6.partner_ref
  22.8 0.0 copy-done
  22.8 4.1 %shard_map.55 = (bf16[16,16,384]{2,1,0:T(8,128)(2,1)S(1)}, bf16[16,16,384]{2,1,0:T(8,128)(2,1)S(1)}, bf16[16,16,384]{2,1,0:T(8,128)(2,1)S(1)}, bf16[16,16,384]{2,1,0:T(8,128)(2,1)S(1)}, bf16[64,384]{1,0:T(8,128)(2,1)S(1)}) custom-call(s32[1,3]{1,0:T(1,128)S(1)} %copy-done, s32[1,1]{1,0:T(1,128)S(6)} %copy.17.count_ref, ...), custom_call_target="tpu_custom_call" | custom-call | flops 1207959552 | bytes 4718592 | tf_op jit(solution)/shard_map/pallas_call | solution.py:130
  26.9 2.0 %collective-permute-start.13 = (bf16[16,16,384]{2,1,0:T(8,128)(2,1)S(1)}, bf16[16,16,384]{2,1,0:T(8,128)(2,1)S(1)}, u32[]{:S(2)}, u32[]{:S(2)}) collective-permute-start(bf16[16,16,384]{2,1,0:T(8,128)(2,1)S(1)} %get-tuple-element.28), channel_id=1, source_target_pairs={{0,32},{32,64},{64,96},{96,0},{1,33},{33,65},{65,97},{97,1},{2,34}... | collective-permute-start | bytes 589832 | tf_op jit(solution)/shard_map/ppermute | solution.py:211
  28.9 3.6 %collective-permute-start.14 = (bf16[16,16,384]{2,1,0:T(8,128)(2,1)S(1)}, bf16[16,16,384]{2,1,0:T(8,128)(2,1)S(1)}, u32[]{:S(2)}, u32[]{:S(2)}) collective-permute-start(bf16[16,16,384]{2,1,0:T(8,128)(2,1)S(1)} %get-tuple-element.29), channel_id=1, source_target_pairs={{0,64},{32,96},{64,0},{96,32},{1,65},{33,97},{65,1},{97,33},{2,66}... | collective-permute-start | bytes 589832 | tf_op jit(solution)/shard_map/ppermute | solution.py:211
  32.5 1.0 %collective-permute-start.15 = (bf16[16,16,384]{2,1,0:T(8,128)(2,1)S(1)}, bf16[16,16,384]{2,1,0:T(8,128)(2,1)S(1)}, u32[]{:S(2)}, u32[]{:S(2)}) collective-permute-start(bf16[16,16,384]{2,1,0:T(8,128)(2,1)S(1)} %get-tuple-element.30), channel_id=1, source_target_pairs={{0,96},{32,0},{64,32},{96,64},{1,97},{33,1},{65,33},{97,65},{2,98}... | collective-permute-start | bytes 589832 | tf_op jit(solution)/shard_map/ppermute | solution.py:211
  33.5 5.9 %shard_map.57 = (bf16[16,32,384]{2,1,0:T(8,128)(2,1)S(1)}, bf16[16,32,384]{2,1,0:T(8,128)(2,1)S(1)}, bf16[16,32,384]{2,1,0:T(8,128)(2,1)S(1)}, bf16[16,32,384]{2,1,0:T(8,128)(2,1)S(1)}) custom-call(bf16[64,384]{1,0:T(8,128)(2,1)S(1)} %get-tuple-element.18.cc_ref, bf16[3,64,384,128]{3,2,1,0:T(8,128)(2,1)} %integrals_ref.5), custom_call_target="tpu_custom_call" | custom-call | flops 2415919104 | bytes 9437184 | tf_op jit(solution)/shard_map/pallas_call | solution.py:138
  39.4 1.1 %collective-permute-start.10 = (bf16[16,32,384]{2,1,0:T(8,128)(2,1)S(1)}, bf16[16,32,384]{2,1,0:T(8,128)(2,1)S(1)}, u32[]{:S(2)}, u32[]{:S(2)}) collective-permute-start(bf16[16,32,384]{2,1,0:T(8,128)(2,1)S(1)} %get-tuple-element.24), channel_id=1, source_target_pairs={{0,32},{32,64},{64,96},{96,0},{1,33},{33,65},{65,97},{97,1},{2,34}... | collective-permute-start | bytes 1179656 | tf_op jit(solution)/shard_map/ppermute | solution.py:211
  40.5 0.4 collective-permute-start.11
  40.9 0.0 collective-permute-done.13.refs_1_
  40.9 2.3 %collective-permute-start.12 = (bf16[16,32,384]{2,1,0:T(8,128)(2,1)S(1)}, bf16[16,32,384]{2,1,0:T(8,128)(2,1)S(1)}, u32[]{:S(2)}, u32[]{:S(2)}) collective-permute-start(bf16[16,32,384]{2,1,0:T(8,128)(2,1)S(1)} %get-tuple-element.26), channel_id=1, source_target_pairs={{0,96},{32,0},{64,32},{96,64},{1,97},{33,1},{65,33},{97,65},{2,98}... | collective-permute-start | bytes 1179656 | tf_op jit(solution)/shard_map/ppermute | solution.py:211
  43.2 0.4 pad_maximum_fusion.refs_4_
  43.7 3.6 %shard_map.56 = (bf16[16,16,384]{2,1,0:T(8,128)(2,1)S(1)}, bf16[16,16,384]{2,1,0:T(8,128)(2,1)S(1)}, bf16[16,16,384]{2,1,0:T(8,128)(2,1)S(1)}, bf16[16,16,384]{2,1,0:T(8,128)(2,1)S(1)}) custom-call(bf16[64,384]{1,0:T(8,128)(2,1)S(1)} %get-tuple-element.18.cc_ref, bf16[3,64,384,128]{3,2,1,0:T(8,128)(2,1)} %integrals_ref.5), custom_call_target="tpu_custom_call" | custom-call | flops 1207959552 | bytes 4718592 | tf_op jit(solution)/shard_map/pallas_call | solution.py:138
  47.2 0.0 collective-permute-done.14.refs_2_
  47.2 0.4 collective-permute-start.7
  47.6 0.0 collective-permute-done.15.refs_3_
  47.6 2.5 %collective-permute-start.8 = (bf16[16,16,384]{2,1,0:T(8,128)(2,1)S(1)}, bf16[16,16,384]{2,1,0:T(8,128)(2,1)S(1)}, u32[]{:S(2)}, u32[]{:S(2)}) collective-permute-start(bf16[16,16,384]{2,1,0:T(8,128)(2,1)S(1)} %get-tuple-element.21), channel_id=1, source_target_pairs={{0,64},{32,96},{64,0},{96,32},{1,65},{33,97},{65,1},{97,33},{2,66}... | collective-permute-start | bytes 589832 | tf_op jit(solution)/shard_map/ppermute | solution.py:211
  50.1 2.5 %shard_map.58.refs_5_ = bf16[16,64,1536]{2,1,0:T(8,128)(2,1)} custom-call(bf16[16,16,384]{2,1,0:T(8,128)(2,1)S(1)} %get-tuple-element.27.refs_0_, bf16[16,16,384]{2,1,0:T(8,128)(2,1)S(1)} %collective-permute-done.13.refs_1_, bf16[16,16,384]{2,1,0:T(8,128)(2,1)S(1)} %collective-permute-done.14.refs_2_, ...), custom_call_target="tpu_custom_call" | custom-call | flops 1207959552 | bytes 1572864 | tf_op jit(solution)/shard_map/pallas_call | solution.py:178
  52.6 8.3 %collective-permute-done.10.refs_1_ = bf16[16,32,384]{2,1,0:T(8,128)(2,1)S(1)} collective-permute-done((bf16[16,32,384]{2,1,0:T(8,128)(2,1)S(1)}, bf16[16,32,384]{2,1,0:T(8,128)(2,1)S(1)}, u32[]{:S(2)}, u32[]{:S(2)}) %collective-permute-start.10) | collective-permute-done | bytes 393248 | tf_op jit(solution)/shard_map/ppermute | solution.py:211
  60.9 0.0 collective-permute-start.9
  60.9 0.0 collective-permute-done.11.refs_2_
  60.9 1.1 %collective-permute-done.12.refs_3_ = bf16[16,32,384]{2,1,0:T(8,128)(2,1)S(1)} collective-permute-done((bf16[16,32,384]{2,1,0:T(8,128)(2,1)S(1)}, bf16[16,32,384]{2,1,0:T(8,128)(2,1)S(1)}, u32[]{:S(2)}, u32[]{:S(2)}) %collective-permute-start.12) | collective-permute-done | bytes 393248 | tf_op jit(solution)/shard_map/ppermute | solution.py:211
  62.0 3.8 %shard_map.59.refs_5_ = bf16[16,64,1536]{2,1,0:T(8,128)(2,1)} custom-call(bf16[16,32,384]{2,1,0:T(8,128)(2,1)S(1)} %get-tuple-element.23.refs_0_, bf16[16,32,384]{2,1,0:T(8,128)(2,1)S(1)} %collective-permute-done.10.refs_1_, bf16[16,32,384]{2,1,0:T(8,128)(2,1)S(1)} %collective-permute-done.11.refs_2_, ...), custom_call_target="tpu_custom_call", output_to_operand_aliasing={{}: (5, {})} | custom-call | flops 2415919104 | bytes 3145728 | tf_op jit(solution)/shard_map/pallas_call | solution.py:178
  65.9 2.3 %collective-permute-done.7.refs_1_ = bf16[16,16,384]{2,1,0:T(8,128)(2,1)S(1)} collective-permute-done((bf16[16,16,384]{2,1,0:T(8,128)(2,1)S(1)}, bf16[16,16,384]{2,1,0:T(8,128)(2,1)S(1)}, u32[]{:S(2)}, u32[]{:S(2)}) %collective-permute-start.7) | collective-permute-done | bytes 196640 | tf_op jit(solution)/shard_map/ppermute | solution.py:211
  68.1 0.0 collective-permute-done.8.refs_2_
  68.1 0.6 collective-permute-done.9.refs_3_
  68.8 2.5 %shard_map.60 = bf16[16,64,1536]{2,1,0:T(8,128)(2,1)} custom-call(bf16[16,16,384]{2,1,0:T(8,128)(2,1)S(1)} %get-tuple-element.19.refs_0_, bf16[16,16,384]{2,1,0:T(8,128)(2,1)S(1)} %collective-permute-done.7.refs_1_, bf16[16,16,384]{2,1,0:T(8,128)(2,1)S(1)} %collective-permute-done.8.refs_2_, ...), custom_call_target="tpu_custom_call", output_to_operand_aliasing={{}: (5, {})} | custom-call | flops 1207959552 | bytes 1572864 | tf_op jit(solution)/shard_map/pallas_call | solution.py:178
  (6 shorter events, 0.0 us)
Async XLA Ops:
  0.0 5.6 %collective-permute-start = (bf16[1,64,256]{2,1,0:T(8,128)(2,1)}, bf16[1,64,256]{2,1,0:T(8,128)(2,1)S(1)}, u32[]{:S(2)}, u32[]{:S(2)}) collective-permute-start(bf16[1,64,256]{2,1,0:T(8,128)(2,1)} %bitcast.7), channel_id=1, source_target_pairs={{0,16},{1,5},{2,18},{3,7},{4,20},{5,1},{6,22},{7,3},{8,24},{9,13},... | collective-permute-start | bytes 98312 | tf_op jit(solution)/shard_map/ppermute | solution.py:46
  1.4 4.2 %collective-permute-start.1 = (bf16[1,64,256]{2,1,0:T(8,128)(2,1)}, bf16[1,64,256]{2,1,0:T(8,128)(2,1)S(1)}, u32[]{:S(2)}, u32[]{:S(2)}) collective-permute-start(bf16[1,64,256]{2,1,0:T(8,128)(2,1)} %bitcast.8), channel_id=1, source_target_pairs={{0,8},{1,3},{2,10},{3,5},{4,12},{5,7},{6,14},{7,1},{8,16},{9,11},{... | collective-permute-start | bytes 98312 | tf_op jit(solution)/shard_map/ppermute | solution.py:46
  3.5 5.3 %collective-permute-start.2 = (bf16[1,64,256]{2,1,0:T(8,128)(2,1)}, bf16[1,64,256]{2,1,0:T(8,128)(2,1)S(1)}, u32[]{:S(2)}, u32[]{:S(2)}) collective-permute-start(bf16[1,64,256]{2,1,0:T(8,128)(2,1)} %bitcast.9), channel_id=1, source_target_pairs={{0,24},{1,7},{2,26},{3,1},{4,28},{5,3},{6,30},{7,5},{8,0},{9,15},{... | collective-permute-start | bytes 98312 | tf_op jit(solution)/shard_map/ppermute | solution.py:46
  9.6 6.6 %collective-permute-start.3 = (bf16[4,64,256]{2,1,0:T(8,128)(2,1)S(1)}, bf16[4,64,256]{2,1,0:T(8,128)(2,1)S(1)}, u32[]{:S(2)}, u32[]{:S(2)}) collective-permute-start(bf16[4,64,256]{2,1,0:T(8,128)(2,1)S(1)} %pad_maximum_fusion.1), channel_id=1, source_target_pairs={{0,4},{1,17},{2,6},{3,19},{4,0},{5,21},{6,2},{7,23},{8,12},{9,25},... | collective-permute-start | bytes 393224 | tf_op jit(solution)/shard_map/ppermute | solution.py:46
  12.9 6.2 %collective-permute-start.4 = (bf16[4,64,256]{2,1,0:T(8,128)(2,1)S(1)}, bf16[4,64,256]{2,1,0:T(8,128)(2,1)S(1)}, u32[]{:S(2)}, u32[]{:S(2)}) collective-permute-start(bf16[4,64,256]{2,1,0:T(8,128)(2,1)S(1)} %pad_maximum_fusion.1), channel_id=1, source_target_pairs={{0,2},{1,9},{2,4},{3,11},{4,6},{5,13},{6,0},{7,15},{8,10},{9,17},{... | collective-permute-start | bytes 393224 | tf_op jit(solution)/shard_map/ppermute | solution.py:46
  13.6 5.5 %collective-permute-start.5 = (bf16[4,64,256]{2,1,0:T(8,128)(2,1)S(1)}, bf16[4,64,256]{2,1,0:T(8,128)(2,1)S(1)}, u32[]{:S(2)}, u32[]{:S(2)}) collective-permute-start(bf16[4,64,256]{2,1,0:T(8,128)(2,1)S(1)} %pad_maximum_fusion.1), channel_id=1, source_target_pairs={{0,6},{1,25},{2,0},{3,27},{4,2},{5,29},{6,4},{7,31},{8,14},{9,1},{... | collective-permute-start | bytes 393224 | tf_op jit(solution)/shard_map/ppermute | solution.py:46
  19.1 3.7 %collective-permute-start.6 = (bf16[16,64,256]{2,1,0:T(8,128)(2,1)S(1)}, bf16[16,64,256]{2,1,0:T(8,128)(2,1)S(1)}, u32[]{:S(2)}, u32[]{:S(2)}) collective-permute-start(bf16[16,64,256]{2,1,0:T(8,128)(2,1)S(1)} %constant_dynamic-update-slice_fusion.mine_ref), channel_id=1, source_target_pairs={{0,1},{1,0},{2,3},{3,2},{4,5},{5,4},{6,7},{7,6},{8,9},{9,8},{10,11... | collective-permute-start | bytes 1572872 | tf_op jit(solution)/shard_map/ppermute | solution.py:48
  19.9 2.9 %copy-start = (s32[1,3]{1,0:T(1,128)S(1)}, s32[1,3]{1,0:T(1,128)}, u32[]{:S(2)}) copy-start(s32[1,3]{1,0:T(1,128)} %nu_ref.1) | copy-start | bytes 40
  26.9 14.0 %collective-permute-start.13 = (bf16[16,16,384]{2,1,0:T(8,128)(2,1)S(1)}, bf16[16,16,384]{2,1,0:T(8,128)(2,1)S(1)}, u32[]{:S(2)}, u32[]{:S(2)}) collective-permute-start(bf16[16,16,384]{2,1,0:T(8,128)(2,1)S(1)} %get-tuple-element.28), channel_id=1, source_target_pairs={{0,32},{32,64},{64,96},{96,0},{1,33},{33,65},{65,97},{97,1},{2,34}... | collective-permute-start | bytes 589832 | tf_op jit(solution)/shard_map/ppermute | solution.py:211
  28.9 18.3 %collective-permute-start.14 = (bf16[16,16,384]{2,1,0:T(8,128)(2,1)S(1)}, bf16[16,16,384]{2,1,0:T(8,128)(2,1)S(1)}, u32[]{:S(2)}, u32[]{:S(2)}) collective-permute-start(bf16[16,16,384]{2,1,0:T(8,128)(2,1)S(1)} %get-tuple-element.29), channel_id=1, source_target_pairs={{0,64},{32,96},{64,0},{96,32},{1,65},{33,97},{65,1},{97,33},{2,66}... | collective-permute-start | bytes 589832 | tf_op jit(solution)/shard_map/ppermute | solution.py:211
  32.5 15.1 %collective-permute-start.15 = (bf16[16,16,384]{2,1,0:T(8,128)(2,1)S(1)}, bf16[16,16,384]{2,1,0:T(8,128)(2,1)S(1)}, u32[]{:S(2)}, u32[]{:S(2)}) collective-permute-start(bf16[16,16,384]{2,1,0:T(8,128)(2,1)S(1)} %get-tuple-element.30), channel_id=1, source_target_pairs={{0,96},{32,0},{64,32},{96,64},{1,97},{33,1},{65,33},{97,65},{2,98}... | collective-permute-start | bytes 589832 | tf_op jit(solution)/shard_map/ppermute | solution.py:211
  39.4 21.6 %collective-permute-start.10 = (bf16[16,32,384]{2,1,0:T(8,128)(2,1)S(1)}, bf16[16,32,384]{2,1,0:T(8,128)(2,1)S(1)}, u32[]{:S(2)}, u32[]{:S(2)}) collective-permute-start(bf16[16,32,384]{2,1,0:T(8,128)(2,1)S(1)} %get-tuple-element.24), channel_id=1, source_target_pairs={{0,32},{32,64},{64,96},{96,0},{1,33},{33,65},{65,97},{97,1},{2,34}... | collective-permute-start | bytes 1179656 | tf_op jit(solution)/shard_map/ppermute | solution.py:211
  40.5 20.5 %collective-permute-start.11 = (bf16[16,32,384]{2,1,0:T(8,128)(2,1)S(1)}, bf16[16,32,384]{2,1,0:T(8,128)(2,1)S(1)}, u32[]{:S(2)}, u32[]{:S(2)}) collective-permute-start(bf16[16,32,384]{2,1,0:T(8,128)(2,1)S(1)} %get-tuple-element.25), channel_id=1, source_target_pairs={{0,64},{32,96},{64,0},{96,32},{1,65},{33,97},{65,1},{97,33},{2,66}... | collective-permute-start | bytes 1179656 | tf_op jit(solution)/shard_map/ppermute | solution.py:211
  40.9 21.1 %collective-permute-start.12 = (bf16[16,32,384]{2,1,0:T(8,128)(2,1)S(1)}, bf16[16,32,384]{2,1,0:T(8,128)(2,1)S(1)}, u32[]{:S(2)}, u32[]{:S(2)}) collective-permute-start(bf16[16,32,384]{2,1,0:T(8,128)(2,1)S(1)} %get-tuple-element.26), channel_id=1, source_target_pairs={{0,96},{32,0},{64,32},{96,64},{1,97},{33,1},{65,33},{97,65},{2,98}... | collective-permute-start | bytes 1179656 | tf_op jit(solution)/shard_map/ppermute | solution.py:211
  47.2 20.9 %collective-permute-start.7 = (bf16[16,16,384]{2,1,0:T(8,128)(2,1)S(1)}, bf16[16,16,384]{2,1,0:T(8,128)(2,1)S(1)}, u32[]{:S(2)}, u32[]{:S(2)}) collective-permute-start(bf16[16,16,384]{2,1,0:T(8,128)(2,1)S(1)} %get-tuple-element.20), channel_id=1, source_target_pairs={{0,32},{32,64},{64,96},{96,0},{1,33},{33,65},{65,97},{97,1},{2,34}... | collective-permute-start | bytes 589832 | tf_op jit(solution)/shard_map/ppermute | solution.py:211
  47.6 20.5 %collective-permute-start.8 = (bf16[16,16,384]{2,1,0:T(8,128)(2,1)S(1)}, bf16[16,16,384]{2,1,0:T(8,128)(2,1)S(1)}, u32[]{:S(2)}, u32[]{:S(2)}) collective-permute-start(bf16[16,16,384]{2,1,0:T(8,128)(2,1)S(1)} %get-tuple-element.21), channel_id=1, source_target_pairs={{0,64},{32,96},{64,0},{96,32},{1,65},{33,97},{65,1},{97,33},{2,66}... | collective-permute-start | bytes 589832 | tf_op jit(solution)/shard_map/ppermute | solution.py:211
  60.9 7.8 %collective-permute-start.9 = (bf16[16,16,384]{2,1,0:T(8,128)(2,1)S(1)}, bf16[16,16,384]{2,1,0:T(8,128)(2,1)S(1)}, u32[]{:S(2)}, u32[]{:S(2)}) collective-permute-start(bf16[16,16,384]{2,1,0:T(8,128)(2,1)S(1)} %get-tuple-element.22), channel_id=1, source_target_pairs={{0,96},{32,0},{64,32},{96,64},{1,97},{33,1},{65,33},{97,65},{2,98}... | collective-permute-start | bytes 589832 | tf_op jit(solution)/shard_map/ppermute | solution.py:211

commit v2 on v1

v2 whole, which is shorter than its diff:
```python
import functools

import jax
import jax.numpy as jnp
from jax import lax
from jax.experimental import pallas as pl
from jax.experimental.pallas import tpu as pltpu
from jax.sharding import PartitionSpec as P

NT = (((1,), (1,)), ((), ()))
VMEM = pl.BlockSpec(memory_space=pltpu.VMEM)
SMEM = pl.BlockSpec(memory_space=pltpu.SMEM)
HBM = pl.BlockSpec(memory_space=pltpu.HBM)

SIDE = 4
GROUP = 16
BLOCK = 4
CHUNKS = ((0, 16), (16, 32), (48, 16))
STAGED = 24
HOPS = (0, 1, 2, 3)
LINES = ((0, 2, 1, 3), (0, 3, 1, 2))


def place_of(phase, step):
    place = 0
    for k, other in enumerate(LINES[phase]):
        place = jnp.where(step == other, k, place)
    return place


def coords(p):
    return p // (2 * SIDE), (p // 2) % SIDE, p % 2


def line_perm(phase, step):
    pairs = []
    for p in range(2 * SIDE * SIDE):
        x, y, core = coords(p)
        if core == phase:
            x = (x + step) % SIDE
        else:
            y = (y + step) % SIDE
        pairs.append((p, (x * SIDE + y) * 2 + core))
    return pairs


def gather_coeff(coeff_t, integrals):
    own = coeff_t[None]
    tiles = stage_call(integrals)
    line = jnp.concatenate(
        [own] + [lax.ppermute(own, "pair", line_perm(0, step)) for step in LINES[0][1:]], 0
    )
    line, tiles = lax.optimization_barrier((line, tiles))
    mine = [line] + [lax.ppermute(line, "pair", line_perm(1, step)) for step in LINES[1][1:]]
    swap = [(p, p ^ 1) for p in range(2 * SIDE * SIDE)]
    partner = [lax.ppermute(lines, "pair", swap) for lines in mine]
    return mine + partner, tiles


def pick_coeff(nu_ref, count_ref, coeff_refs, cc_ref):
    aux = lax.axis_index("aux")
    pair = lax.axis_index("pair")
    my_x, my_y, my_core = coords(pair)
    width = cc_ref.shape[1] // 3
    for slot in range(3):
        block = nu_ref[0, slot]
        x, y, core = coords(block // 2)
        step_x = (my_x - x + SIDE) % SIDE
        step_y = (my_y - y + SIDE) % SIDE
        first_step = place_of(0, jnp.where(core == 0, step_x, step_y))
        second_step = place_of(1, jnp.where(core == 0, step_y, step_x))
        which = jnp.where(core == my_core, 0, SIDE) + second_step
        lanes = pl.ds(pl.multiple_of((block % 2) * width, width), width)
        live = slot < count_ref[0, 0]
        for d in range(SIDE):
            rows = pl.ds(pl.multiple_of(((aux + d) % SIDE) * 16, 16), 16)
            chosen = coeff_refs[0][first_step, rows, lanes]
            for k in range(1, 2 * SIDE):
                chosen = jnp.where(which == k, coeff_refs[k][first_step, rows, lanes], chosen)
            cc_ref[16 * d:16 * d + 16, width * slot:width * (slot + 1)] = jnp.where(
                live, chosen, jnp.zeros_like(chosen)
            )


def stage_kernel(integrals_ref, tiles_ref, sems):
    copies = []
    for b in range(STAGED // BLOCK):
        copy = pltpu.make_async_copy(integrals_ref.at[:, pl.ds(b * BLOCK, BLOCK)], tiles_ref.at[b], sems.at[b])
        copy.start()
        copies.append(copy)
    for copy in copies:
        copy.wait()


def stage_call(integrals):
    return pl.pallas_call(
        stage_kernel,
        in_specs=[HBM],
        out_specs=VMEM,
        out_shape=jax.ShapeDtypeStruct((STAGED // BLOCK, 3, BLOCK) + integrals.shape[2:], integrals.dtype),
        scratch_shapes=[pltpu.SemaphoreType.DMA((STAGED // BLOCK,))],
        compiler_params=pltpu.CompilerParams(vmem_limit_bytes=40 * 2**20),
        cost_estimate=pl.CostEstimate(
            flops=0, bytes_accessed=2 * STAGED * integrals.shape[2] * 384 * 2, transcendentals=0
        ),
    )(integrals)


def half_body(count, cc_ref, out_refs, acc, block):
    cc = cc_ref[...]
    width = out_refs[0].shape[2]
    parts = width // 128
    for g in range(count // GROUP):
        for k in range(GROUP // BLOCK):
            b = g * (GROUP // BLOCK) + k
            tiles, at = block(b)
            tile = jnp.concatenate([tiles[at, s].reshape(BLOCK * width, 128) for s in range(3)], axis=1)
            prod = lax.dot_general(cc, tile, NT, preferred_element_type=jnp.float32)
            for j in range(BLOCK):
                for q in range(parts):
                    lane = (j * parts + q) * 128
                    acc[g, q, pl.ds(k * BLOCK + j, 64, stride=GROUP), :] = prod[:, lane:lane + 128]
        for d in range(SIDE):
            for q in range(parts):
                rows = acc[g, q, 256 * d:256 * d + 256, :].astype(jnp.bfloat16)
                out_refs[d][:, GROUP * g:GROUP * (g + 1), 128 * q:128 * (q + 1)] = rows.reshape(16, GROUP, 128)


def half_first(count, nu_ref, count_ref, *refs):
    coeff_refs, (tiles, o0, o1, o2, o3, cc_ref, acc) = refs[:2 * SIDE], refs[2 * SIDE:]
    pick_coeff(nu_ref, count_ref, coeff_refs, cc_ref)
    half_body(count, cc_ref, (o0, o1, o2, o3), acc, lambda b: (tiles, b))


def half_next(first, count, held, cc_ref, integrals_ref, *refs):
    o0, o1, o2, o3, acc, tiles, sems = refs[-7:]
    copies = []
    for b in range(held, count // BLOCK):
        copy = pltpu.make_async_copy(
            integrals_ref.at[:, pl.ds(first + b * BLOCK, BLOCK)], tiles.at[b - held], sems.at[b - held]
        )
        copy.start()
        copies.append(copy)

    def block(b):
        if b < held:
            return refs[0], CHUNKS[0][1] // BLOCK + b
        copies[b - held].wait()
        return tiles, b - held

    half_body(count, cc_ref, (o0, o1, o2, o3), acc, block)


def half_call(first, count, integrals, tiles, cc, picked_from):
    width = integrals.shape[2]
    outs = [jax.ShapeDtypeStruct((16, count, width), jnp.bfloat16)] * SIDE
    acc = pltpu.VMEM((count // GROUP, width // 128, 64 * GROUP, 128), jnp.float32)
    cost = pl.CostEstimate(
        flops=2 * count * width * 384 * 256, bytes_accessed=count * width * 384 * 2, transcendentals=0
    )
    if cc is None:
        res = pl.pallas_call(
            functools.partial(half_first, count),
            in_specs=[SMEM, SMEM] + [VMEM] * (2 * SIDE + 1),
            out_specs=[VMEM] * 5,
            out_shape=outs + [jax.ShapeDtypeStruct((64, 384), jnp.bfloat16)],
            scratch_shapes=[acc],
            compiler_params=pltpu.CompilerParams(vmem_limit_bytes=24 * 2**20),
            cost_estimate=cost,
        )(*picked_from, tiles)
        return res[:SIDE], res[SIDE]
    operands, specs, held = [cc, integrals], [VMEM, HBM], 0
    if first < STAGED:
        operands.append(tiles)
        specs.append(VMEM)
        held = (STAGED - first) // BLOCK
    copied = count // BLOCK - held
    res = pl.pallas_call(
        functools.partial(half_next, first, count, held),
        in_specs=specs,
        out_specs=[VMEM] * 4,
        out_shape=outs,
        scratch_shapes=[
            acc,
            pltpu.VMEM((copied, 3, BLOCK, width, 128), jnp.bfloat16),
            pltpu.SemaphoreType.DMA((copied,)),
        ],
        compiler_params=pltpu.CompilerParams(vmem_limit_bytes=42 * 2**20),
        cost_estimate=cost,
    )(*operands)
    return res, cc


def arrange_kernel(root_ref, after_ref, out_ref, sems):
    aux = lax.axis_index("aux")
    width = out_ref.shape[1] // SIDE
    copies = []
    for k, d in enumerate(HOPS):
        source = pl.ds(pl.multiple_of(((aux - d + SIDE) % SIDE) * width, 128), width)
        copy = pltpu.make_async_copy(
            root_ref.at[:, source], out_ref.at[:, pl.ds(k * width, width)], sems.at[k]
        )
        copy.start()
        copies.append(copy)
    for copy in copies:
        copy.wait()


def arrange_root(root, after):
    return pl.pallas_call(
        arrange_kernel,
        in_specs=[HBM, HBM],
        out_specs=VMEM,
        out_shape=jax.ShapeDtypeStruct(root.shape, root.dtype),
        scratch_shapes=[pltpu.SemaphoreType.DMA((SIDE,))],
        compiler_params=pltpu.CompilerParams(vmem_limit_bytes=40 * 2**20),
        cost_estimate=pl.CostEstimate(flops=0, bytes_accessed=root.size // 64, transcendentals=0),
    )(root, after)


def fit_kernel(first, count, *refs):
    a_refs, root_ref, (out_ref, stage, sems) = refs[:4], refs[4], refs[-3:]
    rows = 16 * count
    step = stage.shape[3]
    arrived = jnp.concatenate([a[...].reshape(rows, a.shape[2]) for a in a_refs], axis=1)
    copies = []
    for q in range(stage.shape[0]):
        prod = lax.dot_general(
            arrived, root_ref[q * step:(q + 1) * step, :], NT, preferred_element_type=jnp.float32
        )
        stage[q] = prod.astype(jnp.bfloat16).reshape(16, count, step)
        copy = pltpu.make_async_copy(
            stage.at[q], out_ref.at[:, pl.ds(first, count), pl.ds(q * step, step)], sems.at[q]
        )
        copy.start()
        copies.append(copy)
    for copy in copies:
        copy.wait()


def fit_call(first, count, arrived, root, out):
    total = root.shape[0]
    step = total if count == GROUP else 512
    operands = list(arrived) + [root]
    specs = [VMEM] * 5
    aliases = {}
    if out is not None:
        operands.append(out)
        specs.append(HBM)
        aliases = {5: 0}
    return pl.pallas_call(
        functools.partial(fit_kernel, first, count),
        in_specs=specs,
        out_specs=HBM,
        out_shape=jax.ShapeDtypeStruct((16, 64, total), jnp.bfloat16),
        scratch_shapes=[
            pltpu.VMEM((total // step, 16, count, step), jnp.bfloat16),
            pltpu.SemaphoreType.DMA((total // step,)),
        ],
        input_output_aliases=aliases,
        compiler_params=pltpu.CompilerParams(vmem_limit_bytes=24 * 2**20),
        cost_estimate=pl.CostEstimate(
            flops=32 * count * total * total, bytes_accessed=16 * count * total * 4, transcendentals=0
        ),
    )(*operands)


def shards(integrals, coefficients, nu_blocks, tile_count, metric_root):
    coeff, tiles = gather_coeff(coefficients.T, integrals)
    cc = None
    held = []
    for k, (first, count) in enumerate(CHUNKS):
        if k >= 2:
            cc, held[k - 2] = lax.optimization_barrier((cc, held[k - 2]))
        parts, cc = half_call(first, count, integrals, tiles, cc, [nu_blocks, tile_count] + coeff)
        held.append(
            [parts[0]]
            + [lax.ppermute(parts[d], "aux", [(i, (i + d) % SIDE) for i in range(SIDE)]) for d in HOPS[1:]]
        )
    root = arrange_root(metric_root, parts[0])
    out = None
    for (first, count), arrived in zip(CHUNKS, held):
        out = fit_call(first, count, arrived, root, out)
    return out.reshape(out.shape[0], out.shape[1], 1, out.shape[2])


def solution(mesh):
    placed = (
        P("pair", None, "aux", None),
        P("pair", None),
        P("aux", "pair"),
        P("aux", "pair"),
        P(),
    )
    return jax.shard_map(
        shards, mesh=mesh, in_specs=placed, out_specs=P("aux", None, "pair", None), check_vma=False
    )
```

time: 71.9 us -> 65.6 us (0.912)
  local copies, waits for them, and re-layouts: 3.73 us -> 0.01 us
  waiting for transfers between devices: 19.7 us -> 17.1 us
  other arithmetic: 1.19 us -> 0.02 us
  starting transfers between devices: 23.4 us -> 24.5 us
    dynamic_slice x1 -> x0, local copies, waits for them, and re-layouts: 2.86 us -> none  [shards(): lax.dynamic_slice_in_dim(metric_root, (aux - d + SIDE) % SIDE * width, wi...]
    ppermute x7 -> x10, waiting for transfers between devices: 7.42 us -> 5.14 us  [the longest x3 2.47 us: gather_coeff(): lax.ppermute(line, 'pair', line_perm(1, step))]
    concatenate x2 -> x1, other arithmetic: 1.19 us -> 0.02 us  [gather_coeff(): jnp.concatenate([own] + [lax.ppermute(own, 'pair', line_perm(0, step)) fo...]
    pallas_call x3 -> x5, Pallas kernels: 13.5 us -> 14.5 us  [the longest x2 8.4 us: half_call(): pl.pallas_call(functools.partial(half_next, first, count, held), in_specs...]
    unnamed x8, local copies, waits for them, and re-layouts: 0.86 us -> 0.01 us
    ppermute x7 -> x10, starting transfers between devices: 10.1 us -> 10.9 us  [the longest x3 6.51 us: gather_coeff(): lax.ppermute(line, 'pair', line_perm(1, step))]
  transfers between devices with their start and end apart: 16 -> 19, of which waited for: 7 -> 9; matrix products, arithmetic and copies ran while one was open for 6% -> 0% of each run, Pallas kernels for 22% -> 28%
where the time goes in v2:
time: 65.6 us; the launch traced here: 65.5 us
  starting transfers between devices  24.5 us (37%)
  Pallas kernels  23 us (35%)
  waiting for transfers between devices  17.1 us (26%)
  between operations  0.93 us (1%)
    ppermute x9, starting transfers between devices, shards(): lax.ppermute(parts[d], 'aux', [(i, (i + d) % SIDE) for i in range(SIDE)])  13.5 us
    ppermute x9, waiting for transfers between devices, shards(): lax.ppermute(parts[d], 'aux', [(i, (i + d) % SIDE) for i in range(SIDE)])  12 us
    pallas_call x3, Pallas kernels, fit_call(): pl.pallas_call(functools.partial(fit_kernel, first, count), in_specs=spec...  8.46 us
    pallas_call x2, Pallas kernels, half_call(): pl.pallas_call(functools.partial(half_next, first, count, held), in_specs...  8.4 us
    ppermute x3, starting transfers between devices, gather_coeff(): lax.ppermute(line, 'pair', line_perm(1, step))  6.51 us
    ppermute x3, starting transfers between devices, gather_coeff(): lax.ppermute(own, 'pair', line_perm(0, step))  3.43 us
    pallas_call x1, Pallas kernels, stage_call(): pl.pallas_call(stage_kernel, in_specs=[HBM], out_specs=VMEM, out_shape=ja...  3.09 us
    pallas_call x1, Pallas kernels, half_call(): pl.pallas_call(functools.partial(half_first, count), in_specs=[SMEM, SMEM...  2.48 us
  transfers between devices with their start and end apart: 19, of which 9 were waited for; matrix products, arithmetic and copies ran while one was open for 0% of the time, Pallas kernels for 28%

profile of v2, /device:TPU:6, one launch (start us, length us, event | category | flops | bytes accessed | tf_op | source)
XLA Modules:
  0.0 65.5 jit_solution(8662075244018035937)
XLA Ops:
  0.0 0.0 copy-start.1
  0.0 0.0 copy-start
  0.0 0.8 %collective-permute-start.2 = (bf16[1,64,256]{2,1,0:T(8,128)(2,1)}, bf16[1,64,256]{2,1,0:T(8,128)(2,1)S(1)}, u32[]{:S(2)}, u32[]{:S(2)}) collective-permute-start(bf16[1,64,256]{2,1,0:T(8,128)(2,1)} %bitcast.8), channel_id=1, source_target_pairs={{0,24},{1,7},{2,26},{3,1},{4,28},{5,3},{6,30},{7,5},{8,0},{9,15},{... | collective-permute-start | bytes 98312 | tf_op jit(solution)/shard_map/ppermute | solution.py:51
  0.8 2.4 %collective-permute-start.1 = (bf16[1,64,256]{2,1,0:T(8,128)(2,1)}, bf16[1,64,256]{2,1,0:T(8,128)(2,1)S(1)}, u32[]{:S(2)}, u32[]{:S(2)}) collective-permute-start(bf16[1,64,256]{2,1,0:T(8,128)(2,1)} %bitcast.9), channel_id=1, source_target_pairs={{0,8},{1,3},{2,10},{3,5},{4,12},{5,7},{6,14},{7,1},{8,16},{9,11},{... | collective-permute-start | bytes 98312 | tf_op jit(solution)/shard_map/ppermute | solution.py:51
  3.2 0.2 collective-permute-start
  3.4 3.1 %shard_map.55.refs_8_.refs_0_ = bf16[6,3,4,384,128]{4,3,2,1,0:T(8,128)(2,1)S(1)} custom-call(bf16[3,64,384,128]{3,2,1,0:T(8,128)(2,1)} %integrals_ref.5), custom_call_target="tpu_custom_call" | custom-call | bytes 14155776 | tf_op jit(solution)/shard_map/pallas_call | solution.py:96
  6.5 0.0 collective-permute-done.2
  6.5 0.0 collective-permute-done.1
  6.6 2.3 %collective-permute-done = bf16[1,64,256]{2,1,0:T(8,128)(2,1)S(1)} collective-permute-done((bf16[1,64,256]{2,1,0:T(8,128)(2,1)}, bf16[1,64,256]{2,1,0:T(8,128)(2,1)S(1)}, u32[]{:S(2)}, u32[]{:S(2)}) %collective-permute-start) | collective-permute-done | bytes 32800 | tf_op jit(solution)/shard_map/ppermute | solution.py:51
  8.9 0.0 copy-done.1
  8.9 3.3 %collective-permute-start.5 = (bf16[4,64,256]{2,1,0:T(8,128)(2,1)S(1)}, bf16[4,64,256]{2,1,0:T(8,128)(2,1)S(1)}, u32[]{:S(2)}, u32[]{:S(2)}) collective-permute-start(bf16[4,64,256]{2,1,0:T(8,128)(2,1)S(1)} %pad_maximum_fusion.refs_0_), channel_id=1, source_target_pairs={{0,4},{1,17},{2,6},{3,19},{4,0},{5,21},{6,2},{7,23},{8,12},{9,25},... | collective-permute-start | bytes 393224 | tf_op jit(solution)/shard_map/ppermute | solution.py:54
  12.2 0.7 %collective-permute-start.4 = (bf16[4,64,256]{2,1,0:T(8,128)(2,1)S(1)}, bf16[4,64,256]{2,1,0:T(8,128)(2,1)S(1)}, u32[]{:S(2)}, u32[]{:S(2)}) collective-permute-start(bf16[4,64,256]{2,1,0:T(8,128)(2,1)S(1)} %pad_maximum_fusion.refs_0_), channel_id=1, source_target_pairs={{0,2},{1,9},{2,4},{3,11},{4,6},{5,13},{6,0},{7,15},{8,10},{9,17},{... | collective-permute-start | bytes 393224 | tf_op jit(solution)/shard_map/ppermute | solution.py:54
  12.8 2.6 %collective-permute-start.3 = (bf16[4,64,256]{2,1,0:T(8,128)(2,1)S(1)}, bf16[4,64,256]{2,1,0:T(8,128)(2,1)S(1)}, u32[]{:S(2)}, u32[]{:S(2)}) collective-permute-start(bf16[4,64,256]{2,1,0:T(8,128)(2,1)S(1)} %pad_maximum_fusion.refs_0_), channel_id=1, source_target_pairs={{0,6},{1,25},{2,0},{3,27},{4,2},{5,29},{6,4},{7,31},{8,14},{9,1},{... | collective-permute-start | bytes 393224 | tf_op jit(solution)/shard_map/ppermute | solution.py:54
  15.4 0.0 collective-permute-start.6
  15.4 0.0 collective-permute-done.5.refs_3_
  15.4 0.5 collective-permute-start.9
  15.9 2.4 %collective-permute-done.4.refs_2_ = bf16[4,64,256]{2,1,0:T(8,128)(2,1)S(1)} collective-permute-done((bf16[4,64,256]{2,1,0:T(8,128)(2,1)S(1)}, bf16[4,64,256]{2,1,0:T(8,128)(2,1)S(1)}, u32[]{:S(2)}, u32[]{:S(2)}) %collective-permute-start.4) | collective-permute-done | bytes 131104 | tf_op jit(solution)/shard_map/ppermute | solution.py:54
  18.4 0.0 collective-permute-start.8
  18.4 0.0 collective-permute-done.3.refs_1_
  18.4 0.5 collective-permute-start.7
  19.5 0.0 collective-permute-done.6.refs_4_
  19.5 0.0 collective-permute-done.9.refs_7_
  19.5 0.2 collective-permute-done.8.refs_6_
  19.7 0.2 collective-permute-done.7.refs_5_
  19.9 0.0 copy-done
  19.9 0.0 slice-start
  19.9 2.5 %shard_map.56 = (bf16[16,16,384]{2,1,0:T(8,128)(2,1)S(1)}, bf16[16,16,384]{2,1,0:T(8,128)(2,1)S(1)}, bf16[16,16,384]{2,1,0:T(8,128)(2,1)S(1)}, bf16[16,16,384]{2,1,0:T(8,128)(2,1)S(1)}, bf16[64,384]{1,0:T(8,128)(2,1)S(1)}) custom-call(s32[1,3]{1,0:T(1,128)S(1)} %copy-done, s32[1,1]{1,0:T(1,128)S(6)} %copy.11.count_ref, ...), custom_call_target="tpu_custom_call" | custom-call | flops 1207959552 | bytes 4718592 | tf_op jit(solution)/shard_map/pallas_call | solution.py:162
  22.4 2.0 %collective-permute-start.10 = (bf16[16,16,384]{2,1,0:T(8,128)(2,1)S(1)}, bf16[16,16,384]{2,1,0:T(8,128)(2,1)S(1)}, u32[]{:S(2)}, u32[]{:S(2)}) collective-permute-start(bf16[16,16,384]{2,1,0:T(8,128)(2,1)S(1)} %get-tuple-element.29), channel_id=1, source_target_pairs={{0,32},{32,64},{64,96},{96,0},{1,33},{33,65},{65,97},{97,1},{2,34}... | collective-permute-start | bytes 589832 | tf_op jit(solution)/shard_map/ppermute | solution.py:278
  24.4 3.6 %collective-permute-start.11 = (bf16[16,16,384]{2,1,0:T(8,128)(2,1)S(1)}, bf16[16,16,384]{2,1,0:T(8,128)(2,1)S(1)}, u32[]{:S(2)}, u32[]{:S(2)}) collective-permute-start(bf16[16,16,384]{2,1,0:T(8,128)(2,1)S(1)} %get-tuple-element.30), channel_id=1, source_target_pairs={{0,64},{32,96},{64,0},{96,32},{1,65},{33,97},{65,1},{97,33},{2,66}... | collective-permute-start | bytes 589832 | tf_op jit(solution)/shard_map/ppermute | solution.py:278
  28.0 1.0 %collective-permute-start.12 = (bf16[16,16,384]{2,1,0:T(8,128)(2,1)S(1)}, bf16[16,16,384]{2,1,0:T(8,128)(2,1)S(1)}, u32[]{:S(2)}, u32[]{:S(2)}) collective-permute-start(bf16[16,16,384]{2,1,0:T(8,128)(2,1)S(1)} %get-tuple-element.31), channel_id=1, source_target_pairs={{0,96},{32,0},{64,32},{96,64},{1,97},{33,1},{65,33},{97,65},{2,98}... | collective-permute-start | bytes 589832 | tf_op jit(solution)/shard_map/ppermute | solution.py:278
  29.0 0.0 slice-start.1
  29.0 4.8 %shard_map.59 = (bf16[16,32,384]{2,1,0:T(8,128)(2,1)S(1)}, bf16[16,32,384]{2,1,0:T(8,128)(2,1)S(1)}, bf16[16,32,384]{2,1,0:T(8,128)(2,1)S(1)}, bf16[16,32,384]{2,1,0:T(8,128)(2,1)S(1)}) custom-call(bf16[64,384]{1,0:T(8,128)(2,1)S(1)} %get-tuple-element.32.cc_ref, bf16[3,64,384,128]{3,2,1,0:T(8,128)(2,1)} %integrals_ref.5, ...), custom_call_target="tpu_custom_call" | custom-call | flops 2415919104 | bytes 9437184 | tf_op jit(solution)/shard_map/pallas_call | solution.py:178
  33.8 1.1 %collective-permute-start.16 = (bf16[16,32,384]{2,1,0:T(8,128)(2,1)S(1)}, bf16[16,32,384]{2,1,0:T(8,128)(2,1)S(1)}, u32[]{:S(2)}, u32[]{:S(2)}) collective-permute-start(bf16[16,32,384]{2,1,0:T(8,128)(2,1)S(1)} %get-tuple-element.38), channel_id=1, source_target_pairs={{0,32},{32,64},{64,96},{96,0},{1,33},{33,65},{65,97},{97,1},{2,34}... | collective-permute-start | bytes 1179656 | tf_op jit(solution)/shard_map/ppermute | solution.py:278
  34.9 0.5 collective-permute-start.17
  35.3 0.0 collective-permute-done.10.refs_1_
  35.3 2.3 %collective-permute-start.18 = (bf16[16,32,384]{2,1,0:T(8,128)(2,1)S(1)}, bf16[16,32,384]{2,1,0:T(8,128)(2,1)S(1)}, u32[]{:S(2)}, u32[]{:S(2)}) collective-permute-start(bf16[16,32,384]{2,1,0:T(8,128)(2,1)S(1)} %get-tuple-element.40), channel_id=1, source_target_pairs={{0,96},{32,0},{64,32},{96,64},{1,97},{33,1},{65,33},{97,65},{2,98}... | collective-permute-start | bytes 1179656 | tf_op jit(solution)/shard_map/ppermute | solution.py:278
  37.7 0.2 collective-permute-done.11.refs_2_
  37.9 0.0 collective-permute-done.12.refs_3_
  37.9 3.6 %shard_map.57 = (bf16[16,16,384]{2,1,0:T(8,128)(2,1)S(1)}, bf16[16,16,384]{2,1,0:T(8,128)(2,1)S(1)}, bf16[16,16,384]{2,1,0:T(8,128)(2,1)S(1)}, bf16[16,16,384]{2,1,0:T(8,128)(2,1)S(1)}) custom-call(bf16[64,384]{1,0:T(8,128)(2,1)S(1)} %get-tuple-element.32.cc_ref, bf16[3,64,384,128]{3,2,1,0:T(8,128)(2,1)} %integrals_ref.5), custom_call_target="tpu_custom_call" | custom-call | flops 1207959552 | bytes 4718592 | tf_op jit(solution)/shard_map/pallas_call | solution.py:178
  41.4 0.7 %collective-permute-start.13 = (bf16[16,16,384]{2,1,0:T(8,128)(2,1)S(1)}, bf16[16,16,384]{2,1,0:T(8,128)(2,1)S(1)}, u32[]{:S(2)}, u32[]{:S(2)}) collective-permute-start(bf16[16,16,384]{2,1,0:T(8,128)(2,1)S(1)} %get-tuple-element.34), channel_id=1, source_target_pairs={{0,32},{32,64},{64,96},{96,0},{1,33},{33,65},{65,97},{97,1},{2,34}... | collective-permute-start | bytes 589832 | tf_op jit(solution)/shard_map/ppermute | solution.py:278
  42.1 2.4 %collective-permute-start.14 = (bf16[16,16,384]{2,1,0:T(8,128)(2,1)S(1)}, bf16[16,16,384]{2,1,0:T(8,128)(2,1)S(1)}, u32[]{:S(2)}, u32[]{:S(2)}) collective-permute-start(bf16[16,16,384]{2,1,0:T(8,128)(2,1)S(1)} %get-tuple-element.35), channel_id=1, source_target_pairs={{0,64},{32,96},{64,0},{96,32},{1,65},{33,97},{65,1},{97,33},{2,66}... | collective-permute-start | bytes 589832 | tf_op jit(solution)/shard_map/ppermute | solution.py:278
  44.5 0.0 slice-done
  44.5 0.0 slice-done.1
  44.5 0.5 shard_map.58.refs_4_
  45.1 2.3 %shard_map.60.refs_5_ = bf16[16,64,1536]{2,1,0:T(8,128)(2,1)} custom-call(bf16[16,16,384]{2,1,0:T(8,128)(2,1)S(1)} %get-tuple-element.41.refs_0_, bf16[16,16,384]{2,1,0:T(8,128)(2,1)S(1)} %collective-permute-done.10.refs_1_, bf16[16,16,384]{2,1,0:T(8,128)(2,1)S(1)} %collective-permute-done.11.refs_2_, ...), custom_call_target="tpu_custom_call" | custom-call | flops 1207959552 | bytes 1572864 | tf_op jit(solution)/shard_map/pallas_call | solution.py:251
  47.4 8.2 %collective-permute-done.16.refs_1_ = bf16[16,32,384]{2,1,0:T(8,128)(2,1)S(1)} collective-permute-done((bf16[16,32,384]{2,1,0:T(8,128)(2,1)S(1)}, bf16[16,32,384]{2,1,0:T(8,128)(2,1)S(1)}, u32[]{:S(2)}, u32[]{:S(2)}) %collective-permute-start.16) | collective-permute-done | bytes 393248 | tf_op jit(solution)/shard_map/ppermute | solution.py:278
  55.6 0.0 collective-permute-start.15
  55.6 0.0 collective-permute-done.17.refs_2_
  55.6 0.9 %collective-permute-done.18.refs_3_ = bf16[16,32,384]{2,1,0:T(8,128)(2,1)S(1)} collective-permute-done((bf16[16,32,384]{2,1,0:T(8,128)(2,1)S(1)}, bf16[16,32,384]{2,1,0:T(8,128)(2,1)S(1)}, u32[]{:S(2)}, u32[]{:S(2)}) %collective-permute-start.18) | collective-permute-done | bytes 393248 | tf_op jit(solution)/shard_map/ppermute | solution.py:278
  56.5 3.9 %shard_map.61.refs_5_ = bf16[16,64,1536]{2,1,0:T(8,128)(2,1)} custom-call(bf16[16,32,384]{2,1,0:T(8,128)(2,1)S(1)} %get-tuple-element.37.refs_0_, bf16[16,32,384]{2,1,0:T(8,128)(2,1)S(1)} %collective-permute-done.16.refs_1_, bf16[16,32,384]{2,1,0:T(8,128)(2,1)S(1)} %collective-permute-done.17.refs_2_, ...), custom_call_target="tpu_custom_call", output_to_operand_aliasing={{}: (5, {})} | custom-call | flops 2415919104 | bytes 3145728 | tf_op jit(solution)/shard_map/pallas_call | solution.py:251
  60.3 2.5 %collective-permute-done.13.refs_1_ = bf16[16,16,384]{2,1,0:T(8,128)(2,1)S(1)} collective-permute-done((bf16[16,16,384]{2,1,0:T(8,128)(2,1)S(1)}, bf16[16,16,384]{2,1,0:T(8,128)(2,1)S(1)}, u32[]{:S(2)}, u32[]{:S(2)}) %collective-permute-start.13) | collective-permute-done | bytes 196640 | tf_op jit(solution)/shard_map/ppermute | solution.py:278
  62.8 0.0 collective-permute-done.14.refs_2_
  62.8 0.3 collective-permute-done.15.refs_3_
  63.1 2.3 %shard_map.62 = bf16[16,64,1536]{2,1,0:T(8,128)(2,1)} custom-call(bf16[16,16,384]{2,1,0:T(8,128)(2,1)S(1)} %get-tuple-element.33.after_ref.refs_0_, bf16[16,16,384]{2,1,0:T(8,128)(2,1)S(1)} %collective-permute-done.13.refs_1_, bf16[16,16,384]{2,1,0:T(8,128)(2,1)S(1)} %collective-permute-done.14.refs_2_, ...), custom_call_target="tpu_custom_call", output_to_operand_aliasing={{}: (5, {})} | custom-call | flops 1207959552 | bytes 1572864 | tf_op jit(solution)/shard_map/pallas_call | solution.py:251
  (2 shorter events, 0.0 us)
Async XLA Ops:
  0.0 8.9 %copy-start.1 = (bf16[256,64]{0,1:T(8,128)(2,1)S(1)}, bf16[256,64]{0,1:T(8,128)(2,1)}, u32[]{:S(2)}) copy-start(bf16[256,64]{0,1:T(8,128)(2,1)} %param.6) | copy-start | bytes 98308
  0.0 19.9 %copy-start = (s32[1,3]{1,0:T(1,128)S(1)}, s32[1,3]{1,0:T(1,128)}, u32[]{:S(2)}) copy-start(s32[1,3]{1,0:T(1,128)} %nu_ref.1) | copy-start | bytes 40
  0.0 6.5 %collective-permute-start.2 = (bf16[1,64,256]{2,1,0:T(8,128)(2,1)}, bf16[1,64,256]{2,1,0:T(8,128)(2,1)S(1)}, u32[]{:S(2)}, u32[]{:S(2)}) collective-permute-start(bf16[1,64,256]{2,1,0:T(8,128)(2,1)} %bitcast.8), channel_id=1, source_target_pairs={{0,24},{1,7},{2,26},{3,1},{4,28},{5,3},{6,30},{7,5},{8,0},{9,15},{... | collective-permute-start | bytes 98312 | tf_op jit(solution)/shard_map/ppermute | solution.py:51
  0.8 5.7 %collective-permute-start.1 = (bf16[1,64,256]{2,1,0:T(8,128)(2,1)}, bf16[1,64,256]{2,1,0:T(8,128)(2,1)S(1)}, u32[]{:S(2)}, u32[]{:S(2)}) collective-permute-start(bf16[1,64,256]{2,1,0:T(8,128)(2,1)} %bitcast.9), channel_id=1, source_target_pairs={{0,8},{1,3},{2,10},{3,5},{4,12},{5,7},{6,14},{7,1},{8,16},{9,11},{... | collective-permute-start | bytes 98312 | tf_op jit(solution)/shard_map/ppermute | solution.py:51
  3.2 5.6 %collective-permute-start = (bf16[1,64,256]{2,1,0:T(8,128)(2,1)}, bf16[1,64,256]{2,1,0:T(8,128)(2,1)S(1)}, u32[]{:S(2)}, u32[]{:S(2)}) collective-permute-start(bf16[1,64,256]{2,1,0:T(8,128)(2,1)} %bitcast.10), channel_id=1, source_target_pairs={{0,16},{1,5},{2,18},{3,7},{4,20},{5,1},{6,22},{7,3},{8,24},{9,13},... | collective-permute-start | bytes 98312 | tf_op jit(solution)/shard_map/ppermute | solution.py:51
  8.9 6.6 %collective-permute-start.5 = (bf16[4,64,256]{2,1,0:T(8,128)(2,1)S(1)}, bf16[4,64,256]{2,1,0:T(8,128)(2,1)S(1)}, u32[]{:S(2)}, u32[]{:S(2)}) collective-permute-start(bf16[4,64,256]{2,1,0:T(8,128)(2,1)S(1)} %pad_maximum_fusion.refs_0_), channel_id=1, source_target_pairs={{0,4},{1,17},{2,6},{3,19},{4,0},{5,21},{6,2},{7,23},{8,12},{9,25},... | collective-permute-start | bytes 393224 | tf_op jit(solution)/shard_map/ppermute | solution.py:54
  12.2 6.2 %collective-permute-start.4 = (bf16[4,64,256]{2,1,0:T(8,128)(2,1)S(1)}, bf16[4,64,256]{2,1,0:T(8,128)(2,1)S(1)}, u32[]{:S(2)}, u32[]{:S(2)}) collective-permute-start(bf16[4,64,256]{2,1,0:T(8,128)(2,1)S(1)} %pad_maximum_fusion.refs_0_), channel_id=1, source_target_pairs={{0,2},{1,9},{2,4},{3,11},{4,6},{5,13},{6,0},{7,15},{8,10},{9,17},{... | collective-permute-start | bytes 393224 | tf_op jit(solution)/shard_map/ppermute | solution.py:54
  12.8 5.5 %collective-permute-start.3 = (bf16[4,64,256]{2,1,0:T(8,128)(2,1)S(1)}, bf16[4,64,256]{2,1,0:T(8,128)(2,1)S(1)}, u32[]{:S(2)}, u32[]{:S(2)}) collective-permute-start(bf16[4,64,256]{2,1,0:T(8,128)(2,1)S(1)} %pad_maximum_fusion.refs_0_), channel_id=1, source_target_pairs={{0,6},{1,25},{2,0},{3,27},{4,2},{5,29},{6,4},{7,31},{8,14},{9,1},{... | collective-permute-start | bytes 393224 | tf_op jit(solution)/shard_map/ppermute | solution.py:54
  15.4 4.1 %collective-permute-start.6 = (bf16[4,64,256]{2,1,0:T(8,128)(2,1)S(1)}, bf16[4,64,256]{2,1,0:T(8,128)(2,1)S(1)}, u32[]{:S(2)}, u32[]{:S(2)}) collective-permute-start(bf16[4,64,256]{2,1,0:T(8,128)(2,1)S(1)} %pad_maximum_fusion.refs_0_), channel_id=1, source_target_pairs={{0,1},{1,0},{2,3},{3,2},{4,5},{5,4},{6,7},{7,6},{8,9},{9,8},{10,11... | collective-permute-start | bytes 393224 | tf_op jit(solution)/shard_map/ppermute | solution.py:56
  15.4 4.1 %collective-permute-start.9 = (bf16[4,64,256]{2,1,0:T(8,128)(2,1)S(1)}, bf16[4,64,256]{2,1,0:T(8,128)(2,1)S(1)}, u32[]{:S(2)}, u32[]{:S(2)}) collective-permute-start(bf16[4,64,256]{2,1,0:T(8,128)(2,1)S(1)} %collective-permute-done.5.refs_3_), channel_id=1, source_target_pairs={{0,1},{1,0},{2,3},{3,2},{4,5},{5,4},{6,7},{7,6},{8,9},{9,8},{10,11... | collective-permute-start | bytes 393224 | tf_op jit(solution)/shard_map/ppermute | solution.py:56
  18.4 1.3 %collective-permute-start.8 = (bf16[4,64,256]{2,1,0:T(8,128)(2,1)S(1)}, bf16[4,64,256]{2,1,0:T(8,128)(2,1)S(1)}, u32[]{:S(2)}, u32[]{:S(2)}) collective-permute-start(bf16[4,64,256]{2,1,0:T(8,128)(2,1)S(1)} %collective-permute-done.4.refs_2_), channel_id=1, source_target_pairs={{0,1},{1,0},{2,3},{3,2},{4,5},{5,4},{6,7},{7,6},{8,9},{9,8},{10,11... | collective-permute-start | bytes 393224 | tf_op jit(solution)/shard_map/ppermute | solution.py:56
  18.4 1.5 %collective-permute-start.7 = (bf16[4,64,256]{2,1,0:T(8,128)(2,1)S(1)}, bf16[4,64,256]{2,1,0:T(8,128)(2,1)S(1)}, u32[]{:S(2)}, u32[]{:S(2)}) collective-permute-start(bf16[4,64,256]{2,1,0:T(8,128)(2,1)S(1)} %collective-permute-done.3.refs_1_), channel_id=1, source_target_pairs={{0,1},{1,0},{2,3},{3,2},{4,5},{5,4},{6,7},{7,6},{8,9},{9,8},{10,11... | collective-permute-start | bytes 393224 | tf_op jit(solution)/shard_map/ppermute | solution.py:56
  19.9 24.7 %slice-start = ((s8[4718592]{0:T(1024)(128)(4,1)}), s8[4194304]{0:T(1024)(128)(4,1)S(1)}, s32[]{:S(2)}) async-start(s8[4718592]{0:T(1024)(128)(4,1)} %bitcast.6), calls=%async_computation | async-start | bytes 8388608
  22.4 13.0 %collective-permute-start.10 = (bf16[16,16,384]{2,1,0:T(8,128)(2,1)S(1)}, bf16[16,16,384]{2,1,0:T(8,128)(2,1)S(1)}, u32[]{:S(2)}, u32[]{:S(2)}) collective-permute-start(bf16[16,16,384]{2,1,0:T(8,128)(2,1)S(1)} %get-tuple-element.29), channel_id=1, source_target_pairs={{0,32},{32,64},{64,96},{96,0},{1,33},{33,65},{65,97},{97,1},{2,34}... | collective-permute-start | bytes 589832 | tf_op jit(solution)/shard_map/ppermute | solution.py:278
  24.4 13.5 %collective-permute-start.11 = (bf16[16,16,384]{2,1,0:T(8,128)(2,1)S(1)}, bf16[16,16,384]{2,1,0:T(8,128)(2,1)S(1)}, u32[]{:S(2)}, u32[]{:S(2)}) collective-permute-start(bf16[16,16,384]{2,1,0:T(8,128)(2,1)S(1)} %get-tuple-element.30), channel_id=1, source_target_pairs={{0,64},{32,96},{64,0},{96,32},{1,65},{33,97},{65,1},{97,33},{2,66}... | collective-permute-start | bytes 589832 | tf_op jit(solution)/shard_map/ppermute | solution.py:278
  28.0 9.9 %collective-permute-start.12 = (bf16[16,16,384]{2,1,0:T(8,128)(2,1)S(1)}, bf16[16,16,384]{2,1,0:T(8,128)(2,1)S(1)}, u32[]{:S(2)}, u32[]{:S(2)}) collective-permute-start(bf16[16,16,384]{2,1,0:T(8,128)(2,1)S(1)} %get-tuple-element.31), channel_id=1, source_target_pairs={{0,96},{32,0},{64,32},{96,64},{1,97},{33,1},{65,33},{97,65},{2,98}... | collective-permute-start | bytes 589832 | tf_op jit(solution)/shard_map/ppermute | solution.py:278
  29.0 15.6 %slice-start.1 = ((s8[4718592]{0:T(1024)(128)(4,1)}), s8[524288]{0:T(1024)(128)(4,1)S(1)}, s32[]{:S(2)}) async-start(s8[4718592]{0:T(1024)(128)(4,1)} %bitcast.6), calls=%async_computation.1 | async-start | bytes 1048576
  33.8 21.8 %collective-permute-start.16 = (bf16[16,32,384]{2,1,0:T(8,128)(2,1)S(1)}, bf16[16,32,384]{2,1,0:T(8,128)(2,1)S(1)}, u32[]{:S(2)}, u32[]{:S(2)}) collective-permute-start(bf16[16,32,384]{2,1,0:T(8,128)(2,1)S(1)} %get-tuple-element.38), channel_id=1, source_target_pairs={{0,32},{32,64},{64,96},{96,0},{1,33},{33,65},{65,97},{97,1},{2,34}... | collective-permute-start | bytes 1179656 | tf_op jit(solution)/shard_map/ppermute | solution.py:278
  34.9 20.7 %collective-permute-start.17 = (bf16[16,32,384]{2,1,0:T(8,128)(2,1)S(1)}, bf16[16,32,384]{2,1,0:T(8,128)(2,1)S(1)}, u32[]{:S(2)}, u32[]{:S(2)}) collective-permute-start(bf16[16,32,384]{2,1,0:T(8,128)(2,1)S(1)} %get-tuple-element.39), channel_id=1, source_target_pairs={{0,64},{32,96},{64,0},{96,32},{1,65},{33,97},{65,1},{97,33},{2,66}... | collective-permute-start | bytes 1179656 | tf_op jit(solution)/shard_map/ppermute | solution.py:278
  35.3 21.1 %collective-permute-start.18 = (bf16[16,32,384]{2,1,0:T(8,128)(2,1)S(1)}, bf16[16,32,384]{2,1,0:T(8,128)(2,1)S(1)}, u32[]{:S(2)}, u32[]{:S(2)}) collective-permute-start(bf16[16,32,384]{2,1,0:T(8,128)(2,1)S(1)} %get-tuple-element.40), channel_id=1, source_target_pairs={{0,96},{32,0},{64,32},{96,64},{1,97},{33,1},{65,33},{97,65},{2,98}... | collective-permute-start | bytes 1179656 | tf_op jit(solution)/shard_map/ppermute | solution.py:278
  41.4 21.4 %collective-permute-start.13 = (bf16[16,16,384]{2,1,0:T(8,128)(2,1)S(1)}, bf16[16,16,384]{2,1,0:T(8,128)(2,1)S(1)}, u32[]{:S(2)}, u32[]{:S(2)}) collective-permute-start(bf16[16,16,384]{2,1,0:T(8,128)(2,1)S(1)} %get-tuple-element.34), channel_id=1, source_target_pairs={{0,32},{32,64},{64,96},{96,0},{1,33},{33,65},{65,97},{97,1},{2,34}... | collective-permute-start | bytes 589832 | tf_op jit(solution)/shard_map/ppermute | solution.py:278
  42.1 20.6 %collective-permute-start.14 = (bf16[16,16,384]{2,1,0:T(8,128)(2,1)S(1)}, bf16[16,16,384]{2,1,0:T(8,128)(2,1)S(1)}, u32[]{:S(2)}, u32[]{:S(2)}) collective-permute-start(bf16[16,16,384]{2,1,0:T(8,128)(2,1)S(1)} %get-tuple-element.35), channel_id=1, source_target_pairs={{0,64},{32,96},{64,0},{96,32},{1,65},{33,97},{65,1},{97,33},{2,66}... | collective-permute-start | bytes 589832 | tf_op jit(solution)/shard_map/ppermute | solution.py:278
  55.6 7.5 %collective-permute-start.15 = (bf16[16,16,384]{2,1,0:T(8,128)(2,1)S(1)}, bf16[16,16,384]{2,1,0:T(8,128)(2,1)S(1)}, u32[]{:S(2)}, u32[]{:S(2)}) collective-permute-start(bf16[16,16,384]{2,1,0:T(8,128)(2,1)S(1)} %get-tuple-element.36), channel_id=1, source_target_pairs={{0,96},{32,0},{64,32},{96,64},{1,97},{33,1},{65,33},{97,65},{2,98}... | collective-permute-start | bytes 589832 | tf_op jit(solution)/shard_map/ppermute | solution.py:278

commit v3 on v2

--- a/solution.py
+++ b/solution.py
@@ -16,8 +16,9 @@
 GROUP = 16
 BLOCK = 4
 CHUNKS = ((0, 16), (16, 32), (48, 16))
+SENDS = ((0, 1, 3, 2), (0, 3, 1, 2), (0, 1, 3, 2))
 STAGED = 24
-HOPS = (0, 1, 2, 3)
+HOPS = (0, 1, 3, 2)
 LINES = ((0, 2, 1, 3), (0, 3, 1, 2))
 
 
@@ -26,6 +27,10 @@
     for k, other in enumerate(LINES[phase]):
         place = jnp.where(step == other, k, place)
     return place
+
+
+def hop(k, core):
+    return (HOPS[k] * (1 - 2 * core)) % SIDE
 
 
 def coords(p):
@@ -42,6 +47,11 @@
             y = (y + step) % SIDE
         pairs.append((p, (x * SIDE + y) * 2 + core))
     return pairs
+
+
+def aux_perm(k):
+    pairs = 2 * SIDE * SIDE
+    return [(a * pairs + p, (a + hop(k, p % 2)) % SIDE * pairs + p) for a in range(SIDE) for p in range(pairs)]
 
 
 def gather_coeff(coeff_t, integrals):
@@ -71,15 +81,15 @@
         second_step = place_of(1, jnp.where(core == 0, step_y, step_x))
         which = jnp.where(core == my_core, 0, SIDE) + second_step
         lanes = pl.ds(pl.multiple_of((block % 2) * width, width), width)
-        live = slot < count_ref[0, 0]
+        live = jnp.broadcast_to(count_ref[...], (16, width)) > slot
         for d in range(SIDE):
-            rows = pl.ds(pl.multiple_of(((aux + d) % SIDE) * 16, 16), 16)
+            step = jnp.where(my_core == 0, hop(d, 0), hop(d, 1))
+            rows = pl.ds(pl.multiple_of(((aux + step) % SIDE) * 16, 16), 16)
             chosen = coeff_refs[0][first_step, rows, lanes]
             for k in range(1, 2 * SIDE):
                 chosen = jnp.where(which == k, coeff_refs[k][first_step, rows, lanes], chosen)
-            cc_ref[16 * d:16 * d + 16, width * slot:width * (slot + 1)] = jnp.where(
-                live, chosen, jnp.zeros_like(chosen)
-            )
+            chosen = jnp.where(live, chosen.astype(jnp.float32), 0.0)
+            cc_ref[16 * d:16 * d + 16, width * slot:width * (slot + 1)] = chosen.astype(jnp.bfloat16)
 
 
 def stage_kernel(integrals_ref, tiles_ref, sems):
@@ -161,7 +171,7 @@
     if cc is None:
         res = pl.pallas_call(
             functools.partial(half_first, count),
-            in_specs=[SMEM, SMEM] + [VMEM] * (2 * SIDE + 1),
+            in_specs=[SMEM] + [VMEM] * (2 * SIDE + 2),
             out_specs=[VMEM] * 5,
             out_shape=outs + [jax.ShapeDtypeStruct((64, 384), jnp.bfloat16)],
             scratch_shapes=[acc],
@@ -193,10 +203,12 @@
 
 def arrange_kernel(root_ref, after_ref, out_ref, sems):
     aux = lax.axis_index("aux")
+    core = lax.axis_index("pair") % 2
     width = out_ref.shape[1] // SIDE
     copies = []
-    for k, d in enumerate(HOPS):
-        source = pl.ds(pl.multiple_of(((aux - d + SIDE) % SIDE) * width, 128), width)
+    for k in range(SIDE):
+        step = jnp.where(core == 0, hop(k, 0), hop(k, 1))
+        source = pl.ds(pl.multiple_of(((aux - step + SIDE) % SIDE) * width, 128), width)
         copy = pltpu.make_async_copy(
             root_ref.at[:, source], out_ref.at[:, pl.ds(k * width, width)], sems.at[k]
         )
@@ -218,8 +230,9 @@
     )(root, after)
 
 
-def fit_kernel(first, count, *refs):
-    a_refs, root_ref, (out_ref, stage, sems) = refs[:4], refs[4], refs[-3:]
+def fit_kernel(first, count, order, *refs):
+    root_ref, (out_ref, stage, sems) = refs[4], refs[-3:]
+    a_refs = [refs[order.index(k)] for k in range(SIDE)]
     rows = 16 * count
     step = stage.shape[3]
     arrived = jnp.concatenate([a[...].reshape(rows, a.shape[2]) for a in a_refs], axis=1)
@@ -238,10 +251,10 @@
         copy.wait()
 
 
-def fit_call(first, count, arrived, root, out):
+def fit_call(first, count, order, arrived, root, out):
     total = root.shape[0]
     step = total if count == GROUP else 512
-    operands = list(arrived) + [root]
+    operands = [arrived[k] for k in order] + [root]
     specs = [VMEM] * 5
     aliases = {}
     if out is not None:
@@ -249,7 +262,7 @@
         specs.append(HBM)
         aliases = {5: 0}
     return pl.pallas_call(
-        functools.partial(fit_kernel, first, count),
+        functools.partial(fit_kernel, first, count, order),
         in_specs=specs,
         out_specs=HBM,
         out_shape=jax.ShapeDtypeStruct((16, 64, total), jnp.bfloat16),
@@ -275,12 +288,12 @@
         parts, cc = half_call(first, count, integrals, tiles, cc, [nu_blocks, tile_count] + coeff)
         held.append(
             [parts[0]]
-            + [lax.ppermute(parts[d], "aux", [(i, (i + d) % SIDE) for i in range(SIDE)]) for d in HOPS[1:]]
+            + [lax.ppermute(parts[d], ("aux", "pair"), aux_perm(d)) for d in range(1, SIDE)]
         )
     root = arrange_root(metric_root, parts[0])
     out = None
-    for (first, count), arrived in zip(CHUNKS, held):
-        out = fit_call(first, count, arrived, root, out)
+    for (first, count), order, arrived in zip(CHUNKS, SENDS, held):
+        out = fit_call(first, count, order, arrived, root, out)
     return out.reshape(out.shape[0], out.shape[1], 1, out.shape[2])
 
 

time: 65.6 us -> 65.3 us (level)
  waiting for transfers between devices: 17.1 us -> 13.8 us
  starting transfers between devices: 24.5 us -> 27.4 us
    ppermute x9, waiting for transfers between devices: 12 us -> 8.68 us  [shards(): lax.ppermute(parts[d], ('aux', 'pair'), aux_perm(d))]
    ppermute x9, starting transfers between devices: 13.5 us -> 16.5 us  [shards(): lax.ppermute(parts[d], ('aux', 'pair'), aux_perm(d))]
  transfers between devices with their start and end apart: 19 -> 19, of which waited for: 9 -> 7; matrix products, arithmetic and copies ran while one was open for 0% -> 0% of each run, Pallas kernels for 28% -> 28%
where the time goes in v3:
time: 65.3 us; the launch traced here: 65.2 us
  starting transfers between devices  27.4 us (42%)
  Pallas kernels  23 us (35%)
  waiting for transfers between devices  13.8 us (21%)
  between operations  0.96 us (1%)
    ppermute x9, starting transfers between devices, shards(): lax.ppermute(parts[d], ('aux', 'pair'), aux_perm(d))  16.5 us
    ppermute x9, waiting for transfers between devices, shards(): lax.ppermute(parts[d], ('aux', 'pair'), aux_perm(d))  8.68 us
    pallas_call x3, Pallas kernels, fit_call(): pl.pallas_call(functools.partial(fit_kernel, first, count, order), in_spe...  8.46 us
    pallas_call x2, Pallas kernels, half_call(): pl.pallas_call(functools.partial(half_next, first, count, held), in_specs...  8.39 us
    ppermute x3, starting transfers between devices, gather_coeff(): lax.ppermute(line, 'pair', line_perm(1, step))  6.51 us
    ppermute x3, starting transfers between devices, gather_coeff(): lax.ppermute(own, 'pair', line_perm(0, step))  3.43 us
    pallas_call x1, Pallas kernels, stage_call(): pl.pallas_call(stage_kernel, in_specs=[HBM], out_specs=VMEM, out_shape=ja...  3.09 us
    pallas_call x1, Pallas kernels, half_call(): pl.pallas_call(functools.partial(half_first, count), in_specs=[SMEM] + [V...  2.48 us
  transfers between devices with their start and end apart: 19, of which 7 were waited for; matrix products, arithmetic and copies ran while one was open for 0% of the time, Pallas kernels for 28%

profile of v3, /device:TPU:6, one launch (start us, length us, event | category | flops | bytes accessed | tf_op | source)
XLA Modules:
  0.0 65.2 jit_solution(7310310069468544058)
XLA Ops:
  0.0 0.0 copy-start.1
  0.0 0.0 copy-start
  0.0 0.8 %collective-permute-start.2 = (bf16[1,64,256]{2,1,0:T(8,128)(2,1)}, bf16[1,64,256]{2,1,0:T(8,128)(2,1)S(1)}, u32[]{:S(2)}, u32[]{:S(2)}) collective-permute-start(bf16[1,64,256]{2,1,0:T(8,128)(2,1)} %bitcast.8), channel_id=1, source_target_pairs={{0,24},{1,7},{2,26},{3,1},{4,28},{5,3},{6,30},{7,5},{8,0},{9,15},{... | collective-permute-start | bytes 98312 | tf_op jit(solution)/shard_map/ppermute | solution.py:61
  0.8 2.4 %collective-permute-start.1 = (bf16[1,64,256]{2,1,0:T(8,128)(2,1)}, bf16[1,64,256]{2,1,0:T(8,128)(2,1)S(1)}, u32[]{:S(2)}, u32[]{:S(2)}) collective-permute-start(bf16[1,64,256]{2,1,0:T(8,128)(2,1)} %bitcast.9), channel_id=1, source_target_pairs={{0,8},{1,3},{2,10},{3,5},{4,12},{5,7},{6,14},{7,1},{8,16},{9,11},{... | collective-permute-start | bytes 98312 | tf_op jit(solution)/shard_map/ppermute | solution.py:61
  3.2 0.2 collective-permute-start
  3.4 3.1 %shard_map.55.refs_8_.refs_0_ = bf16[6,3,4,384,128]{4,3,2,1,0:T(8,128)(2,1)S(1)} custom-call(bf16[3,64,384,128]{3,2,1,0:T(8,128)(2,1)} %integrals_ref.5), custom_call_target="tpu_custom_call" | custom-call | bytes 14155776 | tf_op jit(solution)/shard_map/pallas_call | solution.py:106
  6.5 0.0 collective-permute-done.2
  6.5 0.0 collective-permute-done.1
  6.6 2.3 %collective-permute-done = bf16[1,64,256]{2,1,0:T(8,128)(2,1)S(1)} collective-permute-done((bf16[1,64,256]{2,1,0:T(8,128)(2,1)}, bf16[1,64,256]{2,1,0:T(8,128)(2,1)S(1)}, u32[]{:S(2)}, u32[]{:S(2)}) %collective-permute-start) | collective-permute-done | bytes 32800 | tf_op jit(solution)/shard_map/ppermute | solution.py:61
  8.9 0.0 copy-done.1
  8.9 3.3 %collective-permute-start.5 = (bf16[4,64,256]{2,1,0:T(8,128)(2,1)S(1)}, bf16[4,64,256]{2,1,0:T(8,128)(2,1)S(1)}, u32[]{:S(2)}, u32[]{:S(2)}) collective-permute-start(bf16[4,64,256]{2,1,0:T(8,128)(2,1)S(1)} %pad_maximum_fusion.refs_0_), channel_id=1, source_target_pairs={{0,4},{1,17},{2,6},{3,19},{4,0},{5,21},{6,2},{7,23},{8,12},{9,25},... | collective-permute-start | bytes 393224 | tf_op jit(solution)/shard_map/ppermute | solution.py:64
  12.2 0.7 %collective-permute-start.4 = (bf16[4,64,256]{2,1,0:T(8,128)(2,1)S(1)}, bf16[4,64,256]{2,1,0:T(8,128)(2,1)S(1)}, u32[]{:S(2)}, u32[]{:S(2)}) collective-permute-start(bf16[4,64,256]{2,1,0:T(8,128)(2,1)S(1)} %pad_maximum_fusion.refs_0_), channel_id=1, source_target_pairs={{0,2},{1,9},{2,4},{3,11},{4,6},{5,13},{6,0},{7,15},{8,10},{9,17},{... | collective-permute-start | bytes 393224 | tf_op jit(solution)/shard_map/ppermute | solution.py:64
  12.8 2.6 %collective-permute-start.3 = (bf16[4,64,256]{2,1,0:T(8,128)(2,1)S(1)}, bf16[4,64,256]{2,1,0:T(8,128)(2,1)S(1)}, u32[]{:S(2)}, u32[]{:S(2)}) collective-permute-start(bf16[4,64,256]{2,1,0:T(8,128)(2,1)S(1)} %pad_maximum_fusion.refs_0_), channel_id=1, source_target_pairs={{0,6},{1,25},{2,0},{3,27},{4,2},{5,29},{6,4},{7,31},{8,14},{9,1},{... | collective-permute-start | bytes 393224 | tf_op jit(solution)/shard_map/ppermute | solution.py:64
  15.4 0.0 collective-permute-start.6
  15.4 0.0 collective-permute-done.5.refs_3_
  15.4 0.5 collective-permute-start.9
  15.9 2.4 %collective-permute-done.4.refs_2_ = bf16[4,64,256]{2,1,0:T(8,128)(2,1)S(1)} collective-permute-done((bf16[4,64,256]{2,1,0:T(8,128)(2,1)S(1)}, bf16[4,64,256]{2,1,0:T(8,128)(2,1)S(1)}, u32[]{:S(2)}, u32[]{:S(2)}) %collective-permute-start.4) | collective-permute-done | bytes 131104 | tf_op jit(solution)/shard_map/ppermute | solution.py:64
  18.4 0.0 collective-permute-start.8
  18.4 0.0 collective-permute-done.3.refs_1_
  18.4 0.5 collective-permute-start.7
  19.5 0.0 collective-permute-done.6.refs_4_
  19.5 0.0 collective-permute-done.9.refs_7_
  19.5 0.2 collective-permute-done.8.refs_6_
  19.7 0.2 collective-permute-done.7.refs_5_
  19.9 0.0 copy-done
  19.9 0.0 slice-start
  19.9 2.5 %shard_map.56 = (bf16[16,16,384]{2,1,0:T(8,128)(2,1)S(1)}, bf16[16,16,384]{2,1,0:T(8,128)(2,1)S(1)}, bf16[16,16,384]{2,1,0:T(8,128)(2,1)S(1)}, bf16[16,16,384]{2,1,0:T(8,128)(2,1)S(1)}, bf16[64,384]{1,0:T(8,128)(2,1)S(1)}) custom-call(s32[1,3]{1,0:T(1,128)S(1)} %copy-done, s32[1,1]{1,0:T(1,128)S(6)} %copy.11.count_ref, ...), custom_call_target="tpu_custom_call" | custom-call | flops 1207959552 | bytes 4718592 | tf_op jit(solution)/shard_map/pallas_call | solution.py:172
  22.4 2.0 %collective-permute-start.10 = (bf16[16,16,384]{2,1,0:T(8,128)(2,1)S(1)}, bf16[16,16,384]{2,1,0:T(8,128)(2,1)S(1)}, u32[]{:S(2)}, u32[]{:S(2)}) collective-permute-start(bf16[16,16,384]{2,1,0:T(8,128)(2,1)S(1)} %get-tuple-element.29), channel_id=1, source_target_pairs={{0,32},{1,97},{2,34},{3,99},{4,36},{5,101},{6,38},{7,103},{8,40},{... | collective-permute-start | bytes 589832 | tf_op jit(solution)/shard_map/ppermute | solution.py:291
  24.4 2.2 %collective-permute-start.11 = (bf16[16,16,384]{2,1,0:T(8,128)(2,1)S(1)}, bf16[16,16,384]{2,1,0:T(8,128)(2,1)S(1)}, u32[]{:S(2)}, u32[]{:S(2)}) collective-permute-start(bf16[16,16,384]{2,1,0:T(8,128)(2,1)S(1)} %get-tuple-element.30), channel_id=1, source_target_pairs={{0,96},{1,33},{2,98},{3,35},{4,100},{5,37},{6,102},{7,39},{8,104},... | collective-permute-start | bytes 589832 | tf_op jit(solution)/shard_map/ppermute | solution.py:291
  26.6 1.8 %collective-permute-start.12 = (bf16[16,16,384]{2,1,0:T(8,128)(2,1)S(1)}, bf16[16,16,384]{2,1,0:T(8,128)(2,1)S(1)}, u32[]{:S(2)}, u32[]{:S(2)}) collective-permute-start(bf16[16,16,384]{2,1,0:T(8,128)(2,1)S(1)} %get-tuple-element.31), channel_id=1, source_target_pairs={{0,64},{1,65},{2,66},{3,67},{4,68},{5,69},{6,70},{7,71},{8,72},{9,... | collective-permute-start | bytes 589832 | tf_op jit(solution)/shard_map/ppermute | solution.py:291
  28.4 0.0 slice-start.1
  28.4 4.8 %shard_map.59 = (bf16[16,32,384]{2,1,0:T(8,128)(2,1)S(1)}, bf16[16,32,384]{2,1,0:T(8,128)(2,1)S(1)}, bf16[16,32,384]{2,1,0:T(8,128)(2,1)S(1)}, bf16[16,32,384]{2,1,0:T(8,128)(2,1)S(1)}) custom-call(bf16[64,384]{1,0:T(8,128)(2,1)S(1)} %get-tuple-element.32.cc_ref, bf16[3,64,384,128]{3,2,1,0:T(8,128)(2,1)} %integrals_ref.5, ...), custom_call_target="tpu_custom_call" | custom-call | flops 2415919104 | bytes 9437184 | tf_op jit(solution)/shard_map/pallas_call | solution.py:188
  33.2 1.8 %collective-permute-start.16 = (bf16[16,32,384]{2,1,0:T(8,128)(2,1)S(1)}, bf16[16,32,384]{2,1,0:T(8,128)(2,1)S(1)}, u32[]{:S(2)}, u32[]{:S(2)}) collective-permute-start(bf16[16,32,384]{2,1,0:T(8,128)(2,1)S(1)} %get-tuple-element.38), channel_id=1, source_target_pairs={{0,64},{1,65},{2,66},{3,67},{4,68},{5,69},{6,70},{7,71},{8,72},{9,... | collective-permute-start | bytes 1179656 | tf_op jit(solution)/shard_map/ppermute | solution.py:291
  35.0 0.0 collective-permute-start.17
  35.0 0.0 collective-permute-done.10.refs_1_
  35.0 3.2 %collective-permute-start.18 = (bf16[16,32,384]{2,1,0:T(8,128)(2,1)S(1)}, bf16[16,32,384]{2,1,0:T(8,128)(2,1)S(1)}, u32[]{:S(2)}, u32[]{:S(2)}) collective-permute-start(bf16[16,32,384]{2,1,0:T(8,128)(2,1)S(1)} %get-tuple-element.40), channel_id=1, source_target_pairs={{0,96},{1,33},{2,98},{3,35},{4,100},{5,37},{6,102},{7,39},{8,104},... | collective-permute-start | bytes 1179656 | tf_op jit(solution)/shard_map/ppermute | solution.py:291
  38.3 5.8 %collective-permute-done.11.refs_3_ = bf16[16,16,384]{2,1,0:T(8,128)(2,1)S(1)} collective-permute-done((bf16[16,16,384]{2,1,0:T(8,128)(2,1)S(1)}, bf16[16,16,384]{2,1,0:T(8,128)(2,1)S(1)}, u32[]{:S(2)}, u32[]{:S(2)}) %collective-permute-start.11) | collective-permute-done | bytes 196640 | tf_op jit(solution)/shard_map/ppermute | solution.py:291
  44.0 0.0 collective-permute-done.12.refs_2_
  44.0 3.6 %shard_map.57 = (bf16[16,16,384]{2,1,0:T(8,128)(2,1)S(1)}, bf16[16,16,384]{2,1,0:T(8,128)(2,1)S(1)}, bf16[16,16,384]{2,1,0:T(8,128)(2,1)S(1)}, bf16[16,16,384]{2,1,0:T(8,128)(2,1)S(1)}) custom-call(bf16[64,384]{1,0:T(8,128)(2,1)S(1)} %get-tuple-element.32.cc_ref, bf16[3,64,384,128]{3,2,1,0:T(8,128)(2,1)} %integrals_ref.5), custom_call_target="tpu_custom_call" | custom-call | flops 1207959552 | bytes 4718592 | tf_op jit(solution)/shard_map/pallas_call | solution.py:188
  47.6 0.1 collective-permute-start.13
  47.7 5.3 %collective-permute-start.14 = (bf16[16,16,384]{2,1,0:T(8,128)(2,1)S(1)}, bf16[16,16,384]{2,1,0:T(8,128)(2,1)S(1)}, u32[]{:S(2)}, u32[]{:S(2)}) collective-permute-start(bf16[16,16,384]{2,1,0:T(8,128)(2,1)S(1)} %get-tuple-element.35), channel_id=1, source_target_pairs={{0,64},{1,65},{2,66},{3,67},{4,68},{5,69},{6,70},{7,71},{8,72},{9,... | collective-permute-start | bytes 589832 | tf_op jit(solution)/shard_map/ppermute | solution.py:291
  53.0 0.0 slice-done
  53.0 0.0 slice-done.1
  53.0 0.5 shard_map.58.refs_4_
  53.5 2.3 %shard_map.60.refs_5_ = bf16[16,64,1536]{2,1,0:T(8,128)(2,1)} custom-call(bf16[16,16,384]{2,1,0:T(8,128)(2,1)S(1)} %get-tuple-element.41.refs_0_, bf16[16,16,384]{2,1,0:T(8,128)(2,1)S(1)} %collective-permute-done.10.refs_1_, bf16[16,16,384]{2,1,0:T(8,128)(2,1)S(1)} %collective-permute-done.12.refs_2_, ...), custom_call_target="tpu_custom_call" | custom-call | flops 1207959552 | bytes 1572864 | tf_op jit(solution)/shard_map/pallas_call | solution.py:264
  55.8 0.0 collective-permute-done.16.refs_1_
  55.9 0.1 collective-permute-start.15
  55.9 0.0 collective-permute-done.17.refs_2_
  55.9 0.0 collective-permute-done.18.refs_3_
  56.0 3.9 %shard_map.61.refs_5_ = bf16[16,64,1536]{2,1,0:T(8,128)(2,1)} custom-call(bf16[16,32,384]{2,1,0:T(8,128)(2,1)S(1)} %get-tuple-element.37.refs_0_, bf16[16,32,384]{2,1,0:T(8,128)(2,1)S(1)} %collective-permute-done.16.refs_1_, bf16[16,32,384]{2,1,0:T(8,128)(2,1)S(1)} %collective-permute-done.17.refs_2_, ...), custom_call_target="tpu_custom_call", output_to_operand_aliasing={{}: (5, {})} | custom-call | flops 2415919104 | bytes 3145728 | tf_op jit(solution)/shard_map/pallas_call | solution.py:264
  59.8 1.6 %collective-permute-done.13.refs_1_ = bf16[16,16,384]{2,1,0:T(8,128)(2,1)S(1)} collective-permute-done((bf16[16,16,384]{2,1,0:T(8,128)(2,1)S(1)}, bf16[16,16,384]{2,1,0:T(8,128)(2,1)S(1)}, u32[]{:S(2)}, u32[]{:S(2)}) %collective-permute-start.13) | collective-permute-done | bytes 196640 | tf_op jit(solution)/shard_map/ppermute | solution.py:291
  61.4 1.3 %collective-permute-done.14.refs_2_ = bf16[16,16,384]{2,1,0:T(8,128)(2,1)S(1)} collective-permute-done((bf16[16,16,384]{2,1,0:T(8,128)(2,1)S(1)}, bf16[16,16,384]{2,1,0:T(8,128)(2,1)S(1)}, u32[]{:S(2)}, u32[]{:S(2)}) %collective-permute-start.14) | collective-permute-done | bytes 196640 | tf_op jit(solution)/shard_map/ppermute | solution.py:291
  62.7 0.0 collective-permute-done.15.refs_3_
  62.7 2.3 %shard_map.62 = bf16[16,64,1536]{2,1,0:T(8,128)(2,1)} custom-call(bf16[16,16,384]{2,1,0:T(8,128)(2,1)S(1)} %get-tuple-element.33.after_ref.refs_0_, bf16[16,16,384]{2,1,0:T(8,128)(2,1)S(1)} %collective-permute-done.13.refs_1_, bf16[16,16,384]{2,1,0:T(8,128)(2,1)S(1)} %collective-permute-done.14.refs_2_, ...), custom_call_target="tpu_custom_call", output_to_operand_aliasing={{}: (5, {})} | custom-call | flops 1207959552 | bytes 1572864 | tf_op jit(solution)/shard_map/pallas_call | solution.py:264
  (2 shorter events, 0.0 us)
Async XLA Ops:
  0.0 8.9 %copy-start.1 = (bf16[256,64]{0,1:T(8,128)(2,1)S(1)}, bf16[256,64]{0,1:T(8,128)(2,1)}, u32[]{:S(2)}) copy-start(bf16[256,64]{0,1:T(8,128)(2,1)} %param.6) | copy-start | bytes 98308
  0.0 19.9 %copy-start = (s32[1,3]{1,0:T(1,128)S(1)}, s32[1,3]{1,0:T(1,128)}, u32[]{:S(2)}) copy-start(s32[1,3]{1,0:T(1,128)} %nu_ref.1) | copy-start | bytes 40
  0.0 6.5 %collective-permute-start.2 = (bf16[1,64,256]{2,1,0:T(8,128)(2,1)}, bf16[1,64,256]{2,1,0:T(8,128)(2,1)S(1)}, u32[]{:S(2)}, u32[]{:S(2)}) collective-permute-start(bf16[1,64,256]{2,1,0:T(8,128)(2,1)} %bitcast.8), channel_id=1, source_target_pairs={{0,24},{1,7},{2,26},{3,1},{4,28},{5,3},{6,30},{7,5},{8,0},{9,15},{... | collective-permute-start | bytes 98312 | tf_op jit(solution)/shard_map/ppermute | solution.py:61
  0.8 5.7 %collective-permute-start.1 = (bf16[1,64,256]{2,1,0:T(8,128)(2,1)}, bf16[1,64,256]{2,1,0:T(8,128)(2,1)S(1)}, u32[]{:S(2)}, u32[]{:S(2)}) collective-permute-start(bf16[1,64,256]{2,1,0:T(8,128)(2,1)} %bitcast.9), channel_id=1, source_target_pairs={{0,8},{1,3},{2,10},{3,5},{4,12},{5,7},{6,14},{7,1},{8,16},{9,11},{... | collective-permute-start | bytes 98312 | tf_op jit(solution)/shard_map/ppermute | solution.py:61
  3.2 5.6 %collective-permute-start = (bf16[1,64,256]{2,1,0:T(8,128)(2,1)}, bf16[1,64,256]{2,1,0:T(8,128)(2,1)S(1)}, u32[]{:S(2)}, u32[]{:S(2)}) collective-permute-start(bf16[1,64,256]{2,1,0:T(8,128)(2,1)} %bitcast.10), channel_id=1, source_target_pairs={{0,16},{1,5},{2,18},{3,7},{4,20},{5,1},{6,22},{7,3},{8,24},{9,13},... | collective-permute-start | bytes 98312 | tf_op jit(solution)/shard_map/ppermute | solution.py:61
  8.9 6.6 %collective-permute-start.5 = (bf16[4,64,256]{2,1,0:T(8,128)(2,1)S(1)}, bf16[4,64,256]{2,1,0:T(8,128)(2,1)S(1)}, u32[]{:S(2)}, u32[]{:S(2)}) collective-permute-start(bf16[4,64,256]{2,1,0:T(8,128)(2,1)S(1)} %pad_maximum_fusion.refs_0_), channel_id=1, source_target_pairs={{0,4},{1,17},{2,6},{3,19},{4,0},{5,21},{6,2},{7,23},{8,12},{9,25},... | collective-permute-start | bytes 393224 | tf_op jit(solution)/shard_map/ppermute | solution.py:64
  12.2 6.2 %collective-permute-start.4 = (bf16[4,64,256]{2,1,0:T(8,128)(2,1)S(1)}, bf16[4,64,256]{2,1,0:T(8,128)(2,1)S(1)}, u32[]{:S(2)}, u32[]{:S(2)}) collective-permute-start(bf16[4,64,256]{2,1,0:T(8,128)(2,1)S(1)} %pad_maximum_fusion.refs_0_), channel_id=1, source_target_pairs={{0,2},{1,9},{2,4},{3,11},{4,6},{5,13},{6,0},{7,15},{8,10},{9,17},{... | collective-permute-start | bytes 393224 | tf_op jit(solution)/shard_map/ppermute | solution.py:64
  12.8 5.5 %collective-permute-start.3 = (bf16[4,64,256]{2,1,0:T(8,128)(2,1)S(1)}, bf16[4,64,256]{2,1,0:T(8,128)(2,1)S(1)}, u32[]{:S(2)}, u32[]{:S(2)}) collective-permute-start(bf16[4,64,256]{2,1,0:T(8,128)(2,1)S(1)} %pad_maximum_fusion.refs_0_), channel_id=1, source_target_pairs={{0,6},{1,25},{2,0},{3,27},{4,2},{5,29},{6,4},{7,31},{8,14},{9,1},{... | collective-permute-start | bytes 393224 | tf_op jit(solution)/shard_map/ppermute | solution.py:64
  15.4 4.1 %collective-permute-start.6 = (bf16[4,64,256]{2,1,0:T(8,128)(2,1)S(1)}, bf16[4,64,256]{2,1,0:T(8,128)(2,1)S(1)}, u32[]{:S(2)}, u32[]{:S(2)}) collective-permute-start(bf16[4,64,256]{2,1,0:T(8,128)(2,1)S(1)} %pad_maximum_fusion.refs_0_), channel_id=1, source_target_pairs={{0,1},{1,0},{2,3},{3,2},{4,5},{5,4},{6,7},{7,6},{8,9},{9,8},{10,11... | collective-permute-start | bytes 393224 | tf_op jit(solution)/shard_map/ppermute | solution.py:66
  15.4 4.1 %collective-permute-start.9 = (bf16[4,64,256]{2,1,0:T(8,128)(2,1)S(1)}, bf16[4,64,256]{2,1,0:T(8,128)(2,1)S(1)}, u32[]{:S(2)}, u32[]{:S(2)}) collective-permute-start(bf16[4,64,256]{2,1,0:T(8,128)(2,1)S(1)} %collective-permute-done.5.refs_3_), channel_id=1, source_target_pairs={{0,1},{1,0},{2,3},{3,2},{4,5},{5,4},{6,7},{7,6},{8,9},{9,8},{10,11... | collective-permute-start | bytes 393224 | tf_op jit(solution)/shard_map/ppermute | solution.py:66
  18.4 1.3 %collective-permute-start.8 = (bf16[4,64,256]{2,1,0:T(8,128)(2,1)S(1)}, bf16[4,64,256]{2,1,0:T(8,128)(2,1)S(1)}, u32[]{:S(2)}, u32[]{:S(2)}) collective-permute-start(bf16[4,64,256]{2,1,0:T(8,128)(2,1)S(1)} %collective-permute-done.4.refs_2_), channel_id=1, source_target_pairs={{0,1},{1,0},{2,3},{3,2},{4,5},{5,4},{6,7},{7,6},{8,9},{9,8},{10,11... | collective-permute-start | bytes 393224 | tf_op jit(solution)/shard_map/ppermute | solution.py:66
  18.4 1.5 %collective-permute-start.7 = (bf16[4,64,256]{2,1,0:T(8,128)(2,1)S(1)}, bf16[4,64,256]{2,1,0:T(8,128)(2,1)S(1)}, u32[]{:S(2)}, u32[]{:S(2)}) collective-permute-start(bf16[4,64,256]{2,1,0:T(8,128)(2,1)S(1)} %collective-permute-done.3.refs_1_), channel_id=1, source_target_pairs={{0,1},{1,0},{2,3},{3,2},{4,5},{5,4},{6,7},{7,6},{8,9},{9,8},{10,11... | collective-permute-start | bytes 393224 | tf_op jit(solution)/shard_map/ppermute | solution.py:66
  19.9 33.1 %slice-start = ((s8[4718592]{0:T(1024)(128)(4,1)}), s8[4194304]{0:T(1024)(128)(4,1)S(1)}, s32[]{:S(2)}) async-start(s8[4718592]{0:T(1024)(128)(4,1)} %bitcast.6), calls=%async_computation | async-start | bytes 8388608
  22.4 12.6 %collective-permute-start.10 = (bf16[16,16,384]{2,1,0:T(8,128)(2,1)S(1)}, bf16[16,16,384]{2,1,0:T(8,128)(2,1)S(1)}, u32[]{:S(2)}, u32[]{:S(2)}) collective-permute-start(bf16[16,16,384]{2,1,0:T(8,128)(2,1)S(1)} %get-tuple-element.29), channel_id=1, source_target_pairs={{0,32},{1,97},{2,34},{3,99},{4,36},{5,101},{6,38},{7,103},{8,40},{... | collective-permute-start | bytes 589832 | tf_op jit(solution)/shard_map/ppermute | solution.py:291
  24.4 19.7 %collective-permute-start.11 = (bf16[16,16,384]{2,1,0:T(8,128)(2,1)S(1)}, bf16[16,16,384]{2,1,0:T(8,128)(2,1)S(1)}, u32[]{:S(2)}, u32[]{:S(2)}) collective-permute-start(bf16[16,16,384]{2,1,0:T(8,128)(2,1)S(1)} %get-tuple-element.30), channel_id=1, source_target_pairs={{0,96},{1,33},{2,98},{3,35},{4,100},{5,37},{6,102},{7,39},{8,104},... | collective-permute-start | bytes 589832 | tf_op jit(solution)/shard_map/ppermute | solution.py:291
  26.6 17.5 %collective-permute-start.12 = (bf16[16,16,384]{2,1,0:T(8,128)(2,1)S(1)}, bf16[16,16,384]{2,1,0:T(8,128)(2,1)S(1)}, u32[]{:S(2)}, u32[]{:S(2)}) collective-permute-start(bf16[16,16,384]{2,1,0:T(8,128)(2,1)S(1)} %get-tuple-element.31), channel_id=1, source_target_pairs={{0,64},{1,65},{2,66},{3,67},{4,68},{5,69},{6,70},{7,71},{8,72},{9,... | collective-permute-start | bytes 589832 | tf_op jit(solution)/shard_map/ppermute | solution.py:291
  28.4 24.6 %slice-start.1 = ((s8[4718592]{0:T(1024)(128)(4,1)}), s8[524288]{0:T(1024)(128)(4,1)S(1)}, s32[]{:S(2)}) async-start(s8[4718592]{0:T(1024)(128)(4,1)} %bitcast.6), calls=%async_computation.1 | async-start | bytes 1048576
  33.2 22.7 %collective-permute-start.16 = (bf16[16,32,384]{2,1,0:T(8,128)(2,1)S(1)}, bf16[16,32,384]{2,1,0:T(8,128)(2,1)S(1)}, u32[]{:S(2)}, u32[]{:S(2)}) collective-permute-start(bf16[16,32,384]{2,1,0:T(8,128)(2,1)S(1)} %get-tuple-element.38), channel_id=1, source_target_pairs={{0,64},{1,65},{2,66},{3,67},{4,68},{5,69},{6,70},{7,71},{8,72},{9,... | collective-permute-start | bytes 1179656 | tf_op jit(solution)/shard_map/ppermute | solution.py:291
  35.0 20.9 %collective-permute-start.17 = (bf16[16,32,384]{2,1,0:T(8,128)(2,1)S(1)}, bf16[16,32,384]{2,1,0:T(8,128)(2,1)S(1)}, u32[]{:S(2)}, u32[]{:S(2)}) collective-permute-start(bf16[16,32,384]{2,1,0:T(8,128)(2,1)S(1)} %get-tuple-element.39), channel_id=1, source_target_pairs={{0,32},{1,97},{2,34},{3,99},{4,36},{5,101},{6,38},{7,103},{8,40},{... | collective-permute-start | bytes 1179656 | tf_op jit(solution)/shard_map/ppermute | solution.py:291
  35.0 20.9 %collective-permute-start.18 = (bf16[16,32,384]{2,1,0:T(8,128)(2,1)S(1)}, bf16[16,32,384]{2,1,0:T(8,128)(2,1)S(1)}, u32[]{:S(2)}, u32[]{:S(2)}) collective-permute-start(bf16[16,32,384]{2,1,0:T(8,128)(2,1)S(1)} %get-tuple-element.40), channel_id=1, source_target_pairs={{0,96},{1,33},{2,98},{3,35},{4,100},{5,37},{6,102},{7,39},{8,104},... | collective-permute-start | bytes 1179656 | tf_op jit(solution)/shard_map/ppermute | solution.py:291
  47.6 13.8 %collective-permute-start.13 = (bf16[16,16,384]{2,1,0:T(8,128)(2,1)S(1)}, bf16[16,16,384]{2,1,0:T(8,128)(2,1)S(1)}, u32[]{:S(2)}, u32[]{:S(2)}) collective-permute-start(bf16[16,16,384]{2,1,0:T(8,128)(2,1)S(1)} %get-tuple-element.34), channel_id=1, source_target_pairs={{0,32},{1,97},{2,34},{3,99},{4,36},{5,101},{6,38},{7,103},{8,40},{... | collective-permute-start | bytes 589832 | tf_op jit(solution)/shard_map/ppermute | solution.py:291
  47.7 15.0 %collective-permute-start.14 = (bf16[16,16,384]{2,1,0:T(8,128)(2,1)S(1)}, bf16[16,16,384]{2,1,0:T(8,128)(2,1)S(1)}, u32[]{:S(2)}, u32[]{:S(2)}) collective-permute-start(bf16[16,16,384]{2,1,0:T(8,128)(2,1)S(1)} %get-tuple-element.35), channel_id=1, source_target_pairs={{0,64},{1,65},{2,66},{3,67},{4,68},{5,69},{6,70},{7,71},{8,72},{9,... | collective-permute-start | bytes 589832 | tf_op jit(solution)/shard_map/ppermute | solution.py:291
  55.9 6.9 %collective-permute-start.15 = (bf16[16,16,384]{2,1,0:T(8,128)(2,1)S(1)}, bf16[16,16,384]{2,1,0:T(8,128)(2,1)S(1)}, u32[]{:S(2)}, u32[]{:S(2)}) collective-permute-start(bf16[16,16,384]{2,1,0:T(8,128)(2,1)S(1)} %get-tuple-element.36), channel_id=1, source_target_pairs={{0,96},{1,33},{2,98},{3,35},{4,100},{5,37},{6,102},{7,39},{8,104},... | collective-permute-start | bytes 589832 | tf_op jit(solution)/shard_map/ppermute | solution.py:291

commit v4 on v3

--- a/solution.py
+++ b/solution.py
@@ -14,6 +14,7 @@
 
 SIDE = 4
 GROUP = 16
+PITCH = 17
 BLOCK = 4
 CHUNKS = ((0, 16), (16, 32), (48, 16))
 SENDS = ((0, 1, 3, 2), (0, 3, 1, 2), (0, 1, 3, 2))
@@ -129,11 +130,12 @@
             for j in range(BLOCK):
                 for q in range(parts):
                     lane = (j * parts + q) * 128
-                    acc[g, q, pl.ds(k * BLOCK + j, 64, stride=GROUP), :] = prod[:, lane:lane + 128]
+                    acc[g, q, pl.ds(k * BLOCK + j, 64, stride=PITCH), :] = prod[:, lane:lane + 128]
         for d in range(SIDE):
             for q in range(parts):
-                rows = acc[g, q, 256 * d:256 * d + 256, :].astype(jnp.bfloat16)
-                out_refs[d][:, GROUP * g:GROUP * (g + 1), 128 * q:128 * (q + 1)] = rows.reshape(16, GROUP, 128)
+                for i in range(16):
+                    rows = acc[g, q, pl.ds((16 * d + i) * PITCH, GROUP), :].astype(jnp.bfloat16)
+                    out_refs[d][i, GROUP * g:GROUP * (g + 1), 128 * q:128 * (q + 1)] = rows
 
 
 def half_first(count, nu_ref, count_ref, *refs):
@@ -164,7 +166,7 @@
 def half_call(first, count, integrals, tiles, cc, picked_from):
     width = integrals.shape[2]
     outs = [jax.ShapeDtypeStruct((16, count, width), jnp.bfloat16)] * SIDE
-    acc = pltpu.VMEM((count // GROUP, width // 128, 64 * GROUP, 128), jnp.float32)
+    acc = pltpu.VMEM((count // GROUP, width // 128, 64 * PITCH, 128), jnp.float32)
     cost = pl.CostEstimate(
         flops=2 * count * width * 384 * 256, bytes_accessed=count * width * 384 * 2, transcendentals=0
     )

time: 65.3 us -> 65.4 us (level)
  Pallas kernels: 23 us -> 22.3 us
  transfers between devices with their start and end apart: 19 -> 19, of which waited for: 7 -> 6; matrix products, arithmetic and copies ran while one was open for 0% -> 0% of each run, Pallas kernels for 28% -> 27%
where the time goes in v4:
time: 65.4 us; the launch traced here: 65 us
  starting transfers between devices  27.6 us (42%)
  Pallas kernels  22.3 us (34%)
  waiting for transfers between devices  14.2 us (22%)
  between operations  0.97 us (1%)
    ppermute x9, starting transfers between devices, shards(): lax.ppermute(parts[d], ('aux', 'pair'), aux_perm(d))  16.6 us
    ppermute x9, waiting for transfers between devices, shards(): lax.ppermute(parts[d], ('aux', 'pair'), aux_perm(d))  9.02 us
    pallas_call x3, Pallas kernels, fit_call(): pl.pallas_call(functools.partial(fit_kernel, first, count, order), in_spe...  8.46 us
    pallas_call x2, Pallas kernels, half_call(): pl.pallas_call(functools.partial(half_next, first, count, held), in_specs...  7.87 us
    ppermute x3, starting transfers between devices, gather_coeff(): lax.ppermute(line, 'pair', line_perm(1, step))  6.51 us
    ppermute x3, starting transfers between devices, gather_coeff(): lax.ppermute(own, 'pair', line_perm(0, step))  3.43 us
    pallas_call x1, Pallas kernels, stage_call(): pl.pallas_call(stage_kernel, in_specs=[HBM], out_specs=VMEM, out_shape=ja...  3.09 us
    ppermute x3, waiting for transfers between devices, gather_coeff(): lax.ppermute(line, 'pair', line_perm(1, step))  2.47 us
  transfers between devices with their start and end apart: 19, of which 6 were waited for; matrix products, arithmetic and copies ran while one was open for 0% of the time, Pallas kernels for 27%

profile of v4, /device:TPU:6, one launch (start us, length us, event | category | flops | bytes accessed | tf_op | source)
XLA Modules:
  0.0 65.0 jit_solution(8979521212155966974)
XLA Ops:
  0.0 0.0 copy-start.1
  0.0 0.0 copy-start
  0.0 0.8 %collective-permute-start.2 = (bf16[1,64,256]{2,1,0:T(8,128)(2,1)}, bf16[1,64,256]{2,1,0:T(8,128)(2,1)S(1)}, u32[]{:S(2)}, u32[]{:S(2)}) collective-permute-start(bf16[1,64,256]{2,1,0:T(8,128)(2,1)} %bitcast.8), channel_id=1, source_target_pairs={{0,24},{1,7},{2,26},{3,1},{4,28},{5,3},{6,30},{7,5},{8,0},{9,15},{... | collective-permute-start | bytes 98312 | tf_op jit(solution)/shard_map/ppermute | solution.py:62
  0.8 2.4 %collective-permute-start.1 = (bf16[1,64,256]{2,1,0:T(8,128)(2,1)}, bf16[1,64,256]{2,1,0:T(8,128)(2,1)S(1)}, u32[]{:S(2)}, u32[]{:S(2)}) collective-permute-start(bf16[1,64,256]{2,1,0:T(8,128)(2,1)} %bitcast.9), channel_id=1, source_target_pairs={{0,8},{1,3},{2,10},{3,5},{4,12},{5,7},{6,14},{7,1},{8,16},{9,11},{... | collective-permute-start | bytes 98312 | tf_op jit(solution)/shard_map/ppermute | solution.py:62
  3.2 0.2 collective-permute-start
  3.4 3.1 %shard_map.55.refs_8_.refs_0_ = bf16[6,3,4,384,128]{4,3,2,1,0:T(8,128)(2,1)S(1)} custom-call(bf16[3,64,384,128]{3,2,1,0:T(8,128)(2,1)} %integrals_ref.5), custom_call_target="tpu_custom_call" | custom-call | bytes 14155776 | tf_op jit(solution)/shard_map/pallas_call | solution.py:107
  6.5 0.0 collective-permute-done.2
  6.5 0.0 collective-permute-done.1
  6.6 2.3 %collective-permute-done = bf16[1,64,256]{2,1,0:T(8,128)(2,1)S(1)} collective-permute-done((bf16[1,64,256]{2,1,0:T(8,128)(2,1)}, bf16[1,64,256]{2,1,0:T(8,128)(2,1)S(1)}, u32[]{:S(2)}, u32[]{:S(2)}) %collective-permute-start) | collective-permute-done | bytes 32800 | tf_op jit(solution)/shard_map/ppermute | solution.py:62
  8.9 0.0 copy-done.1
  8.9 3.3 %collective-permute-start.5 = (bf16[4,64,256]{2,1,0:T(8,128)(2,1)S(1)}, bf16[4,64,256]{2,1,0:T(8,128)(2,1)S(1)}, u32[]{:S(2)}, u32[]{:S(2)}) collective-permute-start(bf16[4,64,256]{2,1,0:T(8,128)(2,1)S(1)} %pad_maximum_fusion.refs_0_), channel_id=1, source_target_pairs={{0,4},{1,17},{2,6},{3,19},{4,0},{5,21},{6,2},{7,23},{8,12},{9,25},... | collective-permute-start | bytes 393224 | tf_op jit(solution)/shard_map/ppermute | solution.py:65
  12.2 0.7 %collective-permute-start.4 = (bf16[4,64,256]{2,1,0:T(8,128)(2,1)S(1)}, bf16[4,64,256]{2,1,0:T(8,128)(2,1)S(1)}, u32[]{:S(2)}, u32[]{:S(2)}) collective-permute-start(bf16[4,64,256]{2,1,0:T(8,128)(2,1)S(1)} %pad_maximum_fusion.refs_0_), channel_id=1, source_target_pairs={{0,2},{1,9},{2,4},{3,11},{4,6},{5,13},{6,0},{7,15},{8,10},{9,17},{... | collective-permute-start | bytes 393224 | tf_op jit(solution)/shard_map/ppermute | solution.py:65
  12.8 2.6 %collective-permute-start.3 = (bf16[4,64,256]{2,1,0:T(8,128)(2,1)S(1)}, bf16[4,64,256]{2,1,0:T(8,128)(2,1)S(1)}, u32[]{:S(2)}, u32[]{:S(2)}) collective-permute-start(bf16[4,64,256]{2,1,0:T(8,128)(2,1)S(1)} %pad_maximum_fusion.refs_0_), channel_id=1, source_target_pairs={{0,6},{1,25},{2,0},{3,27},{4,2},{5,29},{6,4},{7,31},{8,14},{9,1},{... | collective-permute-start | bytes 393224 | tf_op jit(solution)/shard_map/ppermute | solution.py:65
  15.4 0.0 collective-permute-start.6
  15.4 0.0 collective-permute-done.5.refs_3_
  15.4 0.5 collective-permute-start.9
  15.9 2.4 %collective-permute-done.4.refs_2_ = bf16[4,64,256]{2,1,0:T(8,128)(2,1)S(1)} collective-permute-done((bf16[4,64,256]{2,1,0:T(8,128)(2,1)S(1)}, bf16[4,64,256]{2,1,0:T(8,128)(2,1)S(1)}, u32[]{:S(2)}, u32[]{:S(2)}) %collective-permute-start.4) | collective-permute-done | bytes 131104 | tf_op jit(solution)/shard_map/ppermute | solution.py:65
  18.4 0.0 collective-permute-start.8
  18.4 0.0 collective-permute-done.3.refs_1_
  18.4 0.5 collective-permute-start.7
  19.5 0.0 collective-permute-done.6.refs_4_
  19.5 0.0 collective-permute-done.9.refs_7_
  19.5 0.2 collective-permute-done.8.refs_6_
  19.7 0.2 collective-permute-done.7.refs_5_
  19.9 0.0 copy-done
  19.9 0.0 slice-start
  19.9 2.3 %shard_map.56 = (bf16[16,16,384]{2,1,0:T(8,128)(2,1)S(1)}, bf16[16,16,384]{2,1,0:T(8,128)(2,1)S(1)}, bf16[16,16,384]{2,1,0:T(8,128)(2,1)S(1)}, bf16[16,16,384]{2,1,0:T(8,128)(2,1)S(1)}, bf16[64,384]{1,0:T(8,128)(2,1)S(1)}) custom-call(s32[1,3]{1,0:T(1,128)S(1)} %copy-done, s32[1,1]{1,0:T(1,128)S(6)} %copy.11.count_ref, ...), custom_call_target="tpu_custom_call" | custom-call | flops 1207959552 | bytes 4718592 | tf_op jit(solution)/shard_map/pallas_call | solution.py:174
  22.2 2.0 %collective-permute-start.10 = (bf16[16,16,384]{2,1,0:T(8,128)(2,1)S(1)}, bf16[16,16,384]{2,1,0:T(8,128)(2,1)S(1)}, u32[]{:S(2)}, u32[]{:S(2)}) collective-permute-start(bf16[16,16,384]{2,1,0:T(8,128)(2,1)S(1)} %get-tuple-element.29), channel_id=1, source_target_pairs={{0,32},{1,97},{2,34},{3,99},{4,36},{5,101},{6,38},{7,103},{8,40},{... | collective-permute-start | bytes 589832 | tf_op jit(solution)/shard_map/ppermute | solution.py:293
  24.2 2.2 %collective-permute-start.11 = (bf16[16,16,384]{2,1,0:T(8,128)(2,1)S(1)}, bf16[16,16,384]{2,1,0:T(8,128)(2,1)S(1)}, u32[]{:S(2)}, u32[]{:S(2)}) collective-permute-start(bf16[16,16,384]{2,1,0:T(8,128)(2,1)S(1)} %get-tuple-element.30), channel_id=1, source_target_pairs={{0,96},{1,33},{2,98},{3,35},{4,100},{5,37},{6,102},{7,39},{8,104},... | collective-permute-start | bytes 589832 | tf_op jit(solution)/shard_map/ppermute | solution.py:293
  26.4 1.8 %collective-permute-start.12 = (bf16[16,16,384]{2,1,0:T(8,128)(2,1)S(1)}, bf16[16,16,384]{2,1,0:T(8,128)(2,1)S(1)}, u32[]{:S(2)}, u32[]{:S(2)}) collective-permute-start(bf16[16,16,384]{2,1,0:T(8,128)(2,1)S(1)} %get-tuple-element.31), channel_id=1, source_target_pairs={{0,64},{1,65},{2,66},{3,67},{4,68},{5,69},{6,70},{7,71},{8,72},{9,... | collective-permute-start | bytes 589832 | tf_op jit(solution)/shard_map/ppermute | solution.py:293
  28.2 0.0 slice-start.1
  28.2 4.5 %shard_map.59 = (bf16[16,32,384]{2,1,0:T(8,128)(2,1)S(1)}, bf16[16,32,384]{2,1,0:T(8,128)(2,1)S(1)}, bf16[16,32,384]{2,1,0:T(8,128)(2,1)S(1)}, bf16[16,32,384]{2,1,0:T(8,128)(2,1)S(1)}) custom-call(bf16[64,384]{1,0:T(8,128)(2,1)S(1)} %get-tuple-element.32.cc_ref, bf16[3,64,384,128]{3,2,1,0:T(8,128)(2,1)} %integrals_ref.5, ...), custom_call_target="tpu_custom_call" | custom-call | flops 2415919104 | bytes 9437184 | tf_op jit(solution)/shard_map/pallas_call | solution.py:190
  32.7 1.8 %collective-permute-start.16 = (bf16[16,32,384]{2,1,0:T(8,128)(2,1)S(1)}, bf16[16,32,384]{2,1,0:T(8,128)(2,1)S(1)}, u32[]{:S(2)}, u32[]{:S(2)}) collective-permute-start(bf16[16,32,384]{2,1,0:T(8,128)(2,1)S(1)} %get-tuple-element.38), channel_id=1, source_target_pairs={{0,64},{1,65},{2,66},{3,67},{4,68},{5,69},{6,70},{7,71},{8,72},{9,... | collective-permute-start | bytes 1179656 | tf_op jit(solution)/shard_map/ppermute | solution.py:293
  34.5 0.0 collective-permute-start.17
  34.6 0.0 collective-permute-done.10.refs_1_
  34.6 3.2 %collective-permute-start.18 = (bf16[16,32,384]{2,1,0:T(8,128)(2,1)S(1)}, bf16[16,32,384]{2,1,0:T(8,128)(2,1)S(1)}, u32[]{:S(2)}, u32[]{:S(2)}) collective-permute-start(bf16[16,32,384]{2,1,0:T(8,128)(2,1)S(1)} %get-tuple-element.40), channel_id=1, source_target_pairs={{0,96},{1,33},{2,98},{3,35},{4,100},{5,37},{6,102},{7,39},{8,104},... | collective-permute-start | bytes 1179656 | tf_op jit(solution)/shard_map/ppermute | solution.py:293
  37.8 6.4 %collective-permute-done.11.refs_3_ = bf16[16,16,384]{2,1,0:T(8,128)(2,1)S(1)} collective-permute-done((bf16[16,16,384]{2,1,0:T(8,128)(2,1)S(1)}, bf16[16,16,384]{2,1,0:T(8,128)(2,1)S(1)}, u32[]{:S(2)}, u32[]{:S(2)}) %collective-permute-start.11) | collective-permute-done | bytes 196640 | tf_op jit(solution)/shard_map/ppermute | solution.py:293
  44.1 0.0 collective-permute-done.12.refs_2_
  44.2 3.4 %shard_map.57 = (bf16[16,16,384]{2,1,0:T(8,128)(2,1)S(1)}, bf16[16,16,384]{2,1,0:T(8,128)(2,1)S(1)}, bf16[16,16,384]{2,1,0:T(8,128)(2,1)S(1)}, bf16[16,16,384]{2,1,0:T(8,128)(2,1)S(1)}) custom-call(bf16[64,384]{1,0:T(8,128)(2,1)S(1)} %get-tuple-element.32.cc_ref, bf16[3,64,384,128]{3,2,1,0:T(8,128)(2,1)} %integrals_ref.5), custom_call_target="tpu_custom_call" | custom-call | flops 1207959552 | bytes 4718592 | tf_op jit(solution)/shard_map/pallas_call | solution.py:190
  47.5 0.1 collective-permute-start.13
  47.6 5.3 %collective-permute-start.14 = (bf16[16,16,384]{2,1,0:T(8,128)(2,1)S(1)}, bf16[16,16,384]{2,1,0:T(8,128)(2,1)S(1)}, u32[]{:S(2)}, u32[]{:S(2)}) collective-permute-start(bf16[16,16,384]{2,1,0:T(8,128)(2,1)S(1)} %get-tuple-element.35), channel_id=1, source_target_pairs={{0,64},{1,65},{2,66},{3,67},{4,68},{5,69},{6,70},{7,71},{8,72},{9,... | collective-permute-start | bytes 589832 | tf_op jit(solution)/shard_map/ppermute | solution.py:293
  52.9 0.0 slice-done
  52.9 0.0 slice-done.1
  52.9 0.5 shard_map.58.refs_4_
  53.4 2.3 %shard_map.60.refs_5_ = bf16[16,64,1536]{2,1,0:T(8,128)(2,1)} custom-call(bf16[16,16,384]{2,1,0:T(8,128)(2,1)S(1)} %get-tuple-element.41.refs_0_, bf16[16,16,384]{2,1,0:T(8,128)(2,1)S(1)} %collective-permute-done.10.refs_1_, bf16[16,16,384]{2,1,0:T(8,128)(2,1)S(1)} %collective-permute-done.12.refs_2_, ...), custom_call_target="tpu_custom_call" | custom-call | flops 1207959552 | bytes 1572864 | tf_op jit(solution)/shard_map/pallas_call | solution.py:266
  55.8 0.0 collective-permute-done.16.refs_1_
  55.8 0.3 collective-permute-start.15
  56.0 0.0 collective-permute-done.17.refs_2_
  56.0 0.0 collective-permute-done.18.refs_3_
  56.0 3.9 %shard_map.61.refs_5_ = bf16[16,64,1536]{2,1,0:T(8,128)(2,1)} custom-call(bf16[16,32,384]{2,1,0:T(8,128)(2,1)S(1)} %get-tuple-element.37.refs_0_, bf16[16,32,384]{2,1,0:T(8,128)(2,1)S(1)} %collective-permute-done.16.refs_1_, bf16[16,32,384]{2,1,0:T(8,128)(2,1)S(1)} %collective-permute-done.17.refs_2_, ...), custom_call_target="tpu_custom_call", output_to_operand_aliasing={{}: (5, {})} | custom-call | flops 2415919104 | bytes 3145728 | tf_op jit(solution)/shard_map/pallas_call | solution.py:266
  59.9 0.0 collective-permute-done.13.refs_1_
  59.9 2.6 %collective-permute-done.14.refs_2_ = bf16[16,16,384]{2,1,0:T(8,128)(2,1)S(1)} collective-permute-done((bf16[16,16,384]{2,1,0:T(8,128)(2,1)S(1)}, bf16[16,16,384]{2,1,0:T(8,128)(2,1)S(1)}, u32[]{:S(2)}, u32[]{:S(2)}) %collective-permute-start.14) | collective-permute-done | bytes 196640 | tf_op jit(solution)/shard_map/ppermute | solution.py:293
  62.6 0.0 collective-permute-done.15.refs_3_
  62.6 2.3 %shard_map.62 = bf16[16,64,1536]{2,1,0:T(8,128)(2,1)} custom-call(bf16[16,16,384]{2,1,0:T(8,128)(2,1)S(1)} %get-tuple-element.33.after_ref.refs_0_, bf16[16,16,384]{2,1,0:T(8,128)(2,1)S(1)} %collective-permute-done.13.refs_1_, bf16[16,16,384]{2,1,0:T(8,128)(2,1)S(1)} %collective-permute-done.14.refs_2_, ...), custom_call_target="tpu_custom_call", output_to_operand_aliasing={{}: (5, {})} | custom-call | flops 1207959552 | bytes 1572864 | tf_op jit(solution)/shard_map/pallas_call | solution.py:266
  (2 shorter events, 0.0 us)
Async XLA Ops:
  0.0 8.9 %copy-start.1 = (bf16[256,64]{0,1:T(8,128)(2,1)S(1)}, bf16[256,64]{0,1:T(8,128)(2,1)}, u32[]{:S(2)}) copy-start(bf16[256,64]{0,1:T(8,128)(2,1)} %param.6) | copy-start | bytes 98308
  0.0 19.9 %copy-start = (s32[1,3]{1,0:T(1,128)S(1)}, s32[1,3]{1,0:T(1,128)}, u32[]{:S(2)}) copy-start(s32[1,3]{1,0:T(1,128)} %nu_ref.1) | copy-start | bytes 40
  0.0 6.5 %collective-permute-start.2 = (bf16[1,64,256]{2,1,0:T(8,128)(2,1)}, bf16[1,64,256]{2,1,0:T(8,128)(2,1)S(1)}, u32[]{:S(2)}, u32[]{:S(2)}) collective-permute-start(bf16[1,64,256]{2,1,0:T(8,128)(2,1)} %bitcast.8), channel_id=1, source_target_pairs={{0,24},{1,7},{2,26},{3,1},{4,28},{5,3},{6,30},{7,5},{8,0},{9,15},{... | collective-permute-start | bytes 98312 | tf_op jit(solution)/shard_map/ppermute | solution.py:62
  0.8 5.7 %collective-permute-start.1 = (bf16[1,64,256]{2,1,0:T(8,128)(2,1)}, bf16[1,64,256]{2,1,0:T(8,128)(2,1)S(1)}, u32[]{:S(2)}, u32[]{:S(2)}) collective-permute-start(bf16[1,64,256]{2,1,0:T(8,128)(2,1)} %bitcast.9), channel_id=1, source_target_pairs={{0,8},{1,3},{2,10},{3,5},{4,12},{5,7},{6,14},{7,1},{8,16},{9,11},{... | collective-permute-start | bytes 98312 | tf_op jit(solution)/shard_map/ppermute | solution.py:62
  3.2 5.6 %collective-permute-start = (bf16[1,64,256]{2,1,0:T(8,128)(2,1)}, bf16[1,64,256]{2,1,0:T(8,128)(2,1)S(1)}, u32[]{:S(2)}, u32[]{:S(2)}) collective-permute-start(bf16[1,64,256]{2,1,0:T(8,128)(2,1)} %bitcast.10), channel_id=1, source_target_pairs={{0,16},{1,5},{2,18},{3,7},{4,20},{5,1},{6,22},{7,3},{8,24},{9,13},... | collective-permute-start | bytes 98312 | tf_op jit(solution)/shard_map/ppermute | solution.py:62
  8.9 6.6 %collective-permute-start.5 = (bf16[4,64,256]{2,1,0:T(8,128)(2,1)S(1)}, bf16[4,64,256]{2,1,0:T(8,128)(2,1)S(1)}, u32[]{:S(2)}, u32[]{:S(2)}) collective-permute-start(bf16[4,64,256]{2,1,0:T(8,128)(2,1)S(1)} %pad_maximum_fusion.refs_0_), channel_id=1, source_target_pairs={{0,4},{1,17},{2,6},{3,19},{4,0},{5,21},{6,2},{7,23},{8,12},{9,25},... | collective-permute-start | bytes 393224 | tf_op jit(solution)/shard_map/ppermute | solution.py:65
  12.2 6.2 %collective-permute-start.4 = (bf16[4,64,256]{2,1,0:T(8,128)(2,1)S(1)}, bf16[4,64,256]{2,1,0:T(8,128)(2,1)S(1)}, u32[]{:S(2)}, u32[]{:S(2)}) collective-permute-start(bf16[4,64,256]{2,1,0:T(8,128)(2,1)S(1)} %pad_maximum_fusion.refs_0_), channel_id=1, source_target_pairs={{0,2},{1,9},{2,4},{3,11},{4,6},{5,13},{6,0},{7,15},{8,10},{9,17},{... | collective-permute-start | bytes 393224 | tf_op jit(solution)/shard_map/ppermute | solution.py:65
  12.8 5.5 %collective-permute-start.3 = (bf16[4,64,256]{2,1,0:T(8,128)(2,1)S(1)}, bf16[4,64,256]{2,1,0:T(8,128)(2,1)S(1)}, u32[]{:S(2)}, u32[]{:S(2)}) collective-permute-start(bf16[4,64,256]{2,1,0:T(8,128)(2,1)S(1)} %pad_maximum_fusion.refs_0_), channel_id=1, source_target_pairs={{0,6},{1,25},{2,0},{3,27},{4,2},{5,29},{6,4},{7,31},{8,14},{9,1},{... | collective-permute-start | bytes 393224 | tf_op jit(solution)/shard_map/ppermute | solution.py:65
  15.4 4.1 %collective-permute-start.6 = (bf16[4,64,256]{2,1,0:T(8,128)(2,1)S(1)}, bf16[4,64,256]{2,1,0:T(8,128)(2,1)S(1)}, u32[]{:S(2)}, u32[]{:S(2)}) collective-permute-start(bf16[4,64,256]{2,1,0:T(8,128)(2,1)S(1)} %pad_maximum_fusion.refs_0_), channel_id=1, source_target_pairs={{0,1},{1,0},{2,3},{3,2},{4,5},{5,4},{6,7},{7,6},{8,9},{9,8},{10,11... | collective-permute-start | bytes 393224 | tf_op jit(solution)/shard_map/ppermute | solution.py:67
  15.4 4.1 %collective-permute-start.9 = (bf16[4,64,256]{2,1,0:T(8,128)(2,1)S(1)}, bf16[4,64,256]{2,1,0:T(8,128)(2,1)S(1)}, u32[]{:S(2)}, u32[]{:S(2)}) collective-permute-start(bf16[4,64,256]{2,1,0:T(8,128)(2,1)S(1)} %collective-permute-done.5.refs_3_), channel_id=1, source_target_pairs={{0,1},{1,0},{2,3},{3,2},{4,5},{5,4},{6,7},{7,6},{8,9},{9,8},{10,11... | collective-permute-start | bytes 393224 | tf_op jit(solution)/shard_map/ppermute | solution.py:67
  18.4 1.3 %collective-permute-start.8 = (bf16[4,64,256]{2,1,0:T(8,128)(2,1)S(1)}, bf16[4,64,256]{2,1,0:T(8,128)(2,1)S(1)}, u32[]{:S(2)}, u32[]{:S(2)}) collective-permute-start(bf16[4,64,256]{2,1,0:T(8,128)(2,1)S(1)} %collective-permute-done.4.refs_2_), channel_id=1, source_target_pairs={{0,1},{1,0},{2,3},{3,2},{4,5},{5,4},{6,7},{7,6},{8,9},{9,8},{10,11... | collective-permute-start | bytes 393224 | tf_op jit(solution)/shard_map/ppermute | solution.py:67
  18.4 1.5 %collective-permute-start.7 = (bf16[4,64,256]{2,1,0:T(8,128)(2,1)S(1)}, bf16[4,64,256]{2,1,0:T(8,128)(2,1)S(1)}, u32[]{:S(2)}, u32[]{:S(2)}) collective-permute-start(bf16[4,64,256]{2,1,0:T(8,128)(2,1)S(1)} %collective-permute-done.3.refs_1_), channel_id=1, source_target_pairs={{0,1},{1,0},{2,3},{3,2},{4,5},{5,4},{6,7},{7,6},{8,9},{9,8},{10,11... | collective-permute-start | bytes 393224 | tf_op jit(solution)/shard_map/ppermute | solution.py:67
  19.9 33.0 %slice-start = ((s8[4718592]{0:T(1024)(128)(4,1)}), s8[4194304]{0:T(1024)(128)(4,1)S(1)}, s32[]{:S(2)}) async-start(s8[4718592]{0:T(1024)(128)(4,1)} %bitcast.6), calls=%async_computation | async-start | bytes 8388608
  22.2 12.3 %collective-permute-start.10 = (bf16[16,16,384]{2,1,0:T(8,128)(2,1)S(1)}, bf16[16,16,384]{2,1,0:T(8,128)(2,1)S(1)}, u32[]{:S(2)}, u32[]{:S(2)}) collective-permute-start(bf16[16,16,384]{2,1,0:T(8,128)(2,1)S(1)} %get-tuple-element.29), channel_id=1, source_target_pairs={{0,32},{1,97},{2,34},{3,99},{4,36},{5,101},{6,38},{7,103},{8,40},{... | collective-permute-start | bytes 589832 | tf_op jit(solution)/shard_map/ppermute | solution.py:293
  24.2 19.9 %collective-permute-start.11 = (bf16[16,16,384]{2,1,0:T(8,128)(2,1)S(1)}, bf16[16,16,384]{2,1,0:T(8,128)(2,1)S(1)}, u32[]{:S(2)}, u32[]{:S(2)}) collective-permute-start(bf16[16,16,384]{2,1,0:T(8,128)(2,1)S(1)} %get-tuple-element.30), channel_id=1, source_target_pairs={{0,96},{1,33},{2,98},{3,35},{4,100},{5,37},{6,102},{7,39},{8,104},... | collective-permute-start | bytes 589832 | tf_op jit(solution)/shard_map/ppermute | solution.py:293
  26.4 17.7 %collective-permute-start.12 = (bf16[16,16,384]{2,1,0:T(8,128)(2,1)S(1)}, bf16[16,16,384]{2,1,0:T(8,128)(2,1)S(1)}, u32[]{:S(2)}, u32[]{:S(2)}) collective-permute-start(bf16[16,16,384]{2,1,0:T(8,128)(2,1)S(1)} %get-tuple-element.31), channel_id=1, source_target_pairs={{0,64},{1,65},{2,66},{3,67},{4,68},{5,69},{6,70},{7,71},{8,72},{9,... | collective-permute-start | bytes 589832 | tf_op jit(solution)/shard_map/ppermute | solution.py:293
  28.2 24.7 %slice-start.1 = ((s8[4718592]{0:T(1024)(128)(4,1)}), s8[524288]{0:T(1024)(128)(4,1)S(1)}, s32[]{:S(2)}) async-start(s8[4718592]{0:T(1024)(128)(4,1)} %bitcast.6), calls=%async_computation.1 | async-start | bytes 1048576
  32.7 23.0 %collective-permute-start.16 = (bf16[16,32,384]{2,1,0:T(8,128)(2,1)S(1)}, bf16[16,32,384]{2,1,0:T(8,128)(2,1)S(1)}, u32[]{:S(2)}, u32[]{:S(2)}) collective-permute-start(bf16[16,32,384]{2,1,0:T(8,128)(2,1)S(1)} %get-tuple-element.38), channel_id=1, source_target_pairs={{0,64},{1,65},{2,66},{3,67},{4,68},{5,69},{6,70},{7,71},{8,72},{9,... | collective-permute-start | bytes 1179656 | tf_op jit(solution)/shard_map/ppermute | solution.py:293
  34.5 21.5 %collective-permute-start.17 = (bf16[16,32,384]{2,1,0:T(8,128)(2,1)S(1)}, bf16[16,32,384]{2,1,0:T(8,128)(2,1)S(1)}, u32[]{:S(2)}, u32[]{:S(2)}) collective-permute-start(bf16[16,32,384]{2,1,0:T(8,128)(2,1)S(1)} %get-tuple-element.39), channel_id=1, source_target_pairs={{0,32},{1,97},{2,34},{3,99},{4,36},{5,101},{6,38},{7,103},{8,40},{... | collective-permute-start | bytes 1179656 | tf_op jit(solution)/shard_map/ppermute | solution.py:293
  34.6 21.5 %collective-permute-start.18 = (bf16[16,32,384]{2,1,0:T(8,128)(2,1)S(1)}, bf16[16,32,384]{2,1,0:T(8,128)(2,1)S(1)}, u32[]{:S(2)}, u32[]{:S(2)}) collective-permute-start(bf16[16,32,384]{2,1,0:T(8,128)(2,1)S(1)} %get-tuple-element.40), channel_id=1, source_target_pairs={{0,96},{1,33},{2,98},{3,35},{4,100},{5,37},{6,102},{7,39},{8,104},... | collective-permute-start | bytes 1179656 | tf_op jit(solution)/shard_map/ppermute | solution.py:293
  47.5 12.4 %collective-permute-start.13 = (bf16[16,16,384]{2,1,0:T(8,128)(2,1)S(1)}, bf16[16,16,384]{2,1,0:T(8,128)(2,1)S(1)}, u32[]{:S(2)}, u32[]{:S(2)}) collective-permute-start(bf16[16,16,384]{2,1,0:T(8,128)(2,1)S(1)} %get-tuple-element.34), channel_id=1, source_target_pairs={{0,32},{1,97},{2,34},{3,99},{4,36},{5,101},{6,38},{7,103},{8,40},{... | collective-permute-start | bytes 589832 | tf_op jit(solution)/shard_map/ppermute | solution.py:293
  47.6 15.0 %collective-permute-start.14 = (bf16[16,16,384]{2,1,0:T(8,128)(2,1)S(1)}, bf16[16,16,384]{2,1,0:T(8,128)(2,1)S(1)}, u32[]{:S(2)}, u32[]{:S(2)}) collective-permute-start(bf16[16,16,384]{2,1,0:T(8,128)(2,1)S(1)} %get-tuple-element.35), channel_id=1, source_target_pairs={{0,64},{1,65},{2,66},{3,67},{4,68},{5,69},{6,70},{7,71},{8,72},{9,... | collective-permute-start | bytes 589832 | tf_op jit(solution)/shard_map/ppermute | solution.py:293
  55.8 6.8 %collective-permute-start.15 = (bf16[16,16,384]{2,1,0:T(8,128)(2,1)S(1)}, bf16[16,16,384]{2,1,0:T(8,128)(2,1)S(1)}, u32[]{:S(2)}, u32[]{:S(2)}) collective-permute-start(bf16[16,16,384]{2,1,0:T(8,128)(2,1)S(1)} %get-tuple-element.36), channel_id=1, source_target_pairs={{0,96},{1,33},{2,98},{3,35},{4,100},{5,37},{6,102},{7,39},{8,104},... | collective-permute-start | bytes 589832 | tf_op jit(solution)/shard_map/ppermute | solution.py:293

commit v5 on v3

--- a/solution.py
+++ b/solution.py
@@ -16,6 +16,7 @@
 GROUP = 16
 BLOCK = 4
 CHUNKS = ((0, 16), (16, 32), (48, 16))
+EDGES = {16: (0, 1024, 1536), 32: (0, 512, 1024, 1536)}
 SENDS = ((0, 1, 3, 2), (0, 3, 1, 2), (0, 1, 3, 2))
 STAGED = 24
 HOPS = (0, 1, 3, 2)
@@ -234,16 +235,15 @@
     root_ref, (out_ref, stage, sems) = refs[4], refs[-3:]
     a_refs = [refs[order.index(k)] for k in range(SIDE)]
     rows = 16 * count
-    step = stage.shape[3]
     arrived = jnp.concatenate([a[...].reshape(rows, a.shape[2]) for a in a_refs], axis=1)
     copies = []
-    for q in range(stage.shape[0]):
-        prod = lax.dot_general(
-            arrived, root_ref[q * step:(q + 1) * step, :], NT, preferred_element_type=jnp.float32
-        )
-        stage[q] = prod.astype(jnp.bfloat16).reshape(16, count, step)
+    for q, (begin, end) in enumerate(zip(EDGES[count], EDGES[count][1:])):
+        prod = lax.dot_general(arrived, root_ref[begin:end, :], NT, preferred_element_type=jnp.float32)
+        stage[:, :, begin:end] = prod.astype(jnp.bfloat16).reshape(16, count, end - begin)
         copy = pltpu.make_async_copy(
-            stage.at[q], out_ref.at[:, pl.ds(first, count), pl.ds(q * step, step)], sems.at[q]
+            stage.at[:, :, pl.ds(begin, end - begin)],
+            out_ref.at[:, pl.ds(first, count), pl.ds(begin, end - begin)],
+            sems.at[q],
         )
         copy.start()
         copies.append(copy)
@@ -253,7 +253,6 @@
 
 def fit_call(first, count, order, arrived, root, out):
     total = root.shape[0]
-    step = total if count == GROUP else 512
     operands = [arrived[k] for k in order] + [root]
     specs = [VMEM] * 5
     aliases = {}
@@ -267,8 +266,8 @@
         out_specs=HBM,
         out_shape=jax.ShapeDtypeStruct((16, 64, total), jnp.bfloat16),
         scratch_shapes=[
-            pltpu.VMEM((total // step, 16, count, step), jnp.bfloat16),
-            pltpu.SemaphoreType.DMA((total // step,)),
+            pltpu.VMEM((16, count, total), jnp.bfloat16),
+            pltpu.SemaphoreType.DMA((len(EDGES[count]) - 1,)),
         ],
         input_output_aliases=aliases,
         compiler_params=pltpu.CompilerParams(vmem_limit_bytes=24 * 2**20),

time: 65.3 us -> 65.3 us (level)
  no operation moved by 1% of the time
where the time goes in v5:
time: 65.3 us; the launch traced here: 65.2 us
  starting transfers between devices  27.4 us (42%)
  Pallas kernels  23 us (35%)
  waiting for transfers between devices  13.8 us (21%)
  between operations  0.96 us (1%)
    ppermute x9, starting transfers between devices, shards(): lax.ppermute(parts[d], ('aux', 'pair'), aux_perm(d))  16.5 us
    ppermute x9, waiting for transfers between devices, shards(): lax.ppermute(parts[d], ('aux', 'pair'), aux_perm(d))  8.66 us
    pallas_call x3, Pallas kernels, fit_call(): pl.pallas_call(functools.partial(fit_kernel, first, count, order), in_spe...  8.51 us
    pallas_call x2, Pallas kernels, half_call(): pl.pallas_call(functools.partial(half_next, first, count, held), in_specs...  8.39 us
    ppermute x3, starting transfers between devices, gather_coeff(): lax.ppermute(line, 'pair', line_perm(1, step))  6.51 us
    ppermute x3, starting transfers between devices, gather_coeff(): lax.ppermute(own, 'pair', line_perm(0, step))  3.43 us
    pallas_call x1, Pallas kernels, stage_call(): pl.pallas_call(stage_kernel, in_specs=[HBM], out_specs=VMEM, out_shape=ja...  3.09 us
    pallas_call x1, Pallas kernels, half_call(): pl.pallas_call(functools.partial(half_first, count), in_specs=[SMEM] + [V...  2.48 us
  transfers between devices with their start and end apart: 19, of which 7 were waited for; matrix products, arithmetic and copies ran while one was open for 0% of the time, Pallas kernels for 28%

profile of v5, /device:TPU:6, one launch (start us, length us, event | category | flops | bytes accessed | tf_op | source)
XLA Modules:
  0.0 65.2 jit_solution(17529640699885142673)
XLA Ops:
  0.0 0.0 copy-start.1
  0.0 0.0 copy-start
  0.0 0.8 %collective-permute-start.2 = (bf16[1,64,256]{2,1,0:T(8,128)(2,1)}, bf16[1,64,256]{2,1,0:T(8,128)(2,1)S(1)}, u32[]{:S(2)}, u32[]{:S(2)}) collective-permute-start(bf16[1,64,256]{2,1,0:T(8,128)(2,1)} %bitcast.8), channel_id=1, source_target_pairs={{0,24},{1,7},{2,26},{3,1},{4,28},{5,3},{6,30},{7,5},{8,0},{9,15},{... | collective-permute-start | bytes 98312 | tf_op jit(solution)/shard_map/ppermute | solution.py:62
  0.8 2.4 %collective-permute-start.1 = (bf16[1,64,256]{2,1,0:T(8,128)(2,1)}, bf16[1,64,256]{2,1,0:T(8,128)(2,1)S(1)}, u32[]{:S(2)}, u32[]{:S(2)}) collective-permute-start(bf16[1,64,256]{2,1,0:T(8,128)(2,1)} %bitcast.9), channel_id=1, source_target_pairs={{0,8},{1,3},{2,10},{3,5},{4,12},{5,7},{6,14},{7,1},{8,16},{9,11},{... | collective-permute-start | bytes 98312 | tf_op jit(solution)/shard_map/ppermute | solution.py:62
  3.2 0.2 collective-permute-start
  3.4 3.1 %shard_map.55.refs_8_.refs_0_ = bf16[6,3,4,384,128]{4,3,2,1,0:T(8,128)(2,1)S(1)} custom-call(bf16[3,64,384,128]{3,2,1,0:T(8,128)(2,1)} %integrals_ref.5), custom_call_target="tpu_custom_call" | custom-call | bytes 14155776 | tf_op jit(solution)/shard_map/pallas_call | solution.py:107
  6.5 0.0 collective-permute-done.2
  6.5 0.0 collective-permute-done.1
  6.6 2.3 %collective-permute-done = bf16[1,64,256]{2,1,0:T(8,128)(2,1)S(1)} collective-permute-done((bf16[1,64,256]{2,1,0:T(8,128)(2,1)}, bf16[1,64,256]{2,1,0:T(8,128)(2,1)S(1)}, u32[]{:S(2)}, u32[]{:S(2)}) %collective-permute-start) | collective-permute-done | bytes 32800 | tf_op jit(solution)/shard_map/ppermute | solution.py:62
  8.9 0.0 copy-done.1
  8.9 3.3 %collective-permute-start.5 = (bf16[4,64,256]{2,1,0:T(8,128)(2,1)S(1)}, bf16[4,64,256]{2,1,0:T(8,128)(2,1)S(1)}, u32[]{:S(2)}, u32[]{:S(2)}) collective-permute-start(bf16[4,64,256]{2,1,0:T(8,128)(2,1)S(1)} %pad_maximum_fusion.refs_0_), channel_id=1, source_target_pairs={{0,4},{1,17},{2,6},{3,19},{4,0},{5,21},{6,2},{7,23},{8,12},{9,25},... | collective-permute-start | bytes 393224 | tf_op jit(solution)/shard_map/ppermute | solution.py:65
  12.2 0.7 %collective-permute-start.4 = (bf16[4,64,256]{2,1,0:T(8,128)(2,1)S(1)}, bf16[4,64,256]{2,1,0:T(8,128)(2,1)S(1)}, u32[]{:S(2)}, u32[]{:S(2)}) collective-permute-start(bf16[4,64,256]{2,1,0:T(8,128)(2,1)S(1)} %pad_maximum_fusion.refs_0_), channel_id=1, source_target_pairs={{0,2},{1,9},{2,4},{3,11},{4,6},{5,13},{6,0},{7,15},{8,10},{9,17},{... | collective-permute-start | bytes 393224 | tf_op jit(solution)/shard_map/ppermute | solution.py:65
  12.8 2.6 %collective-permute-start.3 = (bf16[4,64,256]{2,1,0:T(8,128)(2,1)S(1)}, bf16[4,64,256]{2,1,0:T(8,128)(2,1)S(1)}, u32[]{:S(2)}, u32[]{:S(2)}) collective-permute-start(bf16[4,64,256]{2,1,0:T(8,128)(2,1)S(1)} %pad_maximum_fusion.refs_0_), channel_id=1, source_target_pairs={{0,6},{1,25},{2,0},{3,27},{4,2},{5,29},{6,4},{7,31},{8,14},{9,1},{... | collective-permute-start | bytes 393224 | tf_op jit(solution)/shard_map/ppermute | solution.py:65
  15.4 0.0 collective-permute-start.6
  15.4 0.0 collective-permute-done.5.refs_3_
  15.4 0.5 collective-permute-start.9
  15.9 2.4 %collective-permute-done.4.refs_2_ = bf16[4,64,256]{2,1,0:T(8,128)(2,1)S(1)} collective-permute-done((bf16[4,64,256]{2,1,0:T(8,128)(2,1)S(1)}, bf16[4,64,256]{2,1,0:T(8,128)(2,1)S(1)}, u32[]{:S(2)}, u32[]{:S(2)}) %collective-permute-start.4) | collective-permute-done | bytes 131104 | tf_op jit(solution)/shard_map/ppermute | solution.py:65
  18.4 0.0 collective-permute-start.8
  18.4 0.0 collective-permute-done.3.refs_1_
  18.4 0.5 collective-permute-start.7
  19.5 0.0 collective-permute-done.6.refs_4_
  19.5 0.0 collective-permute-done.9.refs_7_
  19.5 0.2 collective-permute-done.8.refs_6_
  19.7 0.2 collective-permute-done.7.refs_5_
  19.9 0.0 copy-done
  19.9 0.0 slice-start
  19.9 2.5 %shard_map.56 = (bf16[16,16,384]{2,1,0:T(8,128)(2,1)S(1)}, bf16[16,16,384]{2,1,0:T(8,128)(2,1)S(1)}, bf16[16,16,384]{2,1,0:T(8,128)(2,1)S(1)}, bf16[16,16,384]{2,1,0:T(8,128)(2,1)S(1)}, bf16[64,384]{1,0:T(8,128)(2,1)S(1)}) custom-call(s32[1,3]{1,0:T(1,128)S(1)} %copy-done, s32[1,1]{1,0:T(1,128)S(6)} %copy.11.count_ref, ...), custom_call_target="tpu_custom_call" | custom-call | flops 1207959552 | bytes 4718592 | tf_op jit(solution)/shard_map/pallas_call | solution.py:173
  22.4 2.0 %collective-permute-start.10 = (bf16[16,16,384]{2,1,0:T(8,128)(2,1)S(1)}, bf16[16,16,384]{2,1,0:T(8,128)(2,1)S(1)}, u32[]{:S(2)}, u32[]{:S(2)}) collective-permute-start(bf16[16,16,384]{2,1,0:T(8,128)(2,1)S(1)} %get-tuple-element.29), channel_id=1, source_target_pairs={{0,32},{1,97},{2,34},{3,99},{4,36},{5,101},{6,38},{7,103},{8,40},{... | collective-permute-start | bytes 589832 | tf_op jit(solution)/shard_map/ppermute | solution.py:290
  24.4 2.2 %collective-permute-start.11 = (bf16[16,16,384]{2,1,0:T(8,128)(2,1)S(1)}, bf16[16,16,384]{2,1,0:T(8,128)(2,1)S(1)}, u32[]{:S(2)}, u32[]{:S(2)}) collective-permute-start(bf16[16,16,384]{2,1,0:T(8,128)(2,1)S(1)} %get-tuple-element.30), channel_id=1, source_target_pairs={{0,96},{1,33},{2,98},{3,35},{4,100},{5,37},{6,102},{7,39},{8,104},... | collective-permute-start | bytes 589832 | tf_op jit(solution)/shard_map/ppermute | solution.py:290
  26.6 1.8 %collective-permute-start.12 = (bf16[16,16,384]{2,1,0:T(8,128)(2,1)S(1)}, bf16[16,16,384]{2,1,0:T(8,128)(2,1)S(1)}, u32[]{:S(2)}, u32[]{:S(2)}) collective-permute-start(bf16[16,16,384]{2,1,0:T(8,128)(2,1)S(1)} %get-tuple-element.31), channel_id=1, source_target_pairs={{0,64},{1,65},{2,66},{3,67},{4,68},{5,69},{6,70},{7,71},{8,72},{9,... | collective-permute-start | bytes 589832 | tf_op jit(solution)/shard_map/ppermute | solution.py:290
  28.4 0.0 slice-start.1
  28.4 4.8 %shard_map.59 = (bf16[16,32,384]{2,1,0:T(8,128)(2,1)S(1)}, bf16[16,32,384]{2,1,0:T(8,128)(2,1)S(1)}, bf16[16,32,384]{2,1,0:T(8,128)(2,1)S(1)}, bf16[16,32,384]{2,1,0:T(8,128)(2,1)S(1)}) custom-call(bf16[64,384]{1,0:T(8,128)(2,1)S(1)} %get-tuple-element.32.cc_ref, bf16[3,64,384,128]{3,2,1,0:T(8,128)(2,1)} %integrals_ref.5, ...), custom_call_target="tpu_custom_call" | custom-call | flops 2415919104 | bytes 9437184 | tf_op jit(solution)/shard_map/pallas_call | solution.py:189
  33.2 1.8 %collective-permute-start.16 = (bf16[16,32,384]{2,1,0:T(8,128)(2,1)S(1)}, bf16[16,32,384]{2,1,0:T(8,128)(2,1)S(1)}, u32[]{:S(2)}, u32[]{:S(2)}) collective-permute-start(bf16[16,32,384]{2,1,0:T(8,128)(2,1)S(1)} %get-tuple-element.38), channel_id=1, source_target_pairs={{0,64},{1,65},{2,66},{3,67},{4,68},{5,69},{6,70},{7,71},{8,72},{9,... | collective-permute-start | bytes 1179656 | tf_op jit(solution)/shard_map/ppermute | solution.py:290
  35.0 0.0 collective-permute-start.17
  35.0 0.0 collective-permute-done.10.refs_1_
  35.0 3.2 %collective-permute-start.18 = (bf16[16,32,384]{2,1,0:T(8,128)(2,1)S(1)}, bf16[16,32,384]{2,1,0:T(8,128)(2,1)S(1)}, u32[]{:S(2)}, u32[]{:S(2)}) collective-permute-start(bf16[16,32,384]{2,1,0:T(8,128)(2,1)S(1)} %get-tuple-element.40), channel_id=1, source_target_pairs={{0,96},{1,33},{2,98},{3,35},{4,100},{5,37},{6,102},{7,39},{8,104},... | collective-permute-start | bytes 1179656 | tf_op jit(solution)/shard_map/ppermute | solution.py:290
  38.3 5.8 %collective-permute-done.11.refs_3_ = bf16[16,16,384]{2,1,0:T(8,128)(2,1)S(1)} collective-permute-done((bf16[16,16,384]{2,1,0:T(8,128)(2,1)S(1)}, bf16[16,16,384]{2,1,0:T(8,128)(2,1)S(1)}, u32[]{:S(2)}, u32[]{:S(2)}) %collective-permute-start.11) | collective-permute-done | bytes 196640 | tf_op jit(solution)/shard_map/ppermute | solution.py:290
  44.0 0.0 collective-permute-done.12.refs_2_
  44.0 3.6 %shard_map.57 = (bf16[16,16,384]{2,1,0:T(8,128)(2,1)S(1)}, bf16[16,16,384]{2,1,0:T(8,128)(2,1)S(1)}, bf16[16,16,384]{2,1,0:T(8,128)(2,1)S(1)}, bf16[16,16,384]{2,1,0:T(8,128)(2,1)S(1)}) custom-call(bf16[64,384]{1,0:T(8,128)(2,1)S(1)} %get-tuple-element.32.cc_ref, bf16[3,64,384,128]{3,2,1,0:T(8,128)(2,1)} %integrals_ref.5), custom_call_target="tpu_custom_call" | custom-call | flops 1207959552 | bytes 4718592 | tf_op jit(solution)/shard_map/pallas_call | solution.py:189
  47.6 0.1 collective-permute-start.13
  47.7 5.3 %collective-permute-start.14 = (bf16[16,16,384]{2,1,0:T(8,128)(2,1)S(1)}, bf16[16,16,384]{2,1,0:T(8,128)(2,1)S(1)}, u32[]{:S(2)}, u32[]{:S(2)}) collective-permute-start(bf16[16,16,384]{2,1,0:T(8,128)(2,1)S(1)} %get-tuple-element.35), channel_id=1, source_target_pairs={{0,64},{1,65},{2,66},{3,67},{4,68},{5,69},{6,70},{7,71},{8,72},{9,... | collective-permute-start | bytes 589832 | tf_op jit(solution)/shard_map/ppermute | solution.py:290
  53.0 0.0 slice-done
  53.0 0.0 slice-done.1
  53.0 0.5 shard_map.58.refs_4_
  53.5 2.3 %shard_map.60.refs_5_ = bf16[16,64,1536]{2,1,0:T(8,128)(2,1)} custom-call(bf16[16,16,384]{2,1,0:T(8,128)(2,1)S(1)} %get-tuple-element.41.refs_0_, bf16[16,16,384]{2,1,0:T(8,128)(2,1)S(1)} %collective-permute-done.10.refs_1_, bf16[16,16,384]{2,1,0:T(8,128)(2,1)S(1)} %collective-permute-done.12.refs_2_, ...), custom_call_target="tpu_custom_call" | custom-call | flops 1207959552 | bytes 1572864 | tf_op jit(solution)/shard_map/pallas_call | solution.py:263
  55.9 0.0 collective-permute-done.16.refs_1_
  55.9 0.1 collective-permute-start.15
  56.0 0.0 collective-permute-done.17.refs_2_
  56.0 0.0 collective-permute-done.18.refs_3_
  56.0 3.8 %shard_map.61.refs_5_ = bf16[16,64,1536]{2,1,0:T(8,128)(2,1)} custom-call(bf16[16,32,384]{2,1,0:T(8,128)(2,1)S(1)} %get-tuple-element.37.refs_0_, bf16[16,32,384]{2,1,0:T(8,128)(2,1)S(1)} %collective-permute-done.16.refs_1_, bf16[16,32,384]{2,1,0:T(8,128)(2,1)S(1)} %collective-permute-done.17.refs_2_, ...), custom_call_target="tpu_custom_call", output_to_operand_aliasing={{}: (5, {})} | custom-call | flops 2415919104 | bytes 3145728 | tf_op jit(solution)/shard_map/pallas_call | solution.py:263
  59.8 1.6 %collective-permute-done.13.refs_1_ = bf16[16,16,384]{2,1,0:T(8,128)(2,1)S(1)} collective-permute-done((bf16[16,16,384]{2,1,0:T(8,128)(2,1)S(1)}, bf16[16,16,384]{2,1,0:T(8,128)(2,1)S(1)}, u32[]{:S(2)}, u32[]{:S(2)}) %collective-permute-start.13) | collective-permute-done | bytes 196640 | tf_op jit(solution)/shard_map/ppermute | solution.py:290
  61.4 1.3 %collective-permute-done.14.refs_2_ = bf16[16,16,384]{2,1,0:T(8,128)(2,1)S(1)} collective-permute-done((bf16[16,16,384]{2,1,0:T(8,128)(2,1)S(1)}, bf16[16,16,384]{2,1,0:T(8,128)(2,1)S(1)}, u32[]{:S(2)}, u32[]{:S(2)}) %collective-permute-start.14) | collective-permute-done | bytes 196640 | tf_op jit(solution)/shard_map/ppermute | solution.py:290
  62.7 0.0 collective-permute-done.15.refs_3_
  62.7 2.3 %shard_map.62 = bf16[16,64,1536]{2,1,0:T(8,128)(2,1)} custom-call(bf16[16,16,384]{2,1,0:T(8,128)(2,1)S(1)} %get-tuple-element.33.after_ref.refs_0_, bf16[16,16,384]{2,1,0:T(8,128)(2,1)S(1)} %collective-permute-done.13.refs_1_, bf16[16,16,384]{2,1,0:T(8,128)(2,1)S(1)} %collective-permute-done.14.refs_2_, ...), custom_call_target="tpu_custom_call", output_to_operand_aliasing={{}: (5, {})} | custom-call | flops 1207959552 | bytes 1572864 | tf_op jit(solution)/shard_map/pallas_call | solution.py:263
  (2 shorter events, 0.0 us)
Async XLA Ops:
  0.0 8.9 %copy-start.1 = (bf16[256,64]{0,1:T(8,128)(2,1)S(1)}, bf16[256,64]{0,1:T(8,128)(2,1)}, u32[]{:S(2)}) copy-start(bf16[256,64]{0,1:T(8,128)(2,1)} %param.6) | copy-start | bytes 98308
  0.0 19.9 %copy-start = (s32[1,3]{1,0:T(1,128)S(1)}, s32[1,3]{1,0:T(1,128)}, u32[]{:S(2)}) copy-start(s32[1,3]{1,0:T(1,128)} %nu_ref.1) | copy-start | bytes 40
  0.0 6.5 %collective-permute-start.2 = (bf16[1,64,256]{2,1,0:T(8,128)(2,1)}, bf16[1,64,256]{2,1,0:T(8,128)(2,1)S(1)}, u32[]{:S(2)}, u32[]{:S(2)}) collective-permute-start(bf16[1,64,256]{2,1,0:T(8,128)(2,1)} %bitcast.8), channel_id=1, source_target_pairs={{0,24},{1,7},{2,26},{3,1},{4,28},{5,3},{6,30},{7,5},{8,0},{9,15},{... | collective-permute-start | bytes 98312 | tf_op jit(solution)/shard_map/ppermute | solution.py:62
  0.8 5.7 %collective-permute-start.1 = (bf16[1,64,256]{2,1,0:T(8,128)(2,1)}, bf16[1,64,256]{2,1,0:T(8,128)(2,1)S(1)}, u32[]{:S(2)}, u32[]{:S(2)}) collective-permute-start(bf16[1,64,256]{2,1,0:T(8,128)(2,1)} %bitcast.9), channel_id=1, source_target_pairs={{0,8},{1,3},{2,10},{3,5},{4,12},{5,7},{6,14},{7,1},{8,16},{9,11},{... | collective-permute-start | bytes 98312 | tf_op jit(solution)/shard_map/ppermute | solution.py:62
  3.2 5.6 %collective-permute-start = (bf16[1,64,256]{2,1,0:T(8,128)(2,1)}, bf16[1,64,256]{2,1,0:T(8,128)(2,1)S(1)}, u32[]{:S(2)}, u32[]{:S(2)}) collective-permute-start(bf16[1,64,256]{2,1,0:T(8,128)(2,1)} %bitcast.10), channel_id=1, source_target_pairs={{0,16},{1,5},{2,18},{3,7},{4,20},{5,1},{6,22},{7,3},{8,24},{9,13},... | collective-permute-start | bytes 98312 | tf_op jit(solution)/shard_map/ppermute | solution.py:62
  8.9 6.6 %collective-permute-start.5 = (bf16[4,64,256]{2,1,0:T(8,128)(2,1)S(1)}, bf16[4,64,256]{2,1,0:T(8,128)(2,1)S(1)}, u32[]{:S(2)}, u32[]{:S(2)}) collective-permute-start(bf16[4,64,256]{2,1,0:T(8,128)(2,1)S(1)} %pad_maximum_fusion.refs_0_), channel_id=1, source_target_pairs={{0,4},{1,17},{2,6},{3,19},{4,0},{5,21},{6,2},{7,23},{8,12},{9,25},... | collective-permute-start | bytes 393224 | tf_op jit(solution)/shard_map/ppermute | solution.py:65
  12.2 6.2 %collective-permute-start.4 = (bf16[4,64,256]{2,1,0:T(8,128)(2,1)S(1)}, bf16[4,64,256]{2,1,0:T(8,128)(2,1)S(1)}, u32[]{:S(2)}, u32[]{:S(2)}) collective-permute-start(bf16[4,64,256]{2,1,0:T(8,128)(2,1)S(1)} %pad_maximum_fusion.refs_0_), channel_id=1, source_target_pairs={{0,2},{1,9},{2,4},{3,11},{4,6},{5,13},{6,0},{7,15},{8,10},{9,17},{... | collective-permute-start | bytes 393224 | tf_op jit(solution)/shard_map/ppermute | solution.py:65
  12.8 5.5 %collective-permute-start.3 = (bf16[4,64,256]{2,1,0:T(8,128)(2,1)S(1)}, bf16[4,64,256]{2,1,0:T(8,128)(2,1)S(1)}, u32[]{:S(2)}, u32[]{:S(2)}) collective-permute-start(bf16[4,64,256]{2,1,0:T(8,128)(2,1)S(1)} %pad_maximum_fusion.refs_0_), channel_id=1, source_target_pairs={{0,6},{1,25},{2,0},{3,27},{4,2},{5,29},{6,4},{7,31},{8,14},{9,1},{... | collective-permute-start | bytes 393224 | tf_op jit(solution)/shard_map/ppermute | solution.py:65
  15.4 4.1 %collective-permute-start.6 = (bf16[4,64,256]{2,1,0:T(8,128)(2,1)S(1)}, bf16[4,64,256]{2,1,0:T(8,128)(2,1)S(1)}, u32[]{:S(2)}, u32[]{:S(2)}) collective-permute-start(bf16[4,64,256]{2,1,0:T(8,128)(2,1)S(1)} %pad_maximum_fusion.refs_0_), channel_id=1, source_target_pairs={{0,1},{1,0},{2,3},{3,2},{4,5},{5,4},{6,7},{7,6},{8,9},{9,8},{10,11... | collective-permute-start | bytes 393224 | tf_op jit(solution)/shard_map/ppermute | solution.py:67
  15.4 4.1 %collective-permute-start.9 = (bf16[4,64,256]{2,1,0:T(8,128)(2,1)S(1)}, bf16[4,64,256]{2,1,0:T(8,128)(2,1)S(1)}, u32[]{:S(2)}, u32[]{:S(2)}) collective-permute-start(bf16[4,64,256]{2,1,0:T(8,128)(2,1)S(1)} %collective-permute-done.5.refs_3_), channel_id=1, source_target_pairs={{0,1},{1,0},{2,3},{3,2},{4,5},{5,4},{6,7},{7,6},{8,9},{9,8},{10,11... | collective-permute-start | bytes 393224 | tf_op jit(solution)/shard_map/ppermute | solution.py:67
  18.4 1.3 %collective-permute-start.8 = (bf16[4,64,256]{2,1,0:T(8,128)(2,1)S(1)}, bf16[4,64,256]{2,1,0:T(8,128)(2,1)S(1)}, u32[]{:S(2)}, u32[]{:S(2)}) collective-permute-start(bf16[4,64,256]{2,1,0:T(8,128)(2,1)S(1)} %collective-permute-done.4.refs_2_), channel_id=1, source_target_pairs={{0,1},{1,0},{2,3},{3,2},{4,5},{5,4},{6,7},{7,6},{8,9},{9,8},{10,11... | collective-permute-start | bytes 393224 | tf_op jit(solution)/shard_map/ppermute | solution.py:67
  18.4 1.5 %collective-permute-start.7 = (bf16[4,64,256]{2,1,0:T(8,128)(2,1)S(1)}, bf16[4,64,256]{2,1,0:T(8,128)(2,1)S(1)}, u32[]{:S(2)}, u32[]{:S(2)}) collective-permute-start(bf16[4,64,256]{2,1,0:T(8,128)(2,1)S(1)} %collective-permute-done.3.refs_1_), channel_id=1, source_target_pairs={{0,1},{1,0},{2,3},{3,2},{4,5},{5,4},{6,7},{7,6},{8,9},{9,8},{10,11... | collective-permute-start | bytes 393224 | tf_op jit(solution)/shard_map/ppermute | solution.py:67
  19.9 33.1 %slice-start = ((s8[4718592]{0:T(1024)(128)(4,1)}), s8[4194304]{0:T(1024)(128)(4,1)S(1)}, s32[]{:S(2)}) async-start(s8[4718592]{0:T(1024)(128)(4,1)} %bitcast.6), calls=%async_computation | async-start | bytes 8388608
  22.4 12.6 %collective-permute-start.10 = (bf16[16,16,384]{2,1,0:T(8,128)(2,1)S(1)}, bf16[16,16,384]{2,1,0:T(8,128)(2,1)S(1)}, u32[]{:S(2)}, u32[]{:S(2)}) collective-permute-start(bf16[16,16,384]{2,1,0:T(8,128)(2,1)S(1)} %get-tuple-element.29), channel_id=1, source_target_pairs={{0,32},{1,97},{2,34},{3,99},{4,36},{5,101},{6,38},{7,103},{8,40},{... | collective-permute-start | bytes 589832 | tf_op jit(solution)/shard_map/ppermute | solution.py:290
  24.4 19.7 %collective-permute-start.11 = (bf16[16,16,384]{2,1,0:T(8,128)(2,1)S(1)}, bf16[16,16,384]{2,1,0:T(8,128)(2,1)S(1)}, u32[]{:S(2)}, u32[]{:S(2)}) collective-permute-start(bf16[16,16,384]{2,1,0:T(8,128)(2,1)S(1)} %get-tuple-element.30), channel_id=1, source_target_pairs={{0,96},{1,33},{2,98},{3,35},{4,100},{5,37},{6,102},{7,39},{8,104},... | collective-permute-start | bytes 589832 | tf_op jit(solution)/shard_map/ppermute | solution.py:290
  26.6 17.5 %collective-permute-start.12 = (bf16[16,16,384]{2,1,0:T(8,128)(2,1)S(1)}, bf16[16,16,384]{2,1,0:T(8,128)(2,1)S(1)}, u32[]{:S(2)}, u32[]{:S(2)}) collective-permute-start(bf16[16,16,384]{2,1,0:T(8,128)(2,1)S(1)} %get-tuple-element.31), channel_id=1, source_target_pairs={{0,64},{1,65},{2,66},{3,67},{4,68},{5,69},{6,70},{7,71},{8,72},{9,... | collective-permute-start | bytes 589832 | tf_op jit(solution)/shard_map/ppermute | solution.py:290
  28.4 24.6 %slice-start.1 = ((s8[4718592]{0:T(1024)(128)(4,1)}), s8[524288]{0:T(1024)(128)(4,1)S(1)}, s32[]{:S(2)}) async-start(s8[4718592]{0:T(1024)(128)(4,1)} %bitcast.6), calls=%async_computation.1 | async-start | bytes 1048576
  33.2 22.7 %collective-permute-start.16 = (bf16[16,32,384]{2,1,0:T(8,128)(2,1)S(1)}, bf16[16,32,384]{2,1,0:T(8,128)(2,1)S(1)}, u32[]{:S(2)}, u32[]{:S(2)}) collective-permute-start(bf16[16,32,384]{2,1,0:T(8,128)(2,1)S(1)} %get-tuple-element.38), channel_id=1, source_target_pairs={{0,64},{1,65},{2,66},{3,67},{4,68},{5,69},{6,70},{7,71},{8,72},{9,... | collective-permute-start | bytes 1179656 | tf_op jit(solution)/shard_map/ppermute | solution.py:290
  35.0 20.9 %collective-permute-start.17 = (bf16[16,32,384]{2,1,0:T(8,128)(2,1)S(1)}, bf16[16,32,384]{2,1,0:T(8,128)(2,1)S(1)}, u32[]{:S(2)}, u32[]{:S(2)}) collective-permute-start(bf16[16,32,384]{2,1,0:T(8,128)(2,1)S(1)} %get-tuple-element.39), channel_id=1, source_target_pairs={{0,32},{1,97},{2,34},{3,99},{4,36},{5,101},{6,38},{7,103},{8,40},{... | collective-permute-start | bytes 1179656 | tf_op jit(solution)/shard_map/ppermute | solution.py:290
  35.0 21.0 %collective-permute-start.18 = (bf16[16,32,384]{2,1,0:T(8,128)(2,1)S(1)}, bf16[16,32,384]{2,1,0:T(8,128)(2,1)S(1)}, u32[]{:S(2)}, u32[]{:S(2)}) collective-permute-start(bf16[16,32,384]{2,1,0:T(8,128)(2,1)S(1)} %get-tuple-element.40), channel_id=1, source_target_pairs={{0,96},{1,33},{2,98},{3,35},{4,100},{5,37},{6,102},{7,39},{8,104},... | collective-permute-start | bytes 1179656 | tf_op jit(solution)/shard_map/ppermute | solution.py:290
  47.6 13.8 %collective-permute-start.13 = (bf16[16,16,384]{2,1,0:T(8,128)(2,1)S(1)}, bf16[16,16,384]{2,1,0:T(8,128)(2,1)S(1)}, u32[]{:S(2)}, u32[]{:S(2)}) collective-permute-start(bf16[16,16,384]{2,1,0:T(8,128)(2,1)S(1)} %get-tuple-element.34), channel_id=1, source_target_pairs={{0,32},{1,97},{2,34},{3,99},{4,36},{5,101},{6,38},{7,103},{8,40},{... | collective-permute-start | bytes 589832 | tf_op jit(solution)/shard_map/ppermute | solution.py:290
  47.7 15.0 %collective-permute-start.14 = (bf16[16,16,384]{2,1,0:T(8,128)(2,1)S(1)}, bf16[16,16,384]{2,1,0:T(8,128)(2,1)S(1)}, u32[]{:S(2)}, u32[]{:S(2)}) collective-permute-start(bf16[16,16,384]{2,1,0:T(8,128)(2,1)S(1)} %get-tuple-element.35), channel_id=1, source_target_pairs={{0,64},{1,65},{2,66},{3,67},{4,68},{5,69},{6,70},{7,71},{8,72},{9,... | collective-permute-start | bytes 589832 | tf_op jit(solution)/shard_map/ppermute | solution.py:290
  55.9 6.8 %collective-permute-start.15 = (bf16[16,16,384]{2,1,0:T(8,128)(2,1)S(1)}, bf16[16,16,384]{2,1,0:T(8,128)(2,1)S(1)}, u32[]{:S(2)}, u32[]{:S(2)}) collective-permute-start(bf16[16,16,384]{2,1,0:T(8,128)(2,1)S(1)} %get-tuple-element.36), channel_id=1, source_target_pairs={{0,96},{1,33},{2,98},{3,35},{4,100},{5,37},{6,102},{7,39},{8,104},... | collective-permute-start | bytes 589832 | tf_op jit(solution)/shard_map/ppermute | solution.py:290
